TPU v7x, 256 devices: a whole 4x4x8 slice. The times are simulated.
256 devices in a mesh: dom: 64 (over x, z, core), rep: 4 (over y).
Axes of the slice: x: 4, y: 4, z: 8, core: 2. Of those that a mesh axis runs over, the one named last changes fastest.
Arguments:
- elem_rows: bfloat16 [524288, 512], P(('dom', 'rep')), may hold values from -6 to 6
- elem_block: int32 [524288], P(('dom', 'rep')), may hold values from 0 to 3
- send_lists: int32 [524288], P(('dom', 'rep')), may hold values from 0 to 2047, as said below
- halo_block: int32 [524288], P(('dom', 'rep')), may hold values from 0 to 3
- born_rows: bfloat16 [131072, 512], P(('dom', 'rep')), may hold values from -6 to 6
- born_owner: int32 [131072, 1], P(('dom', 'rep')), may hold values from 0 to 255; in each aligned block of 512 rows (0 to 511, 512 to 1023, ...) at most 4 rows name the same one
- mass: float32 [131072], P(('dom', 'rep')), may hold values from 0.5 to 4
Outputs:
- factor: float32 [131072, 512], P(('dom', 'rep'))
Inputs may be any that keep to these rules, and one draw needn't show every extreme that they name: `send_lists`: each half of one device's list names 1024 distinct rows of that device. `born_owner`: among the born rows of one device at most 4 name the same owner.
All inputs are finite; a program needn't handle non-finite values.
Results may differ from a plain program's by a relative error of at most 0.0003.
Values may be sent and summed in bfloat16 or wider, within the bound.
No kernel may reach another device: no remote copies, remote signals or barrier semaphores. Data moves between devices by JAX's collectives and lax.ppermute only.
A program may use at most 64 MiB of HBM per device.

v0:
```python
import jax
import jax.numpy as jnp
from jax import lax
from jax.sharding import PartitionSpec as P

CAP = 4


def with_halo(value, sides, width):
    for axis, dim in sides:
        devices, length = (lax.axis_size(axis), value.shape[dim])
        up = [(i, (i + 1) % devices) for i in range(devices - 1)]
        down = [(j, i) for i, j in up]
        last = lax.slice_in_dim(value, length - width, length, axis=dim)
        leading = lax.slice_in_dim(value, 0, width, axis=dim)
        before = lax.ppermute(last, axis, up)
        after = lax.ppermute(leading, axis, down)
        value = jnp.concatenate([before, value, after], axis=dim)
    return value


def local(elem_rows, elem_block, send_lists, halo_block, born_rows, born_owner, mass):
    width = elem_rows.shape[1]
    dom_size = lax.axis_size("dom")
    rep_size = lax.axis_size("rep")
    list_half = send_lists.shape[0] // 2
    listed = jnp.take(elem_rows, send_lists, axis=0)
    padded = with_halo(listed, (("dom", 0),), list_half)
    halo_rows = jnp.concatenate([padded[:list_half], padded[3 * list_half :]], axis=0)
    born_count = born_rows.shape[0]
    slot_total = dom_size * rep_size
    owner_codes = born_owner[:, 0]
    onehot = (owner_codes[:, None] == jnp.arange(slot_total, dtype=jnp.int32)[None, :]).astype(
        jnp.bfloat16
    )
    row_index = jnp.arange(born_count, dtype=jnp.int32)
    earlier = (row_index[None, :] < row_index[:, None]).astype(jnp.bfloat16)
    counts = jnp.dot(earlier, onehot, preferred_element_type=jnp.float32)
    slot_rank = jnp.sum(counts * onehot.astype(jnp.float32), axis=1).astype(jnp.int32)
    position = owner_codes * CAP + slot_rank
    packed = jnp.zeros((slot_total * CAP, width), jnp.bfloat16).at[position].set(born_rows)
    arrived = lax.all_to_all(
        packed.reshape(dom_size, rep_size * CAP, width),
        "dom",
        split_axis=0,
        concat_axis=0,
        tiled=True,
    )
    born_pool = arrived.reshape(-1, width)
    born_block = jnp.arange(born_pool.shape[0], dtype=jnp.int32) // CAP % rep_size
    row_pool = jnp.concatenate([elem_rows, halo_rows, born_pool], axis=0)
    pool_block = jnp.concatenate([elem_block, halo_block, born_block], axis=0)
    stacked = jnp.concatenate(
        [
            row_pool * (pool_block == block_id)[:, None].astype(jnp.bfloat16)
            for block_id in range(rep_size)
        ],
        axis=1,
    )
    block_gram = lax.psum_scatter(
        lax.dot_general(
            stacked, row_pool, (((0,), (0,)), ((), ())), preferred_element_type=jnp.float32
        ),
        "rep",
        scatter_dimension=0,
        tiled=True,
    )
    system = jnp.diag(mass) + block_gram / width
    return jnp.linalg.cholesky(system)


def solution(mesh):
    in_specs = (
        P(("dom", "rep"), None),
        P(("dom", "rep")),
        P(("dom", "rep")),
        P(("dom", "rep")),
        P(("dom", "rep"), None),
        P(("dom", "rep"), None),
        P(("dom", "rep")),
    )
    out_specs = P(("dom", "rep"), None)
    return jax.shard_map(local, mesh=mesh, in_specs=in_specs, out_specs=out_specs, check_vma=False)
```

profile of v0, /device:TPU:1, one launch (start us, length us, event | category | flops | bytes accessed | tf_op | source)
XLA Modules:
  0.0 256.5 jit_solution(2242753920005314199)
XLA Ops:
  6.5 1.2 fusion.8
  7.8 0.7 compare_select_fusion.1
  8.4 4.0 %scatter_custom_fusion = bf16[1024,512]{1,0:T(8,128)(2,1)} fusion(s32[512]{0:T(512)S(1)} %bitcast.32, bf16[512,512]{1,0:T(8,128)(2,1)} %param.11, bf16[]{:T(256)} %constant.183.clone.1), kind=kCustom, calls=%fused_computation.32 | custom fusion | bytes 1049088 | tf_op jit(solution)/shard_map/scatter | solution.py:41
  12.4 13.0 %all-to-all-start = ((bf16[64,16,512]{2,1,0:T(8,128)(2,1)}), bf16[64,16,512]{2,1,0:T(8,128)(2,1)S(1)}, u32[]{:S(2)}, u32[]{:S(2)}) async-start(bf16[64,16,512]{2,1,0:T(8,128)(2,1)} %bitcast.29), calls=%async_computation | async-start | bytes 2097152 | tf_op jit(solution)/shard_map/all_to_all | solution.py:42
  25.4 0.7 fusion.25
  26.1 9.2 %gather_fusion = bf16[2048,512]{1,0:T(8,128)(2,1)} fusion(bf16[2048,512]{1,0:T(8,128)(2,1)S(1)} %copy-done, s32[2048]{0:T(1024)S(1)} %fusion.25), kind=kCustom, calls=%fused_computation | custom fusion | bytes 4202496 | tf_op jit(solution)/shard_map/jit(_take)/gather | solution.py:27
  35.3 1.8 broadcast_select_fusion
  37.3 3.5 %collective-permute-start = (bf16[1024,512]{1,0:T(8,128)(2,1)S(1)}, bf16[1024,512]{1,0:T(8,128)(2,1)S(1)}, u32[]{:S(2)}, u32[]{:S(2)}) collective-permute-start(bf16[1024,512]{1,0:T(8,128)(2,1)S(1)} %get-tuple-element.8), channel_id=1, source_target_pairs={{0,4},{4,8},{8,12},{12,16},{16,20},{20,24},{24,28},{28,32},{32,36}... | collective-permute-start | bytes 3145736 | tf_op jit(solution)/shard_map/ppermute | solution.py:16
  40.8 2.1 collective-permute-start.1
  43.0 16.5 %collective-permute-done = bf16[1024,512]{1,0:T(8,128)(2,1)S(1)} collective-permute-done((bf16[1024,512]{1,0:T(8,128)(2,1)S(1)}, bf16[1024,512]{1,0:T(8,128)(2,1)S(1)}, u32[]{:S(2)}, u32[]{:S(2)}) %collective-permute-start) | collective-permute-done | bytes 1048608 | tf_op jit(solution)/shard_map/ppermute | solution.py:16
  59.4 1.0 copy-done.1
  60.4 0.9 collective-permute-done.1
  61.4 8.3 %broadcast_multiply_fusion = bf16[5120,512]{1,0:T(8,128)(2,1)S(1)} fusion(bf16[5120]{0:T(1024)(128)(2,1)S(1)} %get-tuple-element.19, bf16[1024,512]{1,0:T(8,128)(2,1)S(1)} %bitcast.26, bf16[1024,512]{1,0:T(8,128)(2,1)} %collective-permute-done.1, bf16[1024,512]{1,0:T(8,128)(2,1)} %copy-done.1, bf16[2048,512]{1,0:T(8,128)(2,1)S(1)} %copy-done), kind=kLoop, calls=%fused_computation.11 | loop fusion | flops 26214400 | bytes 10496000 | tf_op jit(solution)/shard_map/mul | solution.py:55
  69.7 12.7 %broadcast_multiply_fusion.3 = (bf16[5120,512]{1,0:T(8,128)(2,1)S(1)}, bf16[5120,512]{1,0:T(8,128)(2,1)}, bf16[5120,512]{1,0:T(8,128)(2,1)}) fusion(bf16[5120]{0:T(1024)(128)(2,1)S(1)} %get-tuple-element.16, bf16[1024,512]{1,0:T(8,128)(2,1)S(1)} %bitcast.27, bf16[1024,512]{1,0:T(8,128)(2,1)} %collective-permute-done.1, bf16[1024,512]{1,0:T(8,128)(2,1)S(1)} %copy-done.2, ...), kind=kLoop, calls=%fused_computation.14 | loop fusion | flops 41943040 | bytes 21002240 | tf_op jit(solution)/shard_map/mul | solution.py:55
  82.5 27.0 %fusion = f32[2048,512]{0,1:T(8,128)} fusion(bf16[5120,512]{1,0:T(8,128)(2,1)S(1)} %broadcast_multiply_fusion, bf16[5120,512]{1,0:T(8,128)(2,1)} %get-tuple-element.7, bf16[5120,512]{1,0:T(8,128)(2,1)} %get-tuple-element.6, bf16[5120,512]{1,0:T(8,128)(2,1)S(1)} %get-tuple-element.5, bf16[1024,512]{1,0:T(8,128)(2,1)S(1)} %bitcast.28, ...), kind=kOutput, calls=%fused_computation.2 | convolution fusion | flops 10842275840 | bytes 30408704 | tf_op jit(solution)/shard_map/dot_general | solution.py:61
  109.4 50.9 %reduce-scatter.2.cloned.1.call-done = f32[512,512]{0,1:T(8,128)} async-done(((f32[2048,512]{0,1:T(8,128)}), f32[512,512]{0,1:T(8,128)}) %reduce-scatter.2.cloned.1.call-update) | async-done | bytes 1048592 | tf_op jit(solution)/shard_map/reduce_scatter | solution.py:60
  160.3 1.3 multiply_add_fusion
  161.7 0.3 copy.19
  162.0 1.5 fusion.9
  163.5 11.7 %cholesky.103 = f32[128,128]{1,0:T(8,128)S(1)} custom-call(f32[128,128]{1,0:T(8,128)S(1)} %cholesky.263), custom_call_target="Cholesky" | custom-call | tf_op jit(solution)/shard_map/jit(cholesky)/cholesky | solution.py:69
  175.3 9.8 %custom-call.27 = f32[1,128,128]{1,2,0:T(8,128)S(1)} custom-call(f32[1,128,128]{2,1,0:T(8,128)S(1)} %get-tuple-element.15), custom_call_target="InvertDiagBlocksLowerTriangular" | custom-call | tf_op jit(solution)/shard_map/jit(cholesky)/cholesky | solution.py:69
  185.9 11.7 %cholesky.215 = f32[128,128]{1,0:T(8,128)S(1)} custom-call(f32[128,128]{1,0:T(8,128)S(1)} %cholesky.267), custom_call_target="Cholesky" | custom-call | tf_op jit(solution)/shard_map/jit(cholesky)/cholesky | solution.py:69
  197.8 10.0 %custom-call.28 = f32[1,128,128]{1,2,0:T(8,128)S(1)} custom-call(f32[1,128,128]{2,1,0:T(8,128)S(1)} %get-tuple-element.13), custom_call_target="InvertDiagBlocksLowerTriangular" | custom-call | tf_op jit(solution)/shard_map/jit(cholesky)/cholesky | solution.py:69
  208.3 0.6 convolution_subtract_fusion.1
  208.9 11.7 %cholesky.236 = f32[128,128]{1,0:T(8,128)S(1)} custom-call(f32[128,128]{1,0:T(8,128)S(1)} %cholesky.272), custom_call_target="Cholesky" | custom-call | tf_op jit(solution)/shard_map/jit(cholesky)/cholesky | solution.py:69
  220.8 9.8 %custom-call.29 = f32[1,128,128]{1,2,0:T(8,128)S(1)} custom-call(f32[1,128,128]{2,1,0:T(8,128)S(1)} %get-tuple-element.11), custom_call_target="InvertDiagBlocksLowerTriangular" | custom-call | tf_op jit(solution)/shard_map/jit(cholesky)/cholesky | solution.py:69
  230.9 0.5 convolution_subtract_fusion.2
  231.4 11.7 %cholesky.253 = f32[128,128]{1,0:T(8,128)S(1)} custom-call(f32[128,128]{1,0:T(8,128)S(1)} %convolution_subtract_fusion.2), custom_call_target="Cholesky" | custom-call | tf_op jit(solution)/shard_map/jit(cholesky)/cholesky | solution.py:69
  243.2 0.7 compare_reduce_fusion.1
  244.0 0.6 compare_reduce_fusion
  244.6 0.7 compare_reduce_fusion.2
  247.9 1.3 copy.27
  (43 shorter events, 2.4 us)
Async XLA Ops:
  6.5 19.6 %copy-start = (bf16[2048,512]{1,0:T(8,128)(2,1)S(1)}, bf16[2048,512]{1,0:T(8,128)(2,1)}, u32[]{:S(2)}) copy-start(bf16[2048,512]{1,0:T(8,128)(2,1)} %param.7) | copy-start | bytes 6291460
  12.4 49.0 %all-to-all-start = ((bf16[64,16,512]{2,1,0:T(8,128)(2,1)}), bf16[64,16,512]{2,1,0:T(8,128)(2,1)S(1)}, u32[]{:S(2)}, u32[]{:S(2)}) async-start(bf16[64,16,512]{2,1,0:T(8,128)(2,1)} %bitcast.29), calls=%async_computation | async-start | bytes 2097152 | tf_op jit(solution)/shard_map/all_to_all | solution.py:42
  25.4 134.9 %reduce-scatter.2.cloned.1.call-start = ((), (), s32[]{:S(2)}) async-start(), calls=%async_computation.2 | async-start | bytes 5242880 | tf_op jit(solution)/shard_map/reduce_scatter | solution.py:60
  26.1 9.2 %copy-start.3 = (s32[2048]{0:T(1024)S(1)}, s32[2048]{0:T(1024)}, u32[]{:S(2)}) copy-start(s32[2048]{0:T(1024)} %param.9) | copy-start | bytes 24580
  35.3 7.6 %copy-start.4 = (s32[2048]{0:T(1024)S(1)}, s32[2048]{0:T(1024)}, u32[]{:S(2)}) copy-start(s32[2048]{0:T(1024)} %param.10) | copy-start | bytes 24580
  35.3 7.6 %copy-start.5 = (s32[2048]{0:T(1024)S(1)}, s32[2048]{0:T(1024)}, u32[]{:S(2)}) copy-start(s32[2048]{0:T(1024)} %param.8) | copy-start | bytes 24580
  37.3 22.2 %collective-permute-start = (bf16[1024,512]{1,0:T(8,128)(2,1)S(1)}, bf16[1024,512]{1,0:T(8,128)(2,1)S(1)}, u32[]{:S(2)}, u32[]{:S(2)}) collective-permute-start(bf16[1024,512]{1,0:T(8,128)(2,1)S(1)} %get-tuple-element.8), channel_id=1, source_target_pairs={{0,4},{4,8},{8,12},{12,16},{16,20},{20,24},{24,28},{28,32},{32,36}... | collective-permute-start | bytes 3145736 | tf_op jit(solution)/shard_map/ppermute | solution.py:16
  40.8 20.6 %collective-permute-start.1 = (bf16[1024,512]{1,0:T(8,128)(2,1)S(1)}, bf16[1024,512]{1,0:T(8,128)(2,1)}, u32[]{:S(2)}, u32[]{:S(2)}) collective-permute-start(bf16[1024,512]{1,0:T(8,128)(2,1)S(1)} %get-tuple-element.9), channel_id=1, source_target_pairs={{4,0},{8,4},{12,8},{16,12},{20,16},{24,20},{28,24},{32,28},{36,32}... | collective-permute-start | bytes 3145736 | tf_op jit(solution)/shard_map/ppermute | solution.py:17
  59.4 1.0 copy-start.1
  61.4 8.3 %copy-start.2 = (bf16[1024,512]{1,0:T(8,128)(2,1)S(1)}, bf16[1024,512]{1,0:T(8,128)(2,1)}, u32[]{:S(2)}) copy-start(bf16[1024,512]{1,0:T(8,128)(2,1)} %copy-done.1) | copy-start | bytes 3145732
  82.5 77.9 %copy-start.6 = (f32[512]{0:T(512)S(1)}, f32[512]{0:T(512)}, u32[]{:S(2)}) copy-start(f32[512]{0:T(512)} %param.13) | copy-start | bytes 6148
Sparse Core Ops, SparseCore 0:
  109.6 50.6 reduce-scatter.1
where the time goes:
time: 261 us; the launch traced here: 257 us
  other arithmetic  106 us (41%)
  waiting for transfers between devices  68.3 us (26%)
  matrix products  30.5 us (12%)
  starting transfers between devices  18.7 us (7%)
  between operations  16.7 us (6%)
  local copies, waits for them, and re-layouts  16.6 us (6%)
    another operation x14, other arithmetic, local(): return jnp.linalg.cholesky(system)  78.6 us
    reduce_scatter x1, waiting for transfers between devices, local(): lax.psum_scatter(lax.dot_general(stacked, row_pool, (((0,), (0,)), ((), (...  50.9 us
    dot_general x1, matrix products, local(): lax.dot_general(stacked, row_pool, (((0,), (0,)), ((), ())), preferred_el...  27 us
    mul x2, other arithmetic, local(): row_pool * (pool_block == block_id)[:, None].astype(jnp.bfloat16)  21.1 us
    ppermute x1, waiting for transfers between devices, with_halo(): before = lax.ppermute(last, axis, up)  16.5 us
    all_to_all x1, starting transfers between devices, local(): lax.all_to_all(packed.reshape(dom_size, rep_size * CAP, width), 'dom', sp...  13 us
    gather x1, local copies, waits for them, and re-layouts, local(): listed = jnp.take(elem_rows, send_lists, axis=0)  9.16 us
  transfers between devices with their start and end apart: 4, of which 3 were waited for; matrix products, arithmetic and copies ran while one was open for 5% of the time, Pallas kernels for 0%

commit v1 on v0

v1 whole, which is shorter than its diff:
```python
import functools

import jax
import jax.numpy as jnp
from jax import lax
from jax.experimental import pallas as pl
from jax.experimental.pallas import tpu as pltpu
from jax.sharding import PartitionSpec as P

CAP = 4
W = 512
TILE = 128
F32 = jnp.float32
BF16 = jnp.bfloat16
VMEM_LIMIT = 60 * 1024 * 1024
NT_DIMS = (((1,), (1,)), ((), ()))
HALF_A = ((0, 0, 0), (3, 384, 512))
HALF_B = ((1, 128, 0), (2, 256, 384))
HALF_W = 640


def call(kernel, outs, flops, *args, smem=(), scratch=(), name=None):
    specs = [
        pl.BlockSpec(memory_space=pltpu.SMEM if i in smem else pltpu.VMEM) for i in range(len(args))
    ]
    single = not isinstance(outs, (tuple, list))
    size = sum(a.size * a.dtype.itemsize for a in args)
    return pl.pallas_call(
        kernel,
        out_shape=outs,
        in_specs=specs,
        out_specs=pl.BlockSpec(memory_space=pltpu.VMEM)
        if single
        else [pl.BlockSpec(memory_space=pltpu.VMEM)] * len(outs),
        scratch_shapes=list(scratch),
        compiler_params=pltpu.CompilerParams(vmem_limit_bytes=VMEM_LIMIT),
        cost_estimate=pl.CostEstimate(flops=flops, bytes_accessed=size, transcendentals=0),
        name=name,
    )(*args)


def transposed(rows):
    order = lax.broadcasted_iota(jnp.int32, (W, W), 0) == lax.broadcasted_iota(jnp.int32, (W, W), 1)
    eye = jnp.where(order, 1.0, 0.0).astype(BF16)
    return lax.dot_general(eye, rows, NT_DIMS, preferred_element_type=F32).astype(BF16)


def pick_columns(cols_ref, list_ref, out_ref, first):
    total = cols_ref.shape[1]
    step = 256
    for c in range(0, out_ref.shape[1], step):
        names = list_ref[:, first + c : first + c + step]
        hot = lax.broadcasted_iota(jnp.int32, (total, step), 0) == names
        hot = jnp.where(hot, 1.0, 0.0).astype(BF16)
        out_ref[:, c : c + step] = jnp.dot(
            cols_ref[...], hot, preferred_element_type=F32
        ).astype(BF16)


def upper_list_kernel(rows_ref, list_ref, cols_ref, out_ref):
    for c in range(0, rows_ref.shape[0], 512):
        cols_ref[:, c : c + 512] = transposed(rows_ref[c : c + 512, :])
    pick_columns(cols_ref, list_ref, out_ref, out_ref.shape[1])


def lower_list_kernel(cols_ref, list_ref, out_ref):
    pick_columns(cols_ref, list_ref, out_ref, 0)


def pack_kernel(owner_ref, rows_ref, out_ref):
    owner = owner_ref[...]
    count = owner.shape[1]
    blocks = out_ref.shape[0] // CAP
    named = lax.broadcasted_iota(jnp.int32, (blocks, count), 0) == owner
    named = jnp.where(named, 1.0, 0.0)
    before = lax.broadcasted_iota(jnp.int32, (count, count), 0) < lax.broadcasted_iota(
        jnp.int32, (count, count), 1
    )
    before = jnp.where(before, 1.0, 0.0).astype(BF16)
    earlier = jnp.dot(named.astype(BF16), before, preferred_element_type=F32)
    rank = jnp.sum(named * earlier, axis=0, keepdims=True)
    place = owner * CAP + rank.astype(jnp.int32)
    hot = lax.broadcasted_iota(jnp.int32, (blocks * CAP, count), 0) == place
    hot = jnp.where(hot, 1.0, 0.0).astype(BF16)
    out_ref[...] = jnp.dot(hot, rows_ref[...], preferred_element_type=F32).astype(BF16)


def gram_into(out_ref, acc_ref, ids, half, pools):
    for panel, first, at in half:
        total = None
        width = W - first
        for cols_ref, block_ref in pools:
            left = cols_ref[panel * TILE : (panel + 1) * TILE, :]
            lefts = []
            for block in ids:
                keep = jnp.where(block_ref[...] == block, 1.0, 0.0).astype(BF16)
                lefts.append(left * keep)
            part = lax.dot_general(
                jnp.concatenate(lefts, axis=0),
                cols_ref[first:, :],
                NT_DIMS,
                preferred_element_type=F32,
            )
            total = part if total is None else total + part
        if acc_ref is not None:
            total = total + acc_ref[:, at : at + width]
        out_ref[:, at : at + width] = total


def elem_gram_kernel(rep_ref, cols_ref, block_ref, sa_ref, sb_ref, ka_ref, kb_ref):
    me = rep_ref[0]
    pair, mirror, far = me ^ 1, 3 - me, me ^ 2
    pools = [(cols_ref, block_ref)]
    gram_into(sa_ref, None, (pair, far), HALF_A, pools)
    gram_into(sb_ref, None, (mirror, far), HALF_B, pools)
    gram_into(ka_ref, None, (me, mirror), HALF_A, pools)
    gram_into(kb_ref, None, (me, pair), HALF_B, pools)


def halo_pools(lo_ref, up_ref, block_ref):
    half = lo_ref.shape[1]
    return [(lo_ref, block_ref.at[:, :half]), (up_ref, block_ref.at[:, half:])]


def sent_gram_kernel(rep_ref, lo_ref, up_ref, block_ref, a_ref, b_ref, sa_ref, sb_ref):
    me = rep_ref[0]
    pair, mirror, far = me ^ 1, 3 - me, me ^ 2
    pools = halo_pools(lo_ref, up_ref, block_ref)
    gram_into(sa_ref, a_ref, (pair, far), HALF_A, pools)
    gram_into(sb_ref, b_ref, (mirror, far), HALF_B, pools)


def kept_gram_kernel(rep_ref, lo_ref, up_ref, block_ref, a_ref, b_ref, ka_ref, kb_ref):
    me = rep_ref[0]
    pair, mirror = me ^ 1, 3 - me
    pools = halo_pools(lo_ref, up_ref, block_ref)
    gram_into(ka_ref, a_ref, (me, mirror), HALF_A, pools)
    gram_into(kb_ref, b_ref, (me, pair), HALF_B, pools)


def lane_copy(x, c):
    return jnp.broadcast_to(x[:, c : c + 1], (8, TILE))


def row_copy(x, i):
    return jnp.broadcast_to(x[i : i + 1, :], (8, TILE))


def add_all(xs):
    while len(xs) > 1:
        xs = [xs[i] + xs[i + 1] if i + 1 < len(xs) else xs[i] for i in range(0, len(xs), 2)]
    return xs[0]


def inverse_factor(columns):
    a = [[row_copy(columns[j], i) if i >= j else None for j in range(8)] for i in range(8)]
    low = [[None] * 8 for _ in range(8)]
    pivots = []
    for b in range(0, 8, 2):
        p, q, r = a[b][b], a[b + 1][b], a[b + 1][b + 1]
        det = p * r - q * q
        root, root_det = lax.rsqrt(p), lax.rsqrt(det)
        both = root * root_det
        pivots.append((root, -(q * both), p * both))
        for i in range(b + 2, 8):
            x, y = a[i][b], a[i][b + 1]
            low[i][b] = x * root
            low[i][b + 1] = (y * p - x * q) * both
        for i in range(b + 2, 8):
            for k in range(b + 2, i + 1):
                a[i][k] = a[i][k] - low[i][b] * low[k][b] - low[i][b + 1] * low[k][b + 1]
    inv = [[None] * 8 for _ in range(8)]
    for b in range(0, 8, 2):
        i0, i1, i2 = pivots[b // 2]
        inv[b][b], inv[b + 1][b], inv[b + 1][b + 1] = i0, i1, i2
        for m in range(b):
            s0 = add_all([low[b][k] * inv[k][m] for k in range(m, b)])
            s1 = add_all([low[b + 1][k] * inv[k][m] for k in range(m, b)])
            inv[b][m] = -(i0 * s0)
            inv[b + 1][m] = -(i1 * s0 + i2 * s1)
    return inv


def factor_panel(a_ref, tiles):
    sub = lax.broadcasted_iota(jnp.int32, (8, TILE), 0)
    lane = lax.broadcasted_iota(jnp.int32, (8, TILE), 1)
    cols = [slice(TILE * c, TILE * c + TILE) for c in range(tiles)]
    for s in range(16):
        o = 8 * s
        head = a_ref[o : o + 8, cols[0]]
        inv = inverse_factor([lane_copy(head, o + j) for j in range(8)])
        columns = []
        for m in range(8):
            v = inv[7][m]
            for i in range(6, m - 1, -1):
                v = jnp.where(sub <= i, inv[i][m], v)
            if m > 0:
                v = jnp.where(sub < m, 0.0, v)
            columns.append(v)
        upper = []
        for c in cols:
            x = a_ref[o : o + 8, c]
            upper.append(add_all([columns[m] * row_copy(x, m) for m in range(8)]))
        upper[0] = jnp.where(lane >= sub + o, upper[0], 0.0)
        for u, c in zip(upper, cols):
            a_ref[o : o + 8, c] = u
        if s == 15:
            break
        spread = [[row_copy(u, j) for j in range(8)] for u in upper]
        for g in range(s + 1, 16):
            rows = slice(8 * g, 8 * g + 8)
            x = a_ref[rows, cols[0]]
            b = [lane_copy(x, o + m) for m in range(8)]
            low = [add_all([inv[j][m] * b[m] for m in range(j + 1)]) for j in range(8)]
            for i, c in enumerate(cols):
                y = x if i == 0 else a_ref[rows, c]
                a_ref[rows, c] = y - add_all([low[j] * spread[i][j] for j in range(8)])


def factor_kernel(ka, ra, a2, kb, rb, b2, born, mass, out_ref, a_ref):
    pool = born[...]
    born_gram = lax.dot_general(pool, pool, (((0,), (0,)), ((), ())), preferred_element_type=F32)
    sub = lax.broadcasted_iota(jnp.int32, (TILE, TILE), 0)
    lane = lax.broadcasted_iota(jnp.int32, (TILE, TILE), 1)
    own = slice(0, TILE)
    for k0, r0, s0, half in ((ka, ra, a2, HALF_A), (kb, rb, b2, HALF_B)):
        for panel, first, at in half:
            cols = slice(at, at + W - first)
            rows = slice(panel * TILE, (panel + 1) * TILE)
            g = k0[own, cols] + r0[own, cols] + s0[:, cols] + born_gram[rows, first:]
            a_ref[rows, first:] = g * (1.0 / W)
    for k in range(4):
        rows = slice(TILE * k, TILE * (k + 1))
        first = TILE * k
        diag = a_ref[rows, rows]
        a_ref[rows, rows] = diag + jnp.where(sub == lane, mass[:, rows], 0.0)
        if k > 0:
            a_ref[rows, first:] = a_ref[rows, first:] - jnp.dot(
                out_ref[rows, :first],
                a_ref[:first, first:],
                precision=lax.Precision.HIGHEST,
                preferred_element_type=F32,
            )
            out_ref[: first, rows] = jnp.zeros((first, TILE), F32)
        factor_panel(a_ref.at[rows, first:], 4 - k)
        for c in range(k, 4):
            out_ref[TILE * c : TILE * (c + 1), rows] = a_ref[rows, TILE * c : TILE * (c + 1)].T


def local(elem_rows, elem_block, send_lists, halo_block, born_rows, born_owner, mass):
    rows = elem_rows.shape[0]
    listed = send_lists.shape[0] // 2
    dom_size, rep_size = lax.axis_size("dom"), lax.axis_size("rep")
    rep = lax.axis_index("rep").astype(jnp.int32).reshape(1)
    shape = jax.ShapeDtypeStruct
    lists = send_lists.reshape(1, -1)
    pick_flops = 2 * W * rows * listed

    cols, to_upper = call(
        upper_list_kernel,
        (shape((W, rows), BF16), shape((W, listed), BF16)),
        pick_flops + 2 * W * W * rows,
        elem_rows,
        lists,
        name="upper_list",
    )
    up = [(i, i + 1) for i in range(dom_size - 1)]
    down = [(j, i) for i, j in up]
    from_lower = lax.ppermute(to_upper, "dom", up)
    to_lower = call(
        lower_list_kernel, shape((W, listed), BF16), pick_flops, cols, lists, name="lower_list"
    )
    from_upper = lax.ppermute(to_lower, "dom", down)

    slots = dom_size * rep_size
    packed = call(
        pack_kernel,
        shape((slots * CAP, W), BF16),
        2 * slots * CAP * W * W,
        born_owner.reshape(1, -1),
        born_rows,
        name="pack_born",
    )
    arrived = lax.all_to_all(
        packed.reshape(slots, CAP, W), ("dom", "rep"), split_axis=0, concat_axis=0, tiled=True
    ).reshape(slots * CAP, W)

    part = shape((2 * TILE, HALF_W), F32)
    gram_flops = 4 * 6 * 2 * TILE * 256 * rows
    ids = elem_block.reshape(1, -1)
    sa, sb, ka, kb = call(
        elem_gram_kernel, (part,) * 4, gram_flops, rep, cols, ids, smem=(0,), name="elem_gram"
    )
    halo_ids = halo_block.reshape(1, -1)
    sa, sb = call(
        sent_gram_kernel,
        (part,) * 2,
        gram_flops // 2,
        rep,
        from_lower,
        from_upper,
        halo_ids,
        sa,
        sb,
        smem=(0,),
        name="sent_gram",
    )
    pair = [(i, i ^ 1) for i in range(rep_size)]
    mirror = [(i, 3 - i) for i in range(rep_size)]
    ra = lax.ppermute(sa, "rep", pair)
    rb = lax.ppermute(sb, "rep", mirror)
    ka, kb = call(
        kept_gram_kernel,
        (part,) * 2,
        gram_flops // 2,
        rep,
        from_lower,
        from_upper,
        halo_ids,
        ka,
        kb,
        smem=(0,),
        name="kept_gram",
    )
    a2 = lax.ppermute(ka[TILE:] + ra[TILE:], "rep", mirror)
    b2 = lax.ppermute(kb[TILE:] + rb[TILE:], "rep", pair)
    return call(
        factor_kernel,
        shape((W, W), F32),
        10**9,
        ka,
        ra,
        a2,
        kb,
        rb,
        b2,
        arrived,
        mass.reshape(1, -1),
        scratch=(pltpu.VMEM((W, W), F32),),
        name="factor",
    )


def solution(mesh):
    in_specs = (
        P(("dom", "rep"), None),
        P(("dom", "rep")),
        P(("dom", "rep")),
        P(("dom", "rep")),
        P(("dom", "rep"), None),
        P(("dom", "rep"), None),
        P(("dom", "rep")),
    )
    out_specs = P(("dom", "rep"), None)
    return jax.shard_map(local, mesh=mesh, in_specs=in_specs, out_specs=out_specs, check_vma=False)
```

time: 261 us -> 111 us (0.43); the launches traced: 257 us -> 111 us
  other arithmetic: 106 us -> 3.16 us
  Pallas kernels: 0 us -> 52.3 us
  waiting for transfers between devices: 68.3 us -> 21 us
  matrix products: 30.5 us -> 0 us
  between operations: 16.7 us -> 0.06 us
  local copies, waits for them, and re-layouts: 16.6 us -> 5.33 us
  starting transfers between devices: 18.7 us -> 29 us
    another operation x14 -> x0, other arithmetic: 78.6 us -> none  [local(): return jnp.linalg.cholesky(system)]
    pallas_call x0 -> x7, Pallas kernels: none -> 52.3 us  [call(): pl.pallas_call(kernel, out_shape=outs, in_specs=specs, out_specs=pl.Block...]
    reduce_scatter x1 -> x0, waiting for transfers between devices: 50.9 us -> none  [local(): lax.psum_scatter(lax.dot_general(stacked, row_pool, (((0,), (0,)), ((), (...]
    dot_general x2 -> x0, matrix products: 28.2 us -> none  [the longest x1 27 us: local(): lax.dot_general(stacked, row_pool, (((0,), (0,)), ((), ())), preferred_el...]
    mul x2 -> x0, other arithmetic: 21.1 us -> none  [local(): row_pool * (pool_block == block_id)[:, None].astype(jnp.bfloat16)]
    gather x1 -> x0, local copies, waits for them, and re-layouts: 9.16 us -> none  [local(): listed = jnp.take(elem_rows, send_lists, axis=0)]
    ppermute x2 -> x6, starting transfers between devices: 5.63 us -> 13.4 us  [the longest x1 4.92 us: local(): from_lower = lax.ppermute(to_upper, 'dom', up)]
    scatter x1 -> x0, local copies, waits for them, and re-layouts: 3.95 us -> none  [local(): jnp.zeros((slot_total * CAP, width), jnp.bfloat16).at[position]]
  transfers between devices with their start and end apart: 4 -> 7, of which waited for: 3 -> 3; matrix products, arithmetic and copies ran while one was open for 5% -> 6% of each run, Pallas kernels for 0% -> 21%
where the time goes in v1:
time: 111 us
  Pallas kernels  52.3 us (47%)
  starting transfers between devices  29 us (26%)
  waiting for transfers between devices  21 us (19%)
  local copies, waits for them, and re-layouts  5.33 us (5%)
  other arithmetic  3.16 us (3%)
    pallas_call x7, Pallas kernels, call(): pl.pallas_call(kernel, out_shape=outs, in_specs=specs, out_specs=pl.Block...  52.3 us
    all_to_all x1, starting transfers between devices, local(): lax.all_to_all(packed.reshape(slots, CAP, W), ('dom', 'rep'), split_axis=...  15.6 us
    ppermute x1, waiting for transfers between devices, local(): ra = lax.ppermute(sa, 'rep', pair)  13.7 us
    ppermute x1, starting transfers between devices, local(): from_lower = lax.ppermute(to_upper, 'dom', up)  4.92 us
    ppermute x1, waiting for transfers between devices, local(): a2 = lax.ppermute(ka[TILE:] + ra[TILE:], 'rep', mirror)  3.68 us
    ppermute x1, waiting for transfers between devices, local(): b2 = lax.ppermute(kb[TILE:] + rb[TILE:], 'rep', pair)  3.58 us
    ppermute x1, starting transfers between devices, local(): a2 = lax.ppermute(ka[TILE:] + ra[TILE:], 'rep', mirror)  3.38 us
  transfers between devices with their start and end apart: 7, of which 3 were waited for; matrix products, arithmetic and copies ran while one was open for 6% of the time, Pallas kernels for 21%

profile of v1, /device:TPU:1, one launch (start us, length us, event | category | flops | bytes accessed | tf_op | source)
XLA Modules:
  0.0 110.8 jit_solution(8576034309648533701)
XLA Ops:
  0.0 6.1 %upper_list.1 = (bf16[512,2048]{1,0:T(8,128)(2,1)}, bf16[512,1024]{1,0:T(8,128)(2,1)}) custom-call(bf16[2048,512]{1,0:T(8,128)(2,1)} %rows_ref.2, s32[1,2048]{1,0:T(1,128)} %bitcast.7), custom_call_target="tpu_custom_call" | custom-call | flops 3221225472 | bytes 2105344 | tf_op jit(solution)/shard_map/upper_list/pallas_call | solution.py:28
  6.1 4.9 %collective-permute-start = (bf16[512,1024]{1,0:T(8,128)(2,1)}, bf16[512,1024]{1,0:T(8,128)(2,1)S(1)}, u32[]{:S(2)}, u32[]{:S(2)}) collective-permute-start(bf16[512,1024]{1,0:T(8,128)(2,1)} %get-tuple-element.15), channel_id=1, source_target_pairs={{0,4},{4,8},{8,12},{12,16},{16,20},{20,24},{24,28},{28,32},{32,36}... | collective-permute-start | bytes 3145736 | tf_op jit(solution)/shard_map/ppermute | solution.py:269
  11.0 4.9 %lower_list.1 = bf16[512,1024]{1,0:T(8,128)(2,1)} custom-call(bf16[512,2048]{1,0:T(8,128)(2,1)} %get-tuple-element.16.cols_ref, s32[1,2048]{1,0:T(1,128)} %bitcast.8), custom_call_target="tpu_custom_call" | custom-call | flops 2147483648 | bytes 2105344 | tf_op jit(solution)/shard_map/lower_list/pallas_call | solution.py:28
  15.9 1.9 %collective-permute-start.1 = (bf16[512,1024]{1,0:T(8,128)(2,1)}, bf16[512,1024]{1,0:T(8,128)(2,1)S(1)}, u32[]{:S(2)}, u32[]{:S(2)}) collective-permute-start(bf16[512,1024]{1,0:T(8,128)(2,1)} %lower_list.1), channel_id=1, source_target_pairs={{4,0},{8,4},{12,8},{16,12},{20,16},{24,20},{28,24},{32,28},{36,32}... | collective-permute-start | bytes 3145736 | tf_op jit(solution)/shard_map/ppermute | solution.py:273
  17.8 3.0 %pack_born.1 = bf16[1024,512]{1,0:T(8,128)(2,1)} custom-call(s32[1,512]{1,0:T(1,128)} %bitcast.12, bf16[512,512]{1,0:T(8,128)(2,1)} %rows_ref.3), custom_call_target="tpu_custom_call" | custom-call | flops 536870912 | bytes 526336 | tf_op jit(solution)/shard_map/pack_born/pallas_call | solution.py:28
  20.9 2.2 %reshape.29 = bf16[256,4,512]{2,1,0:T(4,128)(2,1)} reshape(bf16[1024,512]{1,0:T(8,128)(2,1)} %pack_born.1) | data formatting | bytes 2097152 | tf_op jit(solution)/shard_map/reshape | solution.py:285
  23.0 15.6 %all-to-all-start = ((bf16[256,4,512]{2,1,0:T(4,128)(2,1)}), bf16[256,4,512]{2,1,0:T(4,128)(2,1)S(1)}, u32[]{:S(2)}, u32[]{:S(2)}) async-start(bf16[256,4,512]{2,1,0:T(4,128)(2,1)} %reshape.29), calls=%async_computation | async-start | bytes 2097152 | tf_op jit(solution)/shard_map/all_to_all | solution.py:284
  38.6 5.9 %elem_gram.1 = (f32[256,640]{1,0:T(8,128)}, f32[256,640]{1,0:T(8,128)}, f32[256,640]{1,0:T(8,128)}, f32[256,640]{1,0:T(8,128)}) custom-call(s32[1]{0:T(128)} %bitcast.rep_ref, bf16[512,2048]{1,0:T(8,128)(2,1)} %get-tuple-element.16.cols_ref, s32[1,2048]{1,0:T(1,128)} %bitcast.9), custom_call_target="tpu_custom_call" | custom-call | flops 3221225472 | bytes 2105348 | tf_op jit(solution)/shard_map/elem_gram/pallas_call | solution.py:28
  44.5 0.0 collective-permute-done.lo_ref
  44.5 0.0 collective-permute-done.1.up_ref
  44.5 0.0 copy-start.5
  44.5 1.0 copy-done.4
  45.5 0.4 copy-done.5
  45.8 4.6 %sent_gram.1 = (f32[256,640]{1,0:T(8,128)}, f32[256,640]{1,0:T(8,128)}) custom-call(s32[1]{0:T(128)} %bitcast.rep_ref, bf16[512,1024]{1,0:T(8,128)(2,1)} %copy-done.4, bf16[512,1024]{1,0:T(8,128)(2,1)} %copy-done.5, s32[1,2048]{1,0:T(1,128)} %bitcast.10, f32[256,640]{1,0:T(8,128)} %get-tuple-element.20.a_ref, f32[256,640]{1,0:T(8,128)} %get-tuple-element.21.b_ref), custom_call_target="tpu_custom_call" | custom-call | flops 1610612736 | bytes 3416068 | tf_op jit(solution)/shard_map/sent_gram/pallas_call | solution.py:28
  50.4 1.4 %collective-permute-start.2 = (f32[256,640]{1,0:T(8,128)}, f32[256,640]{1,0:T(8,128)S(1)}, u32[]{:S(2)}, u32[]{:S(2)}) collective-permute-start(f32[256,640]{1,0:T(8,128)} %get-tuple-element.22), channel_id=1, source_target_pairs={{0,1},{1,0},{2,3},{3,2},{4,5},{5,4},{6,7},{7,6},{8,9},{9,8},{10,11... | collective-permute-start | bytes 1966088 | tf_op jit(solution)/shard_map/ppermute | solution.py:310
  51.8 1.8 %collective-permute-start.4 = (f32[256,640]{1,0:T(8,128)}, f32[256,640]{1,0:T(8,128)S(1)}, u32[]{:S(2)}, u32[]{:S(2)}) collective-permute-start(f32[256,640]{1,0:T(8,128)} %get-tuple-element.24), channel_id=1, source_target_pairs={{0,3},{1,2},{2,1},{3,0},{4,7},{5,6},{6,5},{7,4},{8,11},{9,10},{10,... | collective-permute-start | bytes 1966088 | tf_op jit(solution)/shard_map/ppermute | solution.py:311
  53.6 4.6 %kept_gram.1 = (f32[256,640]{1,0:T(8,128)}, f32[256,640]{1,0:T(8,128)}) custom-call(s32[1]{0:T(128)} %bitcast.rep_ref, bf16[512,1024]{1,0:T(8,128)(2,1)} %copy-done.4, bf16[512,1024]{1,0:T(8,128)(2,1)} %copy-done.5, s32[1,2048]{1,0:T(1,128)} %bitcast.11, f32[256,640]{1,0:T(8,128)} %get-tuple-element.17.a_ref, f32[256,640]{1,0:T(8,128)} %get-tuple-element.18.b_ref), custom_call_target="tpu_custom_call" | custom-call | flops 1610612736 | bytes 3416068 | tf_op jit(solution)/shard_map/kept_gram/pallas_call | solution.py:28
  58.2 13.7 %collective-permute-done.2.ra = f32[256,640]{1,0:T(8,128)S(1)} collective-permute-done((f32[256,640]{1,0:T(8,128)}, f32[256,640]{1,0:T(8,128)S(1)}, u32[]{:S(2)}, u32[]{:S(2)}) %collective-permute-start.2) | collective-permute-done | bytes 655392 | tf_op jit(solution)/shard_map/ppermute | solution.py:310
  71.9 1.2 %slice_add_fusion.1 = f32[128,640]{1,0:T(8,128)S(1)} fusion(f32[256,640]{1,0:T(8,128)S(1)} %collective-permute-done.2.ra, f32[256,640]{1,0:T(8,128)} %get-tuple-element.19.ka), kind=kLoop, calls=%fused_computation.1 | loop fusion | flops 81920 | bytes 983040 | tf_op jit(solution)/shard_map/add | solution.py:325
  73.1 3.4 %collective-permute-start.3 = (f32[128,640]{1,0:T(8,128)S(1)}, f32[128,640]{1,0:T(8,128)S(1)}, u32[]{:S(2)}, u32[]{:S(2)}) collective-permute-start(f32[128,640]{1,0:T(8,128)S(1)} %slice_add_fusion.1), channel_id=1, source_target_pairs={{0,3},{1,2},{2,1},{3,0},{4,7},{5,6},{6,5},{7,4},{8,11},{9,10},{10,... | collective-permute-start | bytes 983048 | tf_op jit(solution)/shard_map/ppermute | solution.py:325
  76.5 0.0 collective-permute-done.4.rb
  76.5 1.9 %slice_add_fusion = f32[128,640]{1,0:T(8,128)} fusion(f32[256,640]{1,0:T(8,128)S(1)} %collective-permute-done.4.rb, f32[256,640]{1,0:T(8,128)} %get-tuple-element.23.kb), kind=kLoop, calls=%fused_computation | loop fusion | flops 81920 | bytes 983040 | tf_op jit(solution)/shard_map/add | solution.py:326
  78.5 0.0 collective-permute-start.5
  78.5 0.0 all-to-all-done
  78.5 1.1 %reshape.30.born = bf16[1024,512]{1,0:T(8,128)(2,1)} reshape(bf16[256,4,512]{2,1,0:T(4,128)(2,1)S(1)} %all-to-all-done) | data formatting | bytes 2097152 | tf_op jit(solution)/shard_map/reshape | solution.py:286
  79.6 3.7 %collective-permute-done.3.a2 = f32[128,640]{1,0:T(8,128)S(1)} collective-permute-done((f32[128,640]{1,0:T(8,128)S(1)}, f32[128,640]{1,0:T(8,128)S(1)}, u32[]{:S(2)}, u32[]{:S(2)}) %collective-permute-start.3) | collective-permute-done | bytes 327712 | tf_op jit(solution)/shard_map/ppermute | solution.py:325
  83.3 3.6 %collective-permute-done.5.b2 = f32[128,640]{1,0:T(8,128)S(1)} collective-permute-done((f32[128,640]{1,0:T(8,128)}, f32[128,640]{1,0:T(8,128)S(1)}, u32[]{:S(2)}, u32[]{:S(2)}) %collective-permute-start.5) | collective-permute-done | bytes 327712 | tf_op jit(solution)/shard_map/ppermute | solution.py:326
  86.9 0.0 copy-done
  86.9 0.0 copy-done.1
  86.9 0.0 copy-done.2
  86.9 0.7 copy-done.3
  87.6 23.2 %factor.1 = f32[512,512]{1,0:T(8,128)} custom-call(f32[256,640]{1,0:T(8,128)} %get-tuple-element.19.ka, f32[256,640]{1,0:T(8,128)} %copy-done, f32[128,640]{1,0:T(8,128)} %copy-done.2, f32[256,640]{1,0:T(8,128)} %get-tuple-element.23.kb, f32[256,640]{1,0:T(8,128)} %copy-done.1, f32[128,640]{1,0:T(8,128)} %copy-done.3, bf16[1024,512]{1,0:T(8,128)(2,1)} %reshape.30.born, ...), custom_call_target="tpu_custom_call" | custom-call | flops 1000000000 | bytes 4327424 | tf_op jit(solution)/shard_map/factor/pallas_call | solution.py:28
  (5 shorter events, 0.0 us)
Async XLA Ops:
  6.1 38.4 %collective-permute-start = (bf16[512,1024]{1,0:T(8,128)(2,1)}, bf16[512,1024]{1,0:T(8,128)(2,1)S(1)}, u32[]{:S(2)}, u32[]{:S(2)}) collective-permute-start(bf16[512,1024]{1,0:T(8,128)(2,1)} %get-tuple-element.15), channel_id=1, source_target_pairs={{0,4},{4,8},{8,12},{12,16},{16,20},{20,24},{24,28},{28,32},{32,36}... | collective-permute-start | bytes 3145736 | tf_op jit(solution)/shard_map/ppermute | solution.py:269
  15.9 28.6 %collective-permute-start.1 = (bf16[512,1024]{1,0:T(8,128)(2,1)}, bf16[512,1024]{1,0:T(8,128)(2,1)S(1)}, u32[]{:S(2)}, u32[]{:S(2)}) collective-permute-start(bf16[512,1024]{1,0:T(8,128)(2,1)} %lower_list.1), channel_id=1, source_target_pairs={{4,0},{8,4},{12,8},{16,12},{20,16},{24,20},{28,24},{32,28},{36,32}... | collective-permute-start | bytes 3145736 | tf_op jit(solution)/shard_map/ppermute | solution.py:273
  23.0 55.4 %all-to-all-start = ((bf16[256,4,512]{2,1,0:T(4,128)(2,1)}), bf16[256,4,512]{2,1,0:T(4,128)(2,1)S(1)}, u32[]{:S(2)}, u32[]{:S(2)}) async-start(bf16[256,4,512]{2,1,0:T(4,128)(2,1)} %reshape.29), calls=%async_computation | async-start | bytes 2097152 | tf_op jit(solution)/shard_map/all_to_all | solution.py:284
  44.5 1.0 copy-start.4
  44.5 1.3 %copy-start.5 = (bf16[512,1024]{1,0:T(8,128)(2,1)}, bf16[512,1024]{1,0:T(8,128)(2,1)S(1)}, u32[]{:S(2)}) copy-start(bf16[512,1024]{1,0:T(8,128)(2,1)S(1)} %collective-permute-done.1.up_ref) | copy-start | bytes 3145732
  50.4 21.5 %collective-permute-start.2 = (f32[256,640]{1,0:T(8,128)}, f32[256,640]{1,0:T(8,128)S(1)}, u32[]{:S(2)}, u32[]{:S(2)}) collective-permute-start(f32[256,640]{1,0:T(8,128)} %get-tuple-element.22), channel_id=1, source_target_pairs={{0,1},{1,0},{2,3},{3,2},{4,5},{5,4},{6,7},{7,6},{8,9},{9,8},{10,11... | collective-permute-start | bytes 1966088 | tf_op jit(solution)/shard_map/ppermute | solution.py:310
  51.8 24.7 %collective-permute-start.4 = (f32[256,640]{1,0:T(8,128)}, f32[256,640]{1,0:T(8,128)S(1)}, u32[]{:S(2)}, u32[]{:S(2)}) collective-permute-start(f32[256,640]{1,0:T(8,128)} %get-tuple-element.24), channel_id=1, source_target_pairs={{0,3},{1,2},{2,1},{3,0},{4,7},{5,6},{6,5},{7,4},{8,11},{9,10},{10,... | collective-permute-start | bytes 1966088 | tf_op jit(solution)/shard_map/ppermute | solution.py:311
  71.9 15.0 %copy-start = (f32[256,640]{1,0:T(8,128)}, f32[256,640]{1,0:T(8,128)S(1)}, u32[]{:S(2)}) copy-start(f32[256,640]{1,0:T(8,128)S(1)} %collective-permute-done.2.ra) | copy-start | bytes 1966084
  73.1 10.2 %collective-permute-start.3 = (f32[128,640]{1,0:T(8,128)S(1)}, f32[128,640]{1,0:T(8,128)S(1)}, u32[]{:S(2)}, u32[]{:S(2)}) collective-permute-start(f32[128,640]{1,0:T(8,128)S(1)} %slice_add_fusion.1), channel_id=1, source_target_pairs={{0,3},{1,2},{2,1},{3,0},{4,7},{5,6},{6,5},{7,4},{8,11},{9,10},{10,... | collective-permute-start | bytes 983048 | tf_op jit(solution)/shard_map/ppermute | solution.py:325
  76.5 10.4 %copy-start.1 = (f32[256,640]{1,0:T(8,128)}, f32[256,640]{1,0:T(8,128)S(1)}, u32[]{:S(2)}) copy-start(f32[256,640]{1,0:T(8,128)S(1)} %collective-permute-done.4.rb) | copy-start | bytes 1966084
  78.5 8.4 %collective-permute-start.5 = (f32[128,640]{1,0:T(8,128)}, f32[128,640]{1,0:T(8,128)S(1)}, u32[]{:S(2)}, u32[]{:S(2)}) collective-permute-start(f32[128,640]{1,0:T(8,128)} %slice_add_fusion), channel_id=1, source_target_pairs={{0,1},{1,0},{2,3},{3,2},{4,5},{5,4},{6,7},{7,6},{8,9},{9,8},{10,11... | collective-permute-start | bytes 983048 | tf_op jit(solution)/shard_map/ppermute | solution.py:326
  83.3 3.6 %copy-start.2 = (f32[128,640]{1,0:T(8,128)}, f32[128,640]{1,0:T(8,128)S(1)}, u32[]{:S(2)}) copy-start(f32[128,640]{1,0:T(8,128)S(1)} %collective-permute-done.3.a2) | copy-start | bytes 983044
  86.9 0.7 copy-start.3

commit v2 on v1

--- a/solution.py
+++ b/solution.py
@@ -12,16 +12,19 @@
 TILE = 128
 F32 = jnp.float32
 BF16 = jnp.bfloat16
-VMEM_LIMIT = 60 * 1024 * 1024
+VMEM_LIMIT = 32 * 1024 * 1024
 NT_DIMS = (((1,), (1,)), ((), ()))
 HALF_A = ((0, 0, 0), (3, 384, 512))
 HALF_B = ((1, 128, 0), (2, 256, 384))
 HALF_W = 640
 
 
-def call(kernel, outs, flops, *args, smem=(), scratch=(), name=None):
+def call(kernel, outs, flops, *args, smem=(), anywhere=(), scratch=(), name=None):
     specs = [
-        pl.BlockSpec(memory_space=pltpu.SMEM if i in smem else pltpu.VMEM) for i in range(len(args))
+        pl.BlockSpec(
+            memory_space=pltpu.SMEM if i in smem else pl.ANY if i in anywhere else pltpu.VMEM
+        )
+        for i in range(len(args))
     ]
     single = not isinstance(outs, (tuple, list))
     size = sum(a.size * a.dtype.itemsize for a in args)
@@ -45,32 +48,28 @@
     return lax.dot_general(eye, rows, NT_DIMS, preferred_element_type=F32).astype(BF16)
 
 
-def pick_columns(cols_ref, list_ref, out_ref, first):
-    total = cols_ref.shape[1]
-    step = 256
-    for c in range(0, out_ref.shape[1], step):
-        names = list_ref[:, first + c : first + c + step]
-        hot = lax.broadcasted_iota(jnp.int32, (total, step), 0) == names
-        hot = jnp.where(hot, 1.0, 0.0).astype(BF16)
-        out_ref[:, c : c + step] = jnp.dot(
-            cols_ref[...], hot, preferred_element_type=F32
-        ).astype(BF16)
-
-
-def upper_list_kernel(rows_ref, list_ref, cols_ref, out_ref):
-    for c in range(0, rows_ref.shape[0], 512):
+def listed_kernel(rows_ref, list_ref, cols_ref, lower_ref, upper_ref):
+    total, listed = rows_ref.shape[0], lower_ref.shape[1]
+    for c in range(0, total, 512):
         cols_ref[:, c : c + 512] = transposed(rows_ref[c : c + 512, :])
-    pick_columns(cols_ref, list_ref, out_ref, out_ref.shape[1])
-
-
-def lower_list_kernel(cols_ref, list_ref, out_ref):
-    pick_columns(cols_ref, list_ref, out_ref, 0)
+    step, deep = 256, 256
+    places = lax.broadcasted_iota(jnp.int32, (deep, step), 0).astype(BF16)
+    for out_ref, first in ((upper_ref, listed), (lower_ref, 0)):
+        for c in range(0, listed, step):
+            names = list_ref[:, first + c : first + c + step]
+            hot = []
+            for h in range(0, total, deep):
+                near = jnp.clip(names - h, -1, deep).astype(F32).astype(BF16)
+                hot.append(jnp.where(places == near, 1.0, 0.0).astype(BF16))
+            out_ref[:, c : c + step] = jnp.dot(
+                cols_ref[...], jnp.concatenate(hot, axis=0), preferred_element_type=F32
+            ).astype(BF16)
 
 
 def pack_kernel(owner_ref, rows_ref, out_ref):
     owner = owner_ref[...]
     count = owner.shape[1]
-    blocks = out_ref.shape[0] // CAP
+    blocks = out_ref.shape[0]
     named = lax.broadcasted_iota(jnp.int32, (blocks, count), 0) == owner
     named = jnp.where(named, 1.0, 0.0)
     before = lax.broadcasted_iota(jnp.int32, (count, count), 0) < lax.broadcasted_iota(
@@ -82,60 +81,56 @@
     place = owner * CAP + rank.astype(jnp.int32)
     hot = lax.broadcasted_iota(jnp.int32, (blocks * CAP, count), 0) == place
     hot = jnp.where(hot, 1.0, 0.0).astype(BF16)
-    out_ref[...] = jnp.dot(hot, rows_ref[...], preferred_element_type=F32).astype(BF16)
-
-
-def gram_into(out_ref, acc_ref, ids, half, pools):
-    for panel, first, at in half:
-        total = None
-        width = W - first
-        for cols_ref, block_ref in pools:
-            left = cols_ref[panel * TILE : (panel + 1) * TILE, :]
-            lefts = []
-            for block in ids:
-                keep = jnp.where(block_ref[...] == block, 1.0, 0.0).astype(BF16)
-                lefts.append(left * keep)
-            part = lax.dot_general(
-                jnp.concatenate(lefts, axis=0),
-                cols_ref[first:, :],
-                NT_DIMS,
-                preferred_element_type=F32,
-            )
-            total = part if total is None else total + part
-        if acc_ref is not None:
-            total = total + acc_ref[:, at : at + width]
-        out_ref[:, at : at + width] = total
-
-
-def elem_gram_kernel(rep_ref, cols_ref, block_ref, sa_ref, sb_ref, ka_ref, kb_ref):
+    packed = jnp.dot(hot, rows_ref[...], preferred_element_type=F32).astype(BF16)
+    out_ref[...] = packed.reshape(out_ref.shape)
+
+
+def gram_kernel(kept, rep_ref, cols, lo, up, ids, halo_ids, a_ref, b_ref, buf, sems):
     me = rep_ref[0]
     pair, mirror, far = me ^ 1, 3 - me, me ^ 2
-    pools = [(cols_ref, block_ref)]
-    gram_into(sa_ref, None, (pair, far), HALF_A, pools)
-    gram_into(sb_ref, None, (mirror, far), HALF_B, pools)
-    gram_into(ka_ref, None, (me, mirror), HALF_A, pools)
-    gram_into(kb_ref, None, (me, pair), HALF_B, pools)
-
-
-def halo_pools(lo_ref, up_ref, block_ref):
-    half = lo_ref.shape[1]
-    return [(lo_ref, block_ref.at[:, :half]), (up_ref, block_ref.at[:, half:])]
-
-
-def sent_gram_kernel(rep_ref, lo_ref, up_ref, block_ref, a_ref, b_ref, sa_ref, sb_ref):
-    me = rep_ref[0]
-    pair, mirror, far = me ^ 1, 3 - me, me ^ 2
-    pools = halo_pools(lo_ref, up_ref, block_ref)
-    gram_into(sa_ref, a_ref, (pair, far), HALF_A, pools)
-    gram_into(sb_ref, b_ref, (mirror, far), HALF_B, pools)
-
-
-def kept_gram_kernel(rep_ref, lo_ref, up_ref, block_ref, a_ref, b_ref, ka_ref, kb_ref):
-    me = rep_ref[0]
-    pair, mirror = me ^ 1, 3 - me
-    pools = halo_pools(lo_ref, up_ref, block_ref)
-    gram_into(ka_ref, a_ref, (me, mirror), HALF_A, pools)
-    gram_into(kb_ref, b_ref, (me, pair), HALF_B, pools)
+    for_a, for_b = ((me, mirror), (me, pair)) if kept else ((pair, far), (mirror, far))
+    pieces, at = [], 0
+    for i, ref in enumerate((cols, lo, up)):
+        width = ref.shape[1]
+        copy = pltpu.make_async_copy(ref, buf.at[:, at : at + width], sems.at[i])
+        copy.start()
+        pieces.append((copy, at, width))
+        at += width
+    own = cols.shape[1]
+    right = left = None
+    for copy, at, width in pieces:
+        copy.wait()
+        for c in range(at, at + width, 1024):
+            ids_ref, k = (ids, c) if c < own else (halo_ids, c - own)
+            names = ids_ref[:, k : k + 1024]
+            masks_a = [jnp.where(names == b, 1.0, 0.0).astype(BF16) for b in for_a]
+            masks_b = [jnp.where(names == b, 1.0, 0.0).astype(BF16) for b in for_b]
+            part = []
+            for panel, masks in ((0, masks_a), (1, masks_b), (3, masks_a), (2, masks_b)):
+                x = buf[panel * TILE : (panel + 1) * TILE, c : c + 1024]
+                part += [x * m for m in masks]
+            part = jnp.concatenate(part, axis=0)
+            r = lax.dot_general(
+                part, buf[256:, c : c + 1024], NT_DIMS, preferred_element_type=F32
+            )
+            l = lax.dot_general(
+                part[:512], buf[:256, c : c + 1024], NT_DIMS, preferred_element_type=F32
+            )
+            right = r if right is None else right + r
+            left = l if left is None else left + l
+    two = 2 * TILE
+    a_ref[:, :256] = left[:two]
+    a_ref[:, 256:512] = right[:two]
+    a_ref[:, 512:] = right[2 * two : 3 * two, TILE:]
+    b_ref[:, :TILE] = left[two:, TILE:]
+    b_ref[:, TILE:384] = right[two : 2 * two]
+    b_ref[:, 384:] = right[3 * two :]
+
+
+def born_gram_kernel(pool_ref, out_ref):
+    pool = pool_ref[...].reshape(-1, W)
+    dims = (((0,), (0,)), ((), ()))
+    out_ref[...] = lax.dot_general(pool, pool, dims, preferred_element_type=F32)
 
 
 def lane_copy(x, c):
@@ -218,8 +213,6 @@
 
 
 def factor_kernel(ka, ra, a2, kb, rb, b2, born, mass, out_ref, a_ref):
-    pool = born[...]
-    born_gram = lax.dot_general(pool, pool, (((0,), (0,)), ((), ())), preferred_element_type=F32)
     sub = lax.broadcasted_iota(jnp.int32, (TILE, TILE), 0)
     lane = lax.broadcasted_iota(jnp.int32, (TILE, TILE), 1)
     own = slice(0, TILE)
@@ -227,7 +220,7 @@
         for panel, first, at in half:
             cols = slice(at, at + W - first)
             rows = slice(panel * TILE, (panel + 1) * TILE)
-            g = k0[own, cols] + r0[own, cols] + s0[:, cols] + born_gram[rows, first:]
+            g = k0[own, cols] + r0[own, cols] + s0[:, cols] + born[rows, first:]
             a_ref[rows, first:] = g * (1.0 / W)
     for k in range(4):
         rows = slice(TILE * k, TILE * (k + 1))
@@ -254,74 +247,62 @@
     rep = lax.axis_index("rep").astype(jnp.int32).reshape(1)
     shape = jax.ShapeDtypeStruct
     lists = send_lists.reshape(1, -1)
-    pick_flops = 2 * W * rows * listed
-
-    cols, to_upper = call(
-        upper_list_kernel,
-        (shape((W, rows), BF16), shape((W, listed), BF16)),
-        pick_flops + 2 * W * W * rows,
+    narrow = shape((W, listed), BF16)
+    cols, to_lower, to_upper = call(
+        listed_kernel,
+        (shape((W, rows), BF16), narrow, narrow),
+        4 * W * rows * listed + 2 * W * W * rows,
         elem_rows,
         lists,
-        name="upper_list",
+        name="listed",
     )
     up = [(i, i + 1) for i in range(dom_size - 1)]
     down = [(j, i) for i, j in up]
     from_lower = lax.ppermute(to_upper, "dom", up)
-    to_lower = call(
-        lower_list_kernel, shape((W, listed), BF16), pick_flops, cols, lists, name="lower_list"
-    )
     from_upper = lax.ppermute(to_lower, "dom", down)
 
     slots = dom_size * rep_size
     packed = call(
         pack_kernel,
-        shape((slots * CAP, W), BF16),
+        shape((slots, CAP, W), BF16),
         2 * slots * CAP * W * W,
         born_owner.reshape(1, -1),
         born_rows,
         name="pack_born",
     )
-    arrived = lax.all_to_all(
-        packed.reshape(slots, CAP, W), ("dom", "rep"), split_axis=0, concat_axis=0, tiled=True
-    ).reshape(slots * CAP, W)
+    arrived = lax.all_to_all(packed, ("dom", "rep"), split_axis=0, concat_axis=0, tiled=True)
+    born_gram = call(
+        born_gram_kernel, shape((W, W), F32), 2 * slots * CAP * W * W, arrived, name="born_gram"
+    )
 
     part = shape((2 * TILE, HALF_W), F32)
-    gram_flops = 4 * 6 * 2 * TILE * 256 * rows
-    ids = elem_block.reshape(1, -1)
-    sa, sb, ka, kb = call(
-        elem_gram_kernel, (part,) * 4, gram_flops, rep, cols, ids, smem=(0,), name="elem_gram"
-    )
-    halo_ids = halo_block.reshape(1, -1)
-    sa, sb = call(
-        sent_gram_kernel,
-        (part,) * 2,
-        gram_flops // 2,
-        rep,
-        from_lower,
-        from_upper,
-        halo_ids,
-        sa,
-        sb,
-        smem=(0,),
-        name="sent_gram",
-    )
+
+    def gram(kept):
+        return call(
+            functools.partial(gram_kernel, kept),
+            (part,) * 2,
+            2 * 6 * 2 * TILE * 256 * (rows + 2 * listed),
+            rep,
+            cols,
+            from_lower,
+            from_upper,
+            elem_block.reshape(1, -1),
+            halo_block.reshape(1, -1),
+            smem=(0,),
+            anywhere=(1, 2, 3),
+            scratch=(
+                pltpu.VMEM((W, rows + 2 * listed), BF16),
+                pltpu.SemaphoreType.DMA((3,)),
+            ),
+            name="kept_gram" if kept else "sent_gram",
+        )
+
+    sa, sb = gram(False)
     pair = [(i, i ^ 1) for i in range(rep_size)]
     mirror = [(i, 3 - i) for i in range(rep_size)]
     ra = lax.ppermute(sa, "rep", pair)
     rb = lax.ppermute(sb, "rep", mirror)
-    ka, kb = call(
-        kept_gram_kernel,
-        (part,) * 2,
-        gram_flops // 2,
-        rep,
-        from_lower,
-        from_upper,
-        halo_ids,
-        ka,
-        kb,
-        smem=(0,),
-        name="kept_gram",
-    )
+    ka, kb = gram(True)
     a2 = lax.ppermute(ka[TILE:] + ra[TILE:], "rep", mirror)
     b2 = lax.ppermute(kb[TILE:] + rb[TILE:], "rep", pair)
     return call(
@@ -334,7 +315,7 @@
         kb,
         rb,
         b2,
-        arrived,
+        born_gram,
         mass.reshape(1, -1),
         scratch=(pltpu.VMEM((W, W), F32),),
         name="factor",

time: 111 us -> 103 us (0.928); the launches traced: 111 us -> 101 us
  Pallas kernels: 52.3 us -> 42.8 us
  local copies, waits for them, and re-layouts: 5.33 us -> 8.42 us
  other arithmetic: 3.16 us -> 1.51 us
  waiting for transfers between devices: 21 us -> 19.8 us
    ppermute x1, waiting for transfers between devices: 13.7 us -> 0.01 us  [local(): ra = lax.ppermute(sa, 'rep', pair)]
    ppermute x1, waiting for transfers between devices: 0.01 us -> 12.8 us  [local(): rb = lax.ppermute(sb, 'rep', mirror)]
    pallas_call x7 -> x6, Pallas kernels: 52.3 us -> 42.8 us  [call(): pl.pallas_call(kernel, out_shape=outs, in_specs=specs, out_specs=pl.Block...]
    unnamed x12 -> x30, local copies, waits for them, and re-layouts: 2.05 us -> 8.42 us
    reshape x2 -> x0, local copies, waits for them, and re-layouts: 3.28 us -> none  [the longest x1 2.16 us: local(): packed.reshape(slots, CAP, W)]
    ppermute x1, starting transfers between devices: 3.38 us -> 1.8 us  [local(): a2 = lax.ppermute(ka[TILE:] + ra[TILE:], 'rep', mirror)]
    ppermute x1, starting transfers between devices: 0.01 us -> 1.45 us  [local(): b2 = lax.ppermute(kb[TILE:] + rb[TILE:], 'rep', pair)]
    ppermute x1, starting transfers between devices: 1.39 us -> 0.01 us  [local(): ra = lax.ppermute(sa, 'rep', pair)]
  transfers between devices with their start and end apart: 7 -> 7, of which waited for: 3 -> 3; matrix products, arithmetic and copies ran while one was open for 6% -> 1% of each run, Pallas kernels for 21% -> 14%
where the time goes in v2:
time: 103 us; the launch traced here: 101 us
  Pallas kernels  42.8 us (42%)
  starting transfers between devices  28.7 us (28%)
  waiting for transfers between devices  19.8 us (19%)
  local copies, waits for them, and re-layouts  8.42 us (8%)
  other arithmetic  1.51 us (1%)
    pallas_call x6, Pallas kernels, call(): pl.pallas_call(kernel, out_shape=outs, in_specs=specs, out_specs=pl.Block...  42.8 us
    all_to_all x1, starting transfers between devices, local(): lax.all_to_all(packed, ('dom', 'rep'), split_axis=0, concat_axis=0, tiled...  15.6 us
    ppermute x1, waiting for transfers between devices, local(): rb = lax.ppermute(sb, 'rep', mirror)  12.8 us
    unnamed x30, local copies, waits for them, and re-layouts  8.42 us
    ppermute x1, starting transfers between devices, local(): from_lower = lax.ppermute(to_upper, 'dom', up)  5.04 us
    ppermute x1, waiting for transfers between devices, local(): a2 = lax.ppermute(ka[TILE:] + ra[TILE:], 'rep', mirror)  3.88 us
    ppermute x1, waiting for transfers between devices, local(): b2 = lax.ppermute(kb[TILE:] + rb[TILE:], 'rep', pair)  3.07 us
    ppermute x1, starting transfers between devices, local(): rb = lax.ppermute(sb, 'rep', mirror)  2.91 us
  transfers between devices with their start and end apart: 7, of which 3 were waited for; matrix products, arithmetic and copies ran while one was open for 1% of the time, Pallas kernels for 14%

profile of v2, /device:TPU:1, one launch (start us, length us, event | category | flops | bytes accessed | tf_op | source)
XLA Modules:
  0.0 101.4 jit_solution(3500165035476784208)
XLA Ops:
  0.0 1.6 %copy-done.3 = bf16[2048,512]{1,0:T(8,128)(2,1)S(1)} copy-done((bf16[2048,512]{1,0:T(8,128)(2,1)S(1)}, bf16[2048,512]{1,0:T(8,128)(2,1)}, u32[]{:S(2)}) %copy-start.3) | copy-done | bytes 2097176
  1.6 0.7 copy-done.9
  2.3 8.0 %listed.1 = (bf16[512,2048]{1,0:T(8,128)(2,1)S(1)}, bf16[512,1024]{1,0:T(8,128)(2,1)}, bf16[512,1024]{1,0:T(8,128)(2,1)}) custom-call(bf16[2048,512]{1,0:T(8,128)(2,1)S(1)} %copy-done.3, s32[1,2048]{1,0:T(1,128)S(1)} %bitcast.7), custom_call_target="tpu_custom_call" | custom-call | flops 5368709120 | bytes 2105344 | tf_op jit(solution)/shard_map/listed/pallas_call | solution.py:31
  10.3 1.3 %copy-done.13 = bf16[512,2048]{1,0:T(8,128)(2,1)} copy-done((bf16[512,2048]{1,0:T(8,128)(2,1)}, bf16[512,2048]{1,0:T(8,128)(2,1)S(1)}, u32[]{:S(2)}) %copy-start.13) | copy-done | bytes 2097176
  11.7 5.0 %collective-permute-start = (bf16[512,1024]{1,0:T(8,128)(2,1)}, bf16[512,1024]{1,0:T(8,128)(2,1)S(1)}, u32[]{:S(2)}, u32[]{:S(2)}) collective-permute-start(bf16[512,1024]{1,0:T(8,128)(2,1)} %get-tuple-element.13), channel_id=1, source_target_pairs={{0,4},{4,8},{8,12},{12,16},{16,20},{20,24},{24,28},{28,32},{32,36}... | collective-permute-start | bytes 3145736 | tf_op jit(solution)/shard_map/ppermute | solution.py:261
  16.7 1.9 %collective-permute-start.1 = (bf16[512,1024]{1,0:T(8,128)(2,1)}, bf16[512,1024]{1,0:T(8,128)(2,1)S(1)}, u32[]{:S(2)}, u32[]{:S(2)}) collective-permute-start(bf16[512,1024]{1,0:T(8,128)(2,1)} %get-tuple-element.14), channel_id=1, source_target_pairs={{4,0},{8,4},{12,8},{16,12},{20,16},{24,20},{28,24},{32,28},{36,32}... | collective-permute-start | bytes 3145736 | tf_op jit(solution)/shard_map/ppermute | solution.py:262
  18.7 2.0 %pack_born.1 = bf16[256,4,512]{2,1,0:T(4,128)(2,1)} custom-call(s32[1,512]{1,0:T(1,128)S(1)} %bitcast.12, bf16[512,512]{1,0:T(8,128)(2,1)S(1)} %copy-done.8), custom_call_target="tpu_custom_call" | custom-call | flops 536870912 | bytes 526336 | tf_op jit(solution)/shard_map/pack_born/pallas_call | solution.py:31
  20.6 15.6 %all-to-all-start = ((bf16[256,4,512]{2,1,0:T(4,128)(2,1)}), bf16[256,4,512]{2,1,0:T(4,128)(2,1)S(1)}, u32[]{:S(2)}, u32[]{:S(2)}) async-start(bf16[256,4,512]{2,1,0:T(4,128)(2,1)} %pack_born.1), calls=%async_computation | async-start | bytes 2097152 | tf_op jit(solution)/shard_map/all_to_all | solution.py:273
  36.2 0.0 collective-permute-done.lo
  36.2 0.0 copy-start.4
  36.2 0.0 collective-permute-done.1.up
  36.3 0.0 copy-start.6
  36.3 2.3 %copy-done.14 = bf16[512,2048]{1,0:T(8,128)(2,1)S(1)} copy-done((bf16[512,2048]{1,0:T(8,128)(2,1)S(1)}, bf16[512,2048]{1,0:T(8,128)(2,1)}, u32[]{:S(2)}) %copy-start.14) | copy-done | bytes 2097176
  38.6 5.6 %sent_gram.1 = (f32[256,640]{1,0:T(8,128)S(1)}, f32[256,640]{1,0:T(8,128)S(1)}) custom-call(s32[1]{0:T(128)} %bitcast.rep_ref, bf16[512,2048]{1,0:T(8,128)(2,1)S(1)} %copy-done.14, bf16[512,1024]{1,0:T(8,128)(2,1)S(1)} %collective-permute-done.lo, bf16[512,1024]{1,0:T(8,128)(2,1)S(1)} %collective-permute-done.1.up, s32[1,2048]{1,0:T(1,128)S(1)} %bitcast.8, ...), custom_call_target="tpu_custom_call" | custom-call | flops 3221225472 | bytes 4210692 | tf_op jit(solution)/shard_map/sent_gram/pallas_call | solution.py:31
  44.2 2.9 %collective-permute-start.4 = (f32[256,640]{1,0:T(8,128)S(1)}, f32[256,640]{1,0:T(8,128)S(1)}, u32[]{:S(2)}, u32[]{:S(2)}) collective-permute-start(f32[256,640]{1,0:T(8,128)S(1)} %get-tuple-element.18), channel_id=1, source_target_pairs={{0,3},{1,2},{2,1},{3,0},{4,7},{5,6},{6,5},{7,4},{8,11},{9,10},{10,... | collective-permute-start | bytes 1966088 | tf_op jit(solution)/shard_map/ppermute | solution.py:304
  47.1 0.0 collective-permute-start.2
  47.1 1.2 %copy-done.5 = bf16[512,1024]{1,0:T(8,128)(2,1)S(1)} copy-done((bf16[512,1024]{1,0:T(8,128)(2,1)S(1)}, bf16[512,1024]{1,0:T(8,128)(2,1)}, u32[]{:S(2)}) %copy-start.5) | copy-done | bytes 1048600
  48.3 1.2 %copy-done.7 = bf16[512,1024]{1,0:T(8,128)(2,1)S(1)} copy-done((bf16[512,1024]{1,0:T(8,128)(2,1)S(1)}, bf16[512,1024]{1,0:T(8,128)(2,1)}, u32[]{:S(2)}) %copy-start.7) | copy-done | bytes 1048600
  49.6 5.5 %kept_gram.1 = (f32[256,640]{1,0:T(8,128)S(1)}, f32[256,640]{1,0:T(8,128)S(1)}) custom-call(s32[1]{0:T(128)} %bitcast.rep_ref, bf16[512,2048]{1,0:T(8,128)(2,1)S(1)} %copy-done.14, bf16[512,1024]{1,0:T(8,128)(2,1)S(1)} %copy-done.5, bf16[512,1024]{1,0:T(8,128)(2,1)S(1)} %copy-done.7, s32[1,2048]{1,0:T(1,128)S(1)} %bitcast.9, s32[1,2048]{1,0:T(1,128)S(1)} %bitcast.11), custom_call_target="tpu_custom_call" | custom-call | flops 3221225472 | bytes 4210692 | tf_op jit(solution)/shard_map/kept_gram/pallas_call | solution.py:31
  55.0 0.0 copy-start
  55.0 0.0 copy-start.2
  55.1 12.8 %collective-permute-done.4.rb = f32[256,640]{1,0:T(8,128)S(1)} collective-permute-done((f32[256,640]{1,0:T(8,128)S(1)}, f32[256,640]{1,0:T(8,128)S(1)}, u32[]{:S(2)}, u32[]{:S(2)}) %collective-permute-start.4) | collective-permute-done | bytes 655392 | tf_op jit(solution)/shard_map/ppermute | solution.py:304
  67.8 0.8 slice_add_fusion
  68.6 1.5 %collective-permute-start.5 = (f32[128,640]{1,0:T(8,128)}, f32[128,640]{1,0:T(8,128)S(1)}, u32[]{:S(2)}, u32[]{:S(2)}) collective-permute-start(f32[128,640]{1,0:T(8,128)} %slice_add_fusion), channel_id=1, source_target_pairs={{0,1},{1,0},{2,3},{3,2},{4,5},{5,4},{6,7},{7,6},{8,9},{9,8},{10,11... | collective-permute-start | bytes 983048 | tf_op jit(solution)/shard_map/ppermute | solution.py:307
  70.1 0.0 collective-permute-done.2.ra
  70.1 0.8 slice_add_fusion.1
  70.8 1.8 %collective-permute-start.3 = (f32[128,640]{1,0:T(8,128)}, f32[128,640]{1,0:T(8,128)}, u32[]{:S(2)}, u32[]{:S(2)}) collective-permute-start(f32[128,640]{1,0:T(8,128)} %slice_add_fusion.1), channel_id=1, source_target_pairs={{0,3},{1,2},{2,1},{3,0},{4,7},{5,6},{6,5},{7,4},{8,11},{9,10},{10,... | collective-permute-start | bytes 983048 | tf_op jit(solution)/shard_map/ppermute | solution.py:306
  72.6 0.0 all-to-all-done.pool_ref
  72.6 0.7 born_gram.1.born
  73.4 3.1 %collective-permute-done.5.b2 = f32[128,640]{1,0:T(8,128)S(1)} collective-permute-done((f32[128,640]{1,0:T(8,128)}, f32[128,640]{1,0:T(8,128)S(1)}, u32[]{:S(2)}, u32[]{:S(2)}) %collective-permute-start.5) | collective-permute-done | bytes 327712 | tf_op jit(solution)/shard_map/ppermute | solution.py:307
  76.4 3.9 %collective-permute-done.3.a2 = f32[128,640]{1,0:T(8,128)} collective-permute-done((f32[128,640]{1,0:T(8,128)}, f32[128,640]{1,0:T(8,128)}, u32[]{:S(2)}, u32[]{:S(2)}) %collective-permute-start.3) | collective-permute-done | bytes 327712 | tf_op jit(solution)/shard_map/ppermute | solution.py:306
  80.3 21.0 %factor.1 = f32[512,512]{1,0:T(8,128)} custom-call(f32[256,640]{1,0:T(8,128)S(1)} %get-tuple-element.15.ka, f32[256,640]{1,0:T(8,128)S(1)} %collective-permute-done.2.ra, f32[128,640]{1,0:T(8,128)} %collective-permute-done.3.a2, f32[256,640]{1,0:T(8,128)S(1)} %copy-done.1, f32[256,640]{1,0:T(8,128)S(1)} %collective-permute-done.4.rb, ...), custom_call_target="tpu_custom_call" | custom-call | flops 1000000000 | bytes 4327424 | tf_op jit(solution)/shard_map/factor/pallas_call | solution.py:31
  (20 shorter events, 0.0 us)
Async XLA Ops:
  0.0 1.6 %copy-start.3 = (bf16[2048,512]{1,0:T(8,128)(2,1)S(1)}, bf16[2048,512]{1,0:T(8,128)(2,1)}, u32[]{:S(2)}) copy-start(bf16[2048,512]{1,0:T(8,128)(2,1)} %rows_ref.2) | copy-start | bytes 6291460
  1.6 0.7 copy-start.9
  2.3 16.3 %copy-start.8 = (bf16[512,512]{1,0:T(8,128)(2,1)S(1)}, bf16[512,512]{1,0:T(8,128)(2,1)}, u32[]{:S(2)}) copy-start(bf16[512,512]{1,0:T(8,128)(2,1)} %rows_ref.3) | copy-start | bytes 1572868
  2.3 16.4 %copy-start.12 = (s32[512,1]{0,1:T(1,128)S(1)}, s32[512,1]{0,1:T(1,128)}, u32[]{:S(2)}) copy-start(s32[512,1]{0,1:T(1,128)} %param.12) | copy-start | bytes 6148
  10.3 1.3 %copy-start.13 = (bf16[512,2048]{1,0:T(8,128)(2,1)}, bf16[512,2048]{1,0:T(8,128)(2,1)S(1)}, u32[]{:S(2)}) copy-start(bf16[512,2048]{1,0:T(8,128)(2,1)S(1)} %get-tuple-element.12.cols) | copy-start | bytes 6291460
  11.7 24.6 %copy-start.10 = (s32[2048]{0:T(1024)S(1)}, s32[2048]{0:T(1024)}, u32[]{:S(2)}) copy-start(s32[2048]{0:T(1024)} %param.8) | copy-start | bytes 24580
  11.7 24.6 %copy-start.11 = (s32[2048]{0:T(1024)S(1)}, s32[2048]{0:T(1024)}, u32[]{:S(2)}) copy-start(s32[2048]{0:T(1024)} %param.10) | copy-start | bytes 24580
  11.7 24.6 %collective-permute-start = (bf16[512,1024]{1,0:T(8,128)(2,1)}, bf16[512,1024]{1,0:T(8,128)(2,1)S(1)}, u32[]{:S(2)}, u32[]{:S(2)}) collective-permute-start(bf16[512,1024]{1,0:T(8,128)(2,1)} %get-tuple-element.13), channel_id=1, source_target_pairs={{0,4},{4,8},{8,12},{12,16},{16,20},{20,24},{24,28},{28,32},{32,36}... | collective-permute-start | bytes 3145736 | tf_op jit(solution)/shard_map/ppermute | solution.py:261
  16.7 19.5 %collective-permute-start.1 = (bf16[512,1024]{1,0:T(8,128)(2,1)}, bf16[512,1024]{1,0:T(8,128)(2,1)S(1)}, u32[]{:S(2)}, u32[]{:S(2)}) collective-permute-start(bf16[512,1024]{1,0:T(8,128)(2,1)} %get-tuple-element.14), channel_id=1, source_target_pairs={{4,0},{8,4},{12,8},{16,12},{20,16},{24,20},{28,24},{32,28},{36,32}... | collective-permute-start | bytes 3145736 | tf_op jit(solution)/shard_map/ppermute | solution.py:262
  20.6 52.0 %all-to-all-start = ((bf16[256,4,512]{2,1,0:T(4,128)(2,1)}), bf16[256,4,512]{2,1,0:T(4,128)(2,1)S(1)}, u32[]{:S(2)}, u32[]{:S(2)}) async-start(bf16[256,4,512]{2,1,0:T(4,128)(2,1)} %pack_born.1), calls=%async_computation | async-start | bytes 2097152 | tf_op jit(solution)/shard_map/all_to_all | solution.py:273
  36.2 7.9 %copy-start.4 = (bf16[512,1024]{1,0:T(8,128)(2,1)}, bf16[512,1024]{1,0:T(8,128)(2,1)S(1)}, u32[]{:S(2)}) copy-start(bf16[512,1024]{1,0:T(8,128)(2,1)S(1)} %collective-permute-done.lo) | copy-start | bytes 3145732
  36.3 7.9 %copy-start.6 = (bf16[512,1024]{1,0:T(8,128)(2,1)}, bf16[512,1024]{1,0:T(8,128)(2,1)S(1)}, u32[]{:S(2)}) copy-start(bf16[512,1024]{1,0:T(8,128)(2,1)S(1)} %collective-permute-done.1.up) | copy-start | bytes 3145732
  36.3 2.3 %copy-start.14 = (bf16[512,2048]{1,0:T(8,128)(2,1)S(1)}, bf16[512,2048]{1,0:T(8,128)(2,1)}, u32[]{:S(2)}) copy-start(bf16[512,2048]{1,0:T(8,128)(2,1)} %copy-done.13) | copy-start | bytes 6291460
  44.2 23.7 %collective-permute-start.4 = (f32[256,640]{1,0:T(8,128)S(1)}, f32[256,640]{1,0:T(8,128)S(1)}, u32[]{:S(2)}, u32[]{:S(2)}) collective-permute-start(f32[256,640]{1,0:T(8,128)S(1)} %get-tuple-element.18), channel_id=1, source_target_pairs={{0,3},{1,2},{2,1},{3,0},{4,7},{5,6},{6,5},{7,4},{8,11},{9,10},{10,... | collective-permute-start | bytes 1966088 | tf_op jit(solution)/shard_map/ppermute | solution.py:304
  47.1 22.9 %collective-permute-start.2 = (f32[256,640]{1,0:T(8,128)S(1)}, f32[256,640]{1,0:T(8,128)S(1)}, u32[]{:S(2)}, u32[]{:S(2)}) collective-permute-start(f32[256,640]{1,0:T(8,128)S(1)} %get-tuple-element.16), channel_id=1, source_target_pairs={{0,1},{1,0},{2,3},{3,2},{4,5},{5,4},{6,7},{7,6},{8,9},{9,8},{10,11... | collective-permute-start | bytes 1966088 | tf_op jit(solution)/shard_map/ppermute | solution.py:303
  47.1 1.2 %copy-start.5 = (bf16[512,1024]{1,0:T(8,128)(2,1)S(1)}, bf16[512,1024]{1,0:T(8,128)(2,1)}, u32[]{:S(2)}) copy-start(bf16[512,1024]{1,0:T(8,128)(2,1)} %copy-done.4) | copy-start | bytes 3145732
  48.3 1.2 %copy-start.7 = (bf16[512,1024]{1,0:T(8,128)(2,1)S(1)}, bf16[512,1024]{1,0:T(8,128)(2,1)}, u32[]{:S(2)}) copy-start(bf16[512,1024]{1,0:T(8,128)(2,1)} %copy-done.6) | copy-start | bytes 3145732
  55.0 15.8 %copy-start = (f32[256,640]{1,0:T(8,128)}, f32[256,640]{1,0:T(8,128)S(1)}, u32[]{:S(2)}) copy-start(f32[256,640]{1,0:T(8,128)S(1)} %get-tuple-element.17.kb) | copy-start | bytes 1966084
  55.0 25.3 %copy-start.2 = (f32[512]{0:T(512)S(1)}, f32[512]{0:T(512)}, u32[]{:S(2)}) copy-start(f32[512]{0:T(512)} %param.13) | copy-start | bytes 6148
  68.6 7.8 %collective-permute-start.5 = (f32[128,640]{1,0:T(8,128)}, f32[128,640]{1,0:T(8,128)S(1)}, u32[]{:S(2)}, u32[]{:S(2)}) collective-permute-start(f32[128,640]{1,0:T(8,128)} %slice_add_fusion), channel_id=1, source_target_pairs={{0,1},{1,0},{2,3},{3,2},{4,5},{5,4},{6,7},{7,6},{8,9},{9,8},{10,11... | collective-permute-start | bytes 983048 | tf_op jit(solution)/shard_map/ppermute | solution.py:307
  70.8 9.5 %collective-permute-start.3 = (f32[128,640]{1,0:T(8,128)}, f32[128,640]{1,0:T(8,128)}, u32[]{:S(2)}, u32[]{:S(2)}) collective-permute-start(f32[128,640]{1,0:T(8,128)} %slice_add_fusion.1), channel_id=1, source_target_pairs={{0,3},{1,2},{2,1},{3,0},{4,7},{5,6},{6,5},{7,4},{8,11},{9,10},{10,... | collective-permute-start | bytes 983048 | tf_op jit(solution)/shard_map/ppermute | solution.py:306
  72.6 7.7 %copy-start.1 = (f32[256,640]{1,0:T(8,128)S(1)}, f32[256,640]{1,0:T(8,128)}, u32[]{:S(2)}) copy-start(f32[256,640]{1,0:T(8,128)} %copy-done) | copy-start | bytes 1966084

commit v3 on v2

--- a/solution.py
+++ b/solution.py
@@ -13,16 +13,17 @@
 F32 = jnp.float32
 BF16 = jnp.bfloat16
 VMEM_LIMIT = 32 * 1024 * 1024
+VMEM_WHOLE = 63 * 1024 * 1024 + 512 * 1024
 NT_DIMS = (((1,), (1,)), ((), ()))
 HALF_A = ((0, 0, 0), (3, 384, 512))
 HALF_B = ((1, 128, 0), (2, 256, 384))
 HALF_W = 640
 
 
-def call(kernel, outs, flops, *args, smem=(), anywhere=(), scratch=(), name=None):
+def call(kernel, outs, flops, *args, smem=(), anywhere=(), scratch=(), vmem=VMEM_WHOLE, name=None):
     specs = [
         pl.BlockSpec(
-            memory_space=pltpu.SMEM if i in smem else pl.ANY if i in anywhere else pltpu.VMEM
+            memory_space=pltpu.SMEM if i in smem else pltpu.HBM if i in anywhere else pltpu.VMEM
         )
         for i in range(len(args))
     ]
@@ -36,7 +37,7 @@
         if single
         else [pl.BlockSpec(memory_space=pltpu.VMEM)] * len(outs),
         scratch_shapes=list(scratch),
-        compiler_params=pltpu.CompilerParams(vmem_limit_bytes=VMEM_LIMIT),
+        compiler_params=pltpu.CompilerParams(vmem_limit_bytes=vmem),
         cost_estimate=pl.CostEstimate(flops=flops, bytes_accessed=size, transcendentals=0),
         name=name,
     )(*args)
@@ -48,10 +49,18 @@
     return lax.dot_general(eye, rows, NT_DIMS, preferred_element_type=F32).astype(BF16)
 
 
-def listed_kernel(rows_ref, list_ref, cols_ref, lower_ref, upper_ref):
+def listed_kernel(rows_ref, list_ref, cols_ref, lower_ref, upper_ref, rows, sems):
     total, listed = rows_ref.shape[0], lower_ref.shape[1]
-    for c in range(0, total, 512):
-        cols_ref[:, c : c + 512] = transposed(rows_ref[c : c + 512, :])
+    piece = total // sems.shape[0]
+    copies = []
+    for i in range(sems.shape[0]):
+        part = pl.ds(i * piece, piece)
+        copies.append(pltpu.make_async_copy(rows_ref.at[part, :], rows.at[part, :], sems.at[i]))
+        copies[-1].start()
+    for i, copy in enumerate(copies):
+        copy.wait()
+        c = i * piece
+        cols_ref[:, c : c + piece] = transposed(rows[c : c + piece, :])
     step, deep = 256, 256
     places = lax.broadcasted_iota(jnp.int32, (deep, step), 0).astype(BF16)
     for out_ref, first in ((upper_ref, listed), (lower_ref, 0)):
@@ -176,14 +185,31 @@
     return inv
 
 
+SUB = 64
+
+
 def factor_panel(a_ref, tiles):
     sub = lax.broadcasted_iota(jnp.int32, (8, TILE), 0)
     lane = lax.broadcasted_iota(jnp.int32, (8, TILE), 1)
     cols = [slice(TILE * c, TILE * c + TILE) for c in range(tiles)]
+    pivot = None
     for s in range(16):
         o = 8 * s
-        head = a_ref[o : o + 8, cols[0]]
-        inv = inverse_factor([lane_copy(head, o + j) for j in range(8)])
+        last = (o // SUB + 1) * SUB // 8
+        if pivot is None:
+            head = a_ref[o : o + 8, cols[0]]
+            pivot = [lane_copy(head, o + j) for j in range(8)]
+        inv = inverse_factor(pivot)
+        pivot = near = None
+        if s + 1 < last:
+            head = a_ref[o + 8 : o + 16, cols[0]]
+            b = [lane_copy(head, o + m) for m in range(8)]
+            own = [lane_copy(head, o + 8 + j) for j in range(8)]
+            near = [add_all([inv[j][m] * b[m] for m in range(j + 1)]) for j in range(8)]
+            pivot = [
+                own[j] - add_all([near[m] * row_copy(near[m], j) for m in range(8)])
+                for j in range(8)
+            ]
         columns = []
         for m in range(8):
             v = inv[7][m]
@@ -199,17 +225,27 @@
         upper[0] = jnp.where(lane >= sub + o, upper[0], 0.0)
         for u, c in zip(upper, cols):
             a_ref[o : o + 8, c] = u
-        if s == 15:
-            break
-        spread = [[row_copy(u, j) for j in range(8)] for u in upper]
-        for g in range(s + 1, 16):
-            rows = slice(8 * g, 8 * g + 8)
-            x = a_ref[rows, cols[0]]
-            b = [lane_copy(x, o + m) for m in range(8)]
-            low = [add_all([inv[j][m] * b[m] for m in range(j + 1)]) for j in range(8)]
-            for i, c in enumerate(cols):
-                y = x if i == 0 else a_ref[rows, c]
-                a_ref[rows, c] = y - add_all([low[j] * spread[i][j] for j in range(8)])
+        if s + 1 < last:
+            spread = [[row_copy(u, j) for j in range(8)] for u in upper]
+            for g in range(s + 1, last):
+                rows = slice(8 * g, 8 * g + 8)
+                x = a_ref[rows, cols[0]]
+                low = near
+                if g > s + 1:
+                    b = [lane_copy(x, o + m) for m in range(8)]
+                    low = [add_all([inv[j][m] * b[m] for m in range(j + 1)]) for j in range(8)]
+                for i, c in enumerate(cols):
+                    y = x if i == 0 else a_ref[rows, c]
+                    a_ref[rows, c] = y - add_all([low[j] * spread[i][j] for j in range(8)])
+        elif s + 1 < 16:
+            done = a_ref[o + 8 - SUB : o + 8, :]
+            a_ref[o + 8 : TILE, :] = a_ref[o + 8 : TILE, :] - lax.dot_general(
+                done[:, o + 8 : TILE],
+                done,
+                (((0,), (0,)), ((), ())),
+                precision=lax.Precision.HIGHEST,
+                preferred_element_type=F32,
+            )
 
 
 def factor_kernel(ka, ra, a2, kb, rb, b2, born, mass, out_ref, a_ref):
@@ -254,6 +290,8 @@
         4 * W * rows * listed + 2 * W * W * rows,
         elem_rows,
         lists,
+        anywhere=(0,),
+        scratch=(pltpu.VMEM((rows, W), BF16), pltpu.SemaphoreType.DMA((4,))),
         name="listed",
     )
     up = [(i, i + 1) for i in range(dom_size - 1)]
@@ -272,7 +310,7 @@
     )
     arrived = lax.all_to_all(packed, ("dom", "rep"), split_axis=0, concat_axis=0, tiled=True)
     born_gram = call(
-        born_gram_kernel, shape((W, W), F32), 2 * slots * CAP * W * W, arrived, name="born_gram"
+        born_gram_kernel, shape((W, W), F32), 2 * slots * CAP * W * W, arrived, vmem=VMEM_LIMIT, name="born_gram"
     )
 
     part = shape((2 * TILE, HALF_W), F32)
@@ -318,6 +356,7 @@
         born_gram,
         mass.reshape(1, -1),
         scratch=(pltpu.VMEM((W, W), F32),),
+        vmem=VMEM_LIMIT,
         name="factor",
     )
 

time: 103 us -> 98.5 us (0.956)
  local copies, waits for them, and re-layouts: 8.42 us -> 0.02 us
  Pallas kernels: 42.8 us -> 47.2 us
  waiting for transfers between devices: 19.8 us -> 18 us
  starting transfers between devices: 28.7 us -> 29.8 us
    unnamed x30 -> x6, local copies, waits for them, and re-layouts: 8.42 us -> 0.02 us
    pallas_call x6, Pallas kernels: 42.8 us -> 47.2 us  [call(): pl.pallas_call(kernel, out_shape=outs, in_specs=specs, out_specs=pl.Block...]
    ppermute x1, waiting for transfers between devices: 3.07 us -> 0.95 us  [local(): b2 = lax.ppermute(kb[TILE:] + rb[TILE:], 'rep', pair)]
  transfers between devices with their start and end apart: 7 -> 7, of which waited for: 3 -> 3; matrix products, arithmetic and copies ran while one was open for 1% -> 2% of each run, Pallas kernels for 14% -> 22%
where the time goes in v3:
time: 98.5 us; the launch traced here: 97.3 us
  Pallas kernels  47.2 us (48%)
  starting transfers between devices  29.8 us (30%)
  waiting for transfers between devices  18 us (18%)
  other arithmetic  2.21 us (2%)
    pallas_call x6, Pallas kernels, call(): pl.pallas_call(kernel, out_shape=outs, in_specs=specs, out_specs=pl.Block...  47.2 us
    all_to_all x1, starting transfers between devices, local(): lax.all_to_all(packed, ('dom', 'rep'), split_axis=0, concat_axis=0, tiled...  16 us
    ppermute x1, waiting for transfers between devices, local(): rb = lax.ppermute(sb, 'rep', mirror)  12.7 us
    ppermute x1, starting transfers between devices, local(): from_lower = lax.ppermute(to_upper, 'dom', up)  4.94 us
    ppermute x1, waiting for transfers between devices, local(): a2 = lax.ppermute(ka[TILE:] + ra[TILE:], 'rep', mirror)  4.31 us
    ppermute x1, starting transfers between devices, local(): rb = lax.ppermute(sb, 'rep', mirror)  2.92 us
    ppermute x1, starting transfers between devices, local(): from_upper = lax.ppermute(to_lower, 'dom', down)  2.46 us
    ppermute x1, starting transfers between devices, local(): a2 = lax.ppermute(ka[TILE:] + ra[TILE:], 'rep', mirror)  2.07 us
  transfers between devices with their start and end apart: 7, of which 3 were waited for; matrix products, arithmetic and copies ran while one was open for 2% of the time, Pallas kernels for 22%

profile of v3, /device:TPU:1, one launch (start us, length us, event | category | flops | bytes accessed | tf_op | source)
XLA Modules:
  0.0 97.3 jit_solution(14089407581881429696)
XLA Ops:
  0.0 10.6 %listed.1 = (bf16[512,2048]{1,0:T(8,128)(2,1)}, bf16[512,1024]{1,0:T(8,128)(2,1)}, bf16[512,1024]{1,0:T(8,128)(2,1)}) custom-call(bf16[2048,512]{1,0:T(8,128)(2,1)} %rows_ref.2, s32[1,2048]{1,0:T(1,128)} %bitcast.7), custom_call_target="tpu_custom_call" | custom-call | flops 5368709120 | bytes 2105344 | tf_op jit(solution)/shard_map/listed/pallas_call | solution.py:32
  10.6 4.9 %collective-permute-start = (bf16[512,1024]{1,0:T(8,128)(2,1)}, bf16[512,1024]{1,0:T(8,128)(2,1)}, u32[]{:S(2)}, u32[]{:S(2)}) collective-permute-start(bf16[512,1024]{1,0:T(8,128)(2,1)} %get-tuple-element.13), channel_id=1, source_target_pairs={{0,4},{4,8},{8,12},{12,16},{16,20},{20,24},{24,28},{28,32},{32,36}... | collective-permute-start | bytes 3145736 | tf_op jit(solution)/shard_map/ppermute | solution.py:299
  15.6 2.5 %collective-permute-start.1 = (bf16[512,1024]{1,0:T(8,128)(2,1)}, bf16[512,1024]{1,0:T(8,128)(2,1)}, u32[]{:S(2)}, u32[]{:S(2)}) collective-permute-start(bf16[512,1024]{1,0:T(8,128)(2,1)} %get-tuple-element.14), channel_id=1, source_target_pairs={{4,0},{8,4},{12,8},{16,12},{20,16},{24,20},{28,24},{32,28},{36,32}... | collective-permute-start | bytes 3145736 | tf_op jit(solution)/shard_map/ppermute | solution.py:300
  18.0 3.1 %pack_born.1 = bf16[256,4,512]{2,1,0:T(4,128)(2,1)} custom-call(s32[1,512]{1,0:T(1,128)} %bitcast.12, bf16[512,512]{1,0:T(8,128)(2,1)} %rows_ref.3), custom_call_target="tpu_custom_call" | custom-call | flops 536870912 | bytes 526336 | tf_op jit(solution)/shard_map/pack_born/pallas_call | solution.py:32
  21.1 16.0 %all-to-all-start = ((bf16[256,4,512]{2,1,0:T(4,128)(2,1)}), bf16[256,4,512]{2,1,0:T(4,128)(2,1)}, u32[]{:S(2)}, u32[]{:S(2)}) async-start(bf16[256,4,512]{2,1,0:T(4,128)(2,1)} %pack_born.1), calls=%async_computation | async-start | bytes 2097152 | tf_op jit(solution)/shard_map/all_to_all | solution.py:311
  37.1 0.0 collective-permute-done.lo
  37.1 0.0 collective-permute-done.1.up
  37.2 8.1 %sent_gram.1 = (f32[256,640]{1,0:T(8,128)}, f32[256,640]{1,0:T(8,128)}) custom-call(s32[1]{0:T(128)} %bitcast.rep_ref, bf16[512,2048]{1,0:T(8,128)(2,1)} %get-tuple-element.12.cols, bf16[512,1024]{1,0:T(8,128)(2,1)} %collective-permute-done.lo, bf16[512,1024]{1,0:T(8,128)(2,1)} %collective-permute-done.1.up, s32[1,2048]{1,0:T(1,128)} %bitcast.8, ...), custom_call_target="tpu_custom_call" | custom-call | flops 3221225472 | bytes 4210692 | tf_op jit(solution)/shard_map/sent_gram/pallas_call | solution.py:32
  45.2 2.9 %collective-permute-start.4 = (f32[256,640]{1,0:T(8,128)}, f32[256,640]{1,0:T(8,128)}, u32[]{:S(2)}, u32[]{:S(2)}) collective-permute-start(f32[256,640]{1,0:T(8,128)} %get-tuple-element.18), channel_id=1, source_target_pairs={{0,3},{1,2},{2,1},{3,0},{4,7},{5,6},{6,5},{7,4},{8,11},{9,10},{10,... | collective-permute-start | bytes 1966088 | tf_op jit(solution)/shard_map/ppermute | solution.py:342
  48.1 0.0 collective-permute-start.2
  48.2 8.0 %kept_gram.1 = (f32[256,640]{1,0:T(8,128)}, f32[256,640]{1,0:T(8,128)}) custom-call(s32[1]{0:T(128)} %bitcast.rep_ref, bf16[512,2048]{1,0:T(8,128)(2,1)} %get-tuple-element.12.cols, bf16[512,1024]{1,0:T(8,128)(2,1)} %collective-permute-done.lo, bf16[512,1024]{1,0:T(8,128)(2,1)} %collective-permute-done.1.up, s32[1,2048]{1,0:T(1,128)} %bitcast.9, ...), custom_call_target="tpu_custom_call" | custom-call | flops 3221225472 | bytes 4210692 | tf_op jit(solution)/shard_map/kept_gram/pallas_call | solution.py:32
  56.2 0.0 copy-start
  56.2 0.0 copy-start.1
  56.2 0.0 copy-start.2
  56.2 12.7 %collective-permute-done.4.rb = f32[256,640]{1,0:T(8,128)} collective-permute-done((f32[256,640]{1,0:T(8,128)}, f32[256,640]{1,0:T(8,128)}, u32[]{:S(2)}, u32[]{:S(2)}) %collective-permute-start.4) | collective-permute-done | bytes 655392 | tf_op jit(solution)/shard_map/ppermute | solution.py:342
  68.9 1.1 %slice_add_fusion = f32[128,640]{1,0:T(8,128)S(1)} fusion(f32[256,640]{1,0:T(8,128)} %collective-permute-done.4.rb, f32[256,640]{1,0:T(8,128)} %get-tuple-element.17.kb), kind=kLoop, calls=%fused_computation | loop fusion | flops 81920 | bytes 983040 | tf_op jit(solution)/shard_map/add | solution.py:345
  70.0 1.4 %collective-permute-start.5 = (f32[128,640]{1,0:T(8,128)S(1)}, f32[128,640]{1,0:T(8,128)S(1)}, u32[]{:S(2)}, u32[]{:S(2)}) collective-permute-start(f32[128,640]{1,0:T(8,128)S(1)} %slice_add_fusion), channel_id=1, source_target_pairs={{0,1},{1,0},{2,3},{3,2},{4,5},{5,4},{6,7},{7,6},{8,9},{9,8},{10,11... | collective-permute-start | bytes 983048 | tf_op jit(solution)/shard_map/ppermute | solution.py:345
  71.4 0.0 collective-permute-done.2.ra
  71.4 1.1 %slice_add_fusion.1 = f32[128,640]{1,0:T(8,128)S(1)} fusion(f32[256,640]{1,0:T(8,128)} %collective-permute-done.2.ra, f32[256,640]{1,0:T(8,128)} %get-tuple-element.15.ka), kind=kLoop, calls=%fused_computation.1 | loop fusion | flops 81920 | bytes 983040 | tf_op jit(solution)/shard_map/add | solution.py:344
  72.5 2.1 %collective-permute-start.3 = (f32[128,640]{1,0:T(8,128)S(1)}, f32[128,640]{1,0:T(8,128)S(1)}, u32[]{:S(2)}, u32[]{:S(2)}) collective-permute-start(f32[128,640]{1,0:T(8,128)S(1)} %slice_add_fusion.1), channel_id=1, source_target_pairs={{0,3},{1,2},{2,1},{3,0},{4,7},{5,6},{6,5},{7,4},{8,11},{9,10},{10,... | collective-permute-start | bytes 983048 | tf_op jit(solution)/shard_map/ppermute | solution.py:344
  74.6 0.0 all-to-all-done.pool_ref
  74.6 2.0 %born_gram.1.born = f32[512,512]{1,0:T(8,128)S(1)} custom-call(bf16[256,4,512]{2,1,0:T(4,128)(2,1)} %all-to-all-done.pool_ref), custom_call_target="tpu_custom_call" | custom-call | flops 536870912 | bytes 1048576 | tf_op jit(solution)/shard_map/born_gram/pallas_call | solution.py:32
  76.5 0.9 collective-permute-done.5.b2
  77.5 4.3 %collective-permute-done.3.a2 = f32[128,640]{1,0:T(8,128)S(1)} collective-permute-done((f32[128,640]{1,0:T(8,128)S(1)}, f32[128,640]{1,0:T(8,128)S(1)}, u32[]{:S(2)}, u32[]{:S(2)}) %collective-permute-start.3) | collective-permute-done | bytes 327712 | tf_op jit(solution)/shard_map/ppermute | solution.py:344
  81.8 0.0 copy-done
  81.8 0.0 copy-done.1
  81.8 0.0 copy-done.2
  81.8 15.5 %factor.1 = f32[512,512]{1,0:T(8,128)} custom-call(f32[256,640]{1,0:T(8,128)S(1)} %copy-done, f32[256,640]{1,0:T(8,128)} %collective-permute-done.2.ra, f32[128,640]{1,0:T(8,128)S(1)} %collective-permute-done.3.a2, f32[256,640]{1,0:T(8,128)S(1)} %copy-done.1, f32[256,640]{1,0:T(8,128)} %collective-permute-done.4.rb, ...), custom_call_target="tpu_custom_call" | custom-call | flops 1000000000 | bytes 4327424 | tf_op jit(solution)/shard_map/factor/pallas_call | solution.py:32
Async XLA Ops:
  10.6 26.5 %collective-permute-start = (bf16[512,1024]{1,0:T(8,128)(2,1)}, bf16[512,1024]{1,0:T(8,128)(2,1)}, u32[]{:S(2)}, u32[]{:S(2)}) collective-permute-start(bf16[512,1024]{1,0:T(8,128)(2,1)} %get-tuple-element.13), channel_id=1, source_target_pairs={{0,4},{4,8},{8,12},{12,16},{16,20},{20,24},{24,28},{28,32},{32,36}... | collective-permute-start | bytes 3145736 | tf_op jit(solution)/shard_map/ppermute | solution.py:299
  15.6 21.6 %collective-permute-start.1 = (bf16[512,1024]{1,0:T(8,128)(2,1)}, bf16[512,1024]{1,0:T(8,128)(2,1)}, u32[]{:S(2)}, u32[]{:S(2)}) collective-permute-start(bf16[512,1024]{1,0:T(8,128)(2,1)} %get-tuple-element.14), channel_id=1, source_target_pairs={{4,0},{8,4},{12,8},{16,12},{20,16},{24,20},{28,24},{32,28},{36,32}... | collective-permute-start | bytes 3145736 | tf_op jit(solution)/shard_map/ppermute | solution.py:300
  21.1 53.5 %all-to-all-start = ((bf16[256,4,512]{2,1,0:T(4,128)(2,1)}), bf16[256,4,512]{2,1,0:T(4,128)(2,1)}, u32[]{:S(2)}, u32[]{:S(2)}) async-start(bf16[256,4,512]{2,1,0:T(4,128)(2,1)} %pack_born.1), calls=%async_computation | async-start | bytes 2097152 | tf_op jit(solution)/shard_map/all_to_all | solution.py:311
  45.2 23.7 %collective-permute-start.4 = (f32[256,640]{1,0:T(8,128)}, f32[256,640]{1,0:T(8,128)}, u32[]{:S(2)}, u32[]{:S(2)}) collective-permute-start(f32[256,640]{1,0:T(8,128)} %get-tuple-element.18), channel_id=1, source_target_pairs={{0,3},{1,2},{2,1},{3,0},{4,7},{5,6},{6,5},{7,4},{8,11},{9,10},{10,... | collective-permute-start | bytes 1966088 | tf_op jit(solution)/shard_map/ppermute | solution.py:342
  48.1 23.2 %collective-permute-start.2 = (f32[256,640]{1,0:T(8,128)}, f32[256,640]{1,0:T(8,128)}, u32[]{:S(2)}, u32[]{:S(2)}) collective-permute-start(f32[256,640]{1,0:T(8,128)} %get-tuple-element.16), channel_id=1, source_target_pairs={{0,1},{1,0},{2,3},{3,2},{4,5},{5,4},{6,7},{7,6},{8,9},{9,8},{10,11... | collective-permute-start | bytes 1966088 | tf_op jit(solution)/shard_map/ppermute | solution.py:341
  56.2 25.6 %copy-start = (f32[256,640]{1,0:T(8,128)S(1)}, f32[256,640]{1,0:T(8,128)}, u32[]{:S(2)}) copy-start(f32[256,640]{1,0:T(8,128)} %get-tuple-element.15.ka) | copy-start | bytes 1966084
  56.2 25.6 %copy-start.1 = (f32[256,640]{1,0:T(8,128)S(1)}, f32[256,640]{1,0:T(8,128)}, u32[]{:S(2)}) copy-start(f32[256,640]{1,0:T(8,128)} %get-tuple-element.17.kb) | copy-start | bytes 1966084
  56.2 25.6 %copy-start.2 = (f32[512]{0:T(512)S(1)}, f32[512]{0:T(512)}, u32[]{:S(2)}) copy-start(f32[512]{0:T(512)} %param.13) | copy-start | bytes 6148
  70.0 7.5 %collective-permute-start.5 = (f32[128,640]{1,0:T(8,128)S(1)}, f32[128,640]{1,0:T(8,128)S(1)}, u32[]{:S(2)}, u32[]{:S(2)}) collective-permute-start(f32[128,640]{1,0:T(8,128)S(1)} %slice_add_fusion), channel_id=1, source_target_pairs={{0,1},{1,0},{2,3},{3,2},{4,5},{5,4},{6,7},{7,6},{8,9},{9,8},{10,11... | collective-permute-start | bytes 983048 | tf_op jit(solution)/shard_map/ppermute | solution.py:345
  72.5 9.3 %collective-permute-start.3 = (f32[128,640]{1,0:T(8,128)S(1)}, f32[128,640]{1,0:T(8,128)S(1)}, u32[]{:S(2)}, u32[]{:S(2)}) collective-permute-start(f32[128,640]{1,0:T(8,128)S(1)} %slice_add_fusion.1), channel_id=1, source_target_pairs={{0,3},{1,2},{2,1},{3,0},{4,7},{5,6},{6,5},{7,4},{8,11},{9,10},{10,... | collective-permute-start | bytes 983048 | tf_op jit(solution)/shard_map/ppermute | solution.py:344

commit v4 on v3

--- a/solution.py
+++ b/solution.py
@@ -15,12 +15,11 @@
 VMEM_LIMIT = 32 * 1024 * 1024
 VMEM_WHOLE = 63 * 1024 * 1024 + 512 * 1024
 NT_DIMS = (((1,), (1,)), ((), ()))
-HALF_A = ((0, 0, 0), (3, 384, 512))
-HALF_B = ((1, 128, 0), (2, 256, 384))
-HALF_W = 640
-
-
-def call(kernel, outs, flops, *args, smem=(), anywhere=(), scratch=(), vmem=VMEM_WHOLE, name=None):
+PLAIN = 2 * TILE
+MIXED = 2 * TILE + 8
+
+
+def call(kernel, outs, flops, *args, smem=(), anywhere=(), out_space=pltpu.VMEM, scratch=(), vmem=VMEM_WHOLE, name=None):
     specs = [
         pl.BlockSpec(
             memory_space=pltpu.SMEM if i in smem else pltpu.HBM if i in anywhere else pltpu.VMEM
@@ -33,9 +32,9 @@
         kernel,
         out_shape=outs,
         in_specs=specs,
-        out_specs=pl.BlockSpec(memory_space=pltpu.VMEM)
+        out_specs=pl.BlockSpec(memory_space=out_space)
         if single
-        else [pl.BlockSpec(memory_space=pltpu.VMEM)] * len(outs),
+        else [pl.BlockSpec(memory_space=out_space)] * len(outs),
         scratch_shapes=list(scratch),
         compiler_params=pltpu.CompilerParams(vmem_limit_bytes=vmem),
         cost_estimate=pl.CostEstimate(flops=flops, bytes_accessed=size, transcendentals=0),
@@ -49,30 +48,45 @@
     return lax.dot_general(eye, rows, NT_DIMS, preferred_element_type=F32).astype(BF16)
 
 
-def listed_kernel(rows_ref, list_ref, cols_ref, lower_ref, upper_ref, rows, sems):
-    total, listed = rows_ref.shape[0], lower_ref.shape[1]
-    piece = total // sems.shape[0]
+def listed_kernel(
+    rows_ref, list_ref, cols_out, lower_out, upper_out, rows, cols, lower, upper, in_sems, sems
+):
+    total, listed = rows.shape[0], lower.shape[1]
+    piece = total // in_sems.shape[0]
     copies = []
-    for i in range(sems.shape[0]):
+    for i in range(in_sems.shape[0]):
         part = pl.ds(i * piece, piece)
-        copies.append(pltpu.make_async_copy(rows_ref.at[part, :], rows.at[part, :], sems.at[i]))
+        copies.append(pltpu.make_async_copy(rows_ref.at[part, :], rows.at[part, :], in_sems.at[i]))
         copies[-1].start()
+    sent = []
+
+    def send(source, target, c, width):
+        part = pl.ds(c, width)
+        sent.append(
+            pltpu.make_async_copy(source.at[:, part], target.at[:, part], sems.at[len(sent)])
+        )
+        sent[-1].start()
+
     for i, copy in enumerate(copies):
         copy.wait()
         c = i * piece
-        cols_ref[:, c : c + piece] = transposed(rows[c : c + piece, :])
+        cols[:, c : c + piece] = transposed(rows[c : c + piece, :])
+        send(cols, cols_out, c, piece)
     step, deep = 256, 256
     places = lax.broadcasted_iota(jnp.int32, (deep, step), 0).astype(BF16)
-    for out_ref, first in ((upper_ref, listed), (lower_ref, 0)):
+    for buf, target, first in ((upper, upper_out, listed), (lower, lower_out, 0)):
         for c in range(0, listed, step):
             names = list_ref[:, first + c : first + c + step]
             hot = []
             for h in range(0, total, deep):
                 near = jnp.clip(names - h, -1, deep).astype(F32).astype(BF16)
                 hot.append(jnp.where(places == near, 1.0, 0.0).astype(BF16))
-            out_ref[:, c : c + step] = jnp.dot(
-                cols_ref[...], jnp.concatenate(hot, axis=0), preferred_element_type=F32
+            buf[:, c : c + step] = jnp.dot(
+                cols[...], jnp.concatenate(hot, axis=0), preferred_element_type=F32
             ).astype(BF16)
+            send(buf, target, c, step)
+    for copy in sent:
+        copy.wait()
 
 
 def pack_kernel(owner_ref, rows_ref, out_ref):
@@ -94,46 +108,91 @@
     out_ref[...] = packed.reshape(out_ref.shape)
 
 
-def gram_kernel(kept, rep_ref, cols, lo, up, ids, halo_ids, a_ref, b_ref, buf, sems):
+LEFT = {1: ((0, "a"), (1, "a")), 2: ()}
+RIGHT = {1: ((0, "b"),), 2: ((1, "a"), (2, "b"), (3, "b"))}
+
+
+def place_pair(out_ref, at, first, second, between):
+    sub = lax.broadcasted_iota(jnp.int32, (TILE, TILE), 0)
+    lane = lax.broadcasted_iota(jnp.int32, (TILE, TILE), 1)
+    out_ref[at : at + TILE, :] = jnp.where(lane >= sub, first, second)
+    out_ref[at + TILE : at + 2 * TILE, :] = between
+    diagonal = jnp.sum(jnp.where(lane == sub, second, 0.0), axis=0, keepdims=True)
+    out_ref[at + 2 * TILE : at + MIXED, :] = jnp.broadcast_to(diagonal, (8, TILE))
+
+
+def gram_kernel(kept, parts, rep_ref, cols, lo, up, ids, halo_ids, after, *refs):
+    outs, (buf, sems) = refs[: 2 * len(parts)], refs[2 * len(parts) :]
     me = rep_ref[0]
     pair, mirror, far = me ^ 1, 3 - me, me ^ 2
-    for_a, for_b = ((me, mirror), (me, pair)) if kept else ((pair, far), (mirror, far))
-    pieces, at = [], 0
-    for i, ref in enumerate((cols, lo, up)):
-        width = ref.shape[1]
-        copy = pltpu.make_async_copy(ref, buf.at[:, at : at + width], sems.at[i])
-        copy.start()
-        pieces.append((copy, at, width))
-        at += width
-    own = cols.shape[1]
-    right = left = None
-    for copy, at, width in pieces:
+    blocks = {
+        "a": (me, mirror) if kept else (pair, far),
+        "b": (me, pair) if kept else (mirror, far),
+    }
+    half, own = lo.shape[1], cols.shape[1]
+    pieces = []
+    for ref, begin, widths in (
+        (cols, 0, (512, 512, 1024)),
+        (lo, own, (half,)),
+        (up, own + half, (half,)),
+    ):
+        at = 0
+        for width in widths:
+            copy = pltpu.make_async_copy(
+                ref.at[:, pl.ds(at, width)],
+                buf.at[:, pl.ds(begin + at, width)],
+                sems.at[len(pieces)],
+            )
+            copy.start()
+            pieces.append((copy, begin + at, width))
+            at += width
+    left_rows = [r for part in parts for r in LEFT[part]]
+    right_rows = [r for part in parts for r in RIGHT[part]]
+    left = right = None
+    for copy, c, width in pieces:
         copy.wait()
-        for c in range(at, at + width, 1024):
-            ids_ref, k = (ids, c) if c < own else (halo_ids, c - own)
-            names = ids_ref[:, k : k + 1024]
-            masks_a = [jnp.where(names == b, 1.0, 0.0).astype(BF16) for b in for_a]
-            masks_b = [jnp.where(names == b, 1.0, 0.0).astype(BF16) for b in for_b]
-            part = []
-            for panel, masks in ((0, masks_a), (1, masks_b), (3, masks_a), (2, masks_b)):
-                x = buf[panel * TILE : (panel + 1) * TILE, c : c + 1024]
-                part += [x * m for m in masks]
-            part = jnp.concatenate(part, axis=0)
-            r = lax.dot_general(
-                part, buf[256:, c : c + 1024], NT_DIMS, preferred_element_type=F32
+        span = slice(c, c + width)
+        names = ids[:, span] if c < own else halo_ids[:, c - own : c - own + width]
+        masks = {
+            k: [jnp.where(names == block, 1.0, 0.0).astype(BF16) for block in v]
+            for k, v in blocks.items()
+        }
+        part = {}
+        for panel, k in dict.fromkeys(left_rows + right_rows):
+            x = buf[panel * TILE : (panel + 1) * TILE, span]
+            part[panel, k] = [x * m for m in masks[k]]
+
+        def product(rows, columns):
+            stack = jnp.concatenate([x for r in rows for x in part[r]], axis=0)
+            return lax.dot_general(
+                stack, buf[columns, span], NT_DIMS, preferred_element_type=F32
             )
-            l = lax.dot_general(
-                part[:512], buf[:256, c : c + 1024], NT_DIMS, preferred_element_type=F32
-            )
-            right = r if right is None else right + r
+
+        r = product(right_rows, slice(256, 512))
+        right = r if right is None else right + r
+        if left_rows:
+            l = product(left_rows, slice(0, 256))
             left = l if left is None else left + l
-    two = 2 * TILE
-    a_ref[:, :256] = left[:two]
-    a_ref[:, 256:512] = right[:two]
-    a_ref[:, 512:] = right[2 * two : 3 * two, TILE:]
-    b_ref[:, :TILE] = left[two:, TILE:]
-    b_ref[:, TILE:384] = right[two : 2 * two]
-    b_ref[:, 384:] = right[3 * two :]
+
+    def tiles(value, rows, which, i):
+        at = (2 * rows.index(which) + i) * TILE
+        return value[at : at + TILE, :TILE], value[at : at + TILE, TILE:]
+
+    for part, a_ref, b_ref in zip(parts, outs[::2], outs[1::2]):
+        for i in range(2):
+            if part == 1:
+                first, between = tiles(left, left_rows, (0, "a"), i)
+                _, second = tiles(left, left_rows, (1, "a"), i)
+                place_pair(a_ref, i * MIXED, first, second, between)
+                plain_ref, plain = b_ref, tiles(right, right_rows, (0, "b"), i)
+            else:
+                first, between = tiles(right, right_rows, (2, "b"), i)
+                _, second = tiles(right, right_rows, (3, "b"), i)
+                place_pair(b_ref, i * MIXED, first, second, between)
+                plain_ref, plain = a_ref, tiles(right, right_rows, (1, "a"), i)
+            for j in range(2):
+                at = i * PLAIN + j * TILE
+                plain_ref[at : at + TILE, :] = plain[j]
 
 
 def born_gram_kernel(pool_ref, out_ref):
@@ -248,21 +307,65 @@
             )
 
 
-def factor_kernel(ka, ra, a2, kb, rb, b2, born, mass, out_ref, a_ref):
+def onward_kernel(ka, ra, kb, rb, after, a_ref, b_ref):
+    a_size, b_size = a_ref.shape[0], b_ref.shape[0]
+    a_ref[...] = ka[a_size:, :] + ra[a_size:, :]
+    b_ref[...] = kb[b_size:, :] + rb[b_size:, :]
+
+
+def tile_sum(kept, come, last, at):
+    span = slice(at, at + TILE)
+    return kept[span, :] + come[span, :] + last[span, :]
+
+
+def split_pair(kept, come, last):
     sub = lax.broadcasted_iota(jnp.int32, (TILE, TILE), 0)
     lane = lax.broadcasted_iota(jnp.int32, (TILE, TILE), 1)
-    own = slice(0, TILE)
-    for k0, r0, s0, half in ((ka, ra, a2, HALF_A), (kb, rb, b2, HALF_B)):
-        for panel, first, at in half:
-            cols = slice(at, at + W - first)
-            rows = slice(panel * TILE, (panel + 1) * TILE)
-            g = k0[own, cols] + r0[own, cols] + s0[:, cols] + born[rows, first:]
-            a_ref[rows, first:] = g * (1.0 / W)
+    both = tile_sum(kept, come, last, 0)
+    flip = both.T
+    row = slice(2 * TILE, 2 * TILE + 1)
+    diagonal = kept[row, :] + come[row, :] + last[row, :]
+    second = jnp.where(lane < sub, both, jnp.where(lane == sub, diagonal, flip))
+    return jnp.where(lane >= sub, both, flip), second
+
+
+def system_tile(gram, born, mass, k, c):
+    rows, cols = slice(TILE * k, TILE * (k + 1)), slice(TILE * c, TILE * (c + 1))
+    value = (gram + born[rows, cols]) * (1.0 / W)
+    if k == c:
+        sub = lax.broadcasted_iota(jnp.int32, (TILE, TILE), 0)
+        lane = lax.broadcasted_iota(jnp.int32, (TILE, TILE), 1)
+        value = value + jnp.where(sub == lane, mass[:, rows], 0.0)
+    return value
+
+
+def first_panel_kernel(ka, ra, a2, kb, rb, b2, born, mass, top_ref, next_ref):
+    first, second = split_pair(ka, ra, a2)
+    top = [first, tile_sum(ka, ra, a2, TILE), tile_sum(kb, rb, b2, 0), tile_sum(kb, rb, b2, TILE)]
+    for c in range(4):
+        top_ref[:, TILE * c : TILE * (c + 1)] = system_tile(top[c], born, mass, 0, c)
+    next_ref[...] = system_tile(second, born, mass, 1, 1)
+    factor_panel(top_ref, 4)
+
+
+def other_panels_kernel(ka, ra, a2, kb, rb, b2, born, mass, top_ref, next_ref, out_ref, a_ref):
+    third, fourth = split_pair(kb, rb, b2)
+    grams = {
+        (1, 2): tile_sum(ka, ra, a2, 0),
+        (1, 3): tile_sum(ka, ra, a2, TILE),
+        (2, 2): third,
+        (2, 3): tile_sum(kb, rb, b2, TILE),
+        (3, 3): fourth,
+    }
+    a_ref[:TILE, :] = top_ref[...]
+    a_ref[TILE : 2 * TILE, TILE : 2 * TILE] = next_ref[...]
+    for (k, c), gram in grams.items():
+        a_ref[TILE * k : TILE * (k + 1), TILE * c : TILE * (c + 1)] = system_tile(
+            gram, born, mass, k, c
+        )
     for k in range(4):
         rows = slice(TILE * k, TILE * (k + 1))
         first = TILE * k
-        diag = a_ref[rows, rows]
-        a_ref[rows, rows] = diag + jnp.where(sub == lane, mass[:, rows], 0.0)
         if k > 0:
             a_ref[rows, first:] = a_ref[rows, first:] - jnp.dot(
                 out_ref[rows, :first],
@@ -270,8 +373,8 @@
                 precision=lax.Precision.HIGHEST,
                 preferred_element_type=F32,
             )
-            out_ref[: first, rows] = jnp.zeros((first, TILE), F32)
-        factor_panel(a_ref.at[rows, first:], 4 - k)
+            out_ref[:first, rows] = jnp.zeros((first, TILE), F32)
+            factor_panel(a_ref.at[rows, first:], 4 - k)
         for c in range(k, 4):
             out_ref[TILE * c : TILE * (c + 1), rows] = a_ref[rows, TILE * c : TILE * (c + 1)].T
 
@@ -291,7 +394,15 @@
         elem_rows,
         lists,
         anywhere=(0,),
-        scratch=(pltpu.VMEM((rows, W), BF16), pltpu.SemaphoreType.DMA((4,))),
+        out_space=pltpu.HBM,
+        scratch=(
+            pltpu.VMEM((rows, W), BF16),
+            pltpu.VMEM((W, rows), BF16),
+            pltpu.VMEM((W, listed), BF16),
+            pltpu.VMEM((W, listed), BF16),
+            pltpu.SemaphoreType.DMA((4,)),
+            pltpu.SemaphoreType.DMA((12,)),
+        ),
         name="listed",
     )
     up = [(i, i + 1) for i in range(dom_size - 1)]
@@ -313,51 +424,82 @@
         born_gram_kernel, shape((W, W), F32), 2 * slots * CAP * W * W, arrived, vmem=VMEM_LIMIT, name="born_gram"
     )
 
-    part = shape((2 * TILE, HALF_W), F32)
-
-    def gram(kept):
+    mixed, plain = shape((2 * MIXED, TILE), F32), shape((2 * PLAIN, TILE), F32)
+    halves = {1: (mixed, plain), 2: (plain, mixed)}
+
+    def gram(kept, parts, after, name):
         return call(
-            functools.partial(gram_kernel, kept),
-            (part,) * 2,
-            2 * 6 * 2 * TILE * 256 * (rows + 2 * listed),
+            functools.partial(gram_kernel, kept, parts),
+            tuple(half for part in parts for half in halves[part]),
+            3 * 6 * 2 * TILE * 256 * (rows + 2 * listed) * len(parts),
             rep,
             cols,
             from_lower,
             from_upper,
             elem_block.reshape(1, -1),
             halo_block.reshape(1, -1),
+            after,
             smem=(0,),
-            anywhere=(1, 2, 3),
+            anywhere=(1, 2, 3, 6),
             scratch=(
                 pltpu.VMEM((W, rows + 2 * listed), BF16),
-                pltpu.SemaphoreType.DMA((3,)),
+                pltpu.SemaphoreType.DMA((5,)),
             ),
-            name="kept_gram" if kept else "sent_gram",
+            name=name,
         )
 
-    sa, sb = gram(False)
     pair = [(i, i ^ 1) for i in range(rep_size)]
     mirror = [(i, 3 - i) for i in range(rep_size)]
-    ra = lax.ppermute(sa, "rep", pair)
-    rb = lax.ppermute(sb, "rep", mirror)
-    ka, kb = gram(True)
-    a2 = lax.ppermute(ka[TILE:] + ra[TILE:], "rep", mirror)
-    b2 = lax.ppermute(kb[TILE:] + rb[TILE:], "rep", pair)
+    come, after = {}, packed
+    for part, name in ((1, "sent_gram_1"), (2, "sent_gram_2")):
+        a, b = gram(False, (part,), after, name)
+        after = a
+        come[part] = lax.ppermute(a, "rep", pair), lax.ppermute(b, "rep", mirror)
+    ka1, kb1, ka2, kb2 = gram(True, (1, 2), after, "kept_gram")
+    pieces = {}
+    after = ka2
+    for part, ka, kb in ((1, ka1, kb1), (2, ka2, kb2)):
+        ra, rb = come[part]
+        a_size, b_size = ka.shape[0] // 2, kb.shape[0] // 2
+        a_next, b_next = call(
+            onward_kernel,
+            (shape((a_size, TILE), F32), shape((b_size, TILE), F32)),
+            10**6,
+            ka,
+            ra,
+            kb,
+            rb,
+            after,
+            anywhere=(4,),
+            name=f"onward_{part}",
+        )
+        after = a_next
+        a2 = lax.ppermute(a_next, "rep", mirror)
+        b2 = lax.ppermute(b_next, "rep", pair)
+        pieces[part] = ka, ra, a2, kb, rb, b2
+    mass_row = mass.reshape(1, -1)
+    top, following = call(
+        first_panel_kernel,
+        (shape((TILE, W), F32), shape((TILE, TILE), F32)),
+        10**9,
+        *pieces[1],
+        born_gram,
+        mass_row,
+        vmem=VMEM_LIMIT,
+        name="first_panel",
+    )
     return call(
-        factor_kernel,
+        other_panels_kernel,
         shape((W, W), F32),
-        10**9,
-        ka,
-        ra,
-        a2,
-        kb,
-        rb,
-        b2,
+        2 * 10**9,
+        *pieces[2],
         born_gram,
-        mass.reshape(1, -1),
+        mass_row,
+        top,
+        following,
         scratch=(pltpu.VMEM((W, W), F32),),
         vmem=VMEM_LIMIT,
-        name="factor",
+        name="other_panels",
     )
 
 

time: 98.5 us -> 90.3 us (0.917)
  waiting for transfers between devices: 18 us -> 0.03 us
  Pallas kernels: 47.2 us -> 55.4 us
  starting transfers between devices: 29.8 us -> 32.2 us
  other arithmetic: 2.21 us -> 0 us
    ppermute x4 -> x8, waiting for transfers between devices: 18 us -> 0.02 us  [the longest x4 0.01 us: local(): come[part] = (lax.ppermute(a, 'rep', pair), lax.ppermute(b, 'rep', mirror))]
    pallas_call x6 -> x10, Pallas kernels: 47.2 us -> 55.4 us  [call(): pl.pallas_call(kernel, out_shape=outs, in_specs=specs, out_specs=pl.Block...]
    ppermute x4 -> x8, starting transfers between devices: 6.36 us -> 8.75 us  [the longest x4 4.58 us: local(): come[part] = (lax.ppermute(a, 'rep', pair), lax.ppermute(b, 'rep', mirror))]
    add x2 -> x0, other arithmetic: 2.21 us -> none  [the longest x1 1.11 us: local(): a2 = lax.ppermute(ka[TILE:] + ra[TILE:], 'rep', mirror)]
  transfers between devices with their start and end apart: 7 -> 11, of which waited for: 3 -> 0; matrix products, arithmetic and copies ran while one was open for 2% -> 0% of each run, Pallas kernels for 22% -> 38%
where the time goes in v4:
time: 90.3 us; the launch traced here: 88.6 us
  Pallas kernels  55.4 us (61%)
  starting transfers between devices  32.2 us (36%)
    pallas_call x10, Pallas kernels, call(): pl.pallas_call(kernel, out_shape=outs, in_specs=specs, out_specs=pl.Block...  55.4 us
    all_to_all x1, starting transfers between devices, local(): lax.all_to_all(packed, ('dom', 'rep'), split_axis=0, concat_axis=0, tiled...  16 us
    ppermute x1, starting transfers between devices, local(): from_lower = lax.ppermute(to_upper, 'dom', up)  4.94 us
    ppermute x4, starting transfers between devices, local(): come[part] = (lax.ppermute(a, 'rep', pair), lax.ppermute(b, 'rep', mirror))  4.58 us
    ppermute x2, starting transfers between devices, local(): a2 = lax.ppermute(a_next, 'rep', mirror)  3.2 us
    ppermute x1, starting transfers between devices, local(): from_upper = lax.ppermute(to_lower, 'dom', down)  2.5 us
  transfers between devices with their start and end apart: 11, of which 0 were waited for; matrix products, arithmetic and copies ran while one was open for 0% of the time, Pallas kernels for 38%

profile of v4, /device:TPU:1, one launch (start us, length us, event | category | flops | bytes accessed | tf_op | source)
XLA Modules:
  0.0 88.6 jit_solution(6673227539620893344)
XLA Ops:
  0.0 10.2 %listed.1 = (bf16[512,2048]{1,0:T(8,128)(2,1)}, bf16[512,1024]{1,0:T(8,128)(2,1)}, bf16[512,1024]{1,0:T(8,128)(2,1)}) custom-call(bf16[2048,512]{1,0:T(8,128)(2,1)} %rows_ref.2, s32[1,2048]{1,0:T(1,128)} %bitcast.8), custom_call_target="tpu_custom_call" | custom-call | flops 5368709120 | bytes 2105344 | tf_op jit(solution)/shard_map/listed/pallas_call | solution.py:31
  10.2 4.9 %collective-permute-start = (bf16[512,1024]{1,0:T(8,128)(2,1)}, bf16[512,1024]{1,0:T(8,128)(2,1)}, u32[]{:S(2)}, u32[]{:S(2)}) collective-permute-start(bf16[512,1024]{1,0:T(8,128)(2,1)} %get-tuple-element.23), channel_id=1, source_target_pairs={{0,4},{4,8},{8,12},{12,16},{16,20},{20,24},{24,28},{28,32},{32,36}... | collective-permute-start | bytes 3145736 | tf_op jit(solution)/shard_map/ppermute | solution.py:410
  15.2 2.5 %collective-permute-start.1 = (bf16[512,1024]{1,0:T(8,128)(2,1)}, bf16[512,1024]{1,0:T(8,128)(2,1)}, u32[]{:S(2)}, u32[]{:S(2)}) collective-permute-start(bf16[512,1024]{1,0:T(8,128)(2,1)} %get-tuple-element.24), channel_id=1, source_target_pairs={{4,0},{8,4},{12,8},{16,12},{20,16},{24,20},{28,24},{32,28},{36,32}... | collective-permute-start | bytes 3145736 | tf_op jit(solution)/shard_map/ppermute | solution.py:411
  17.7 3.0 %pack_born.1.after = bf16[256,4,512]{2,1,0:T(4,128)(2,1)} custom-call(s32[1,512]{1,0:T(1,128)} %bitcast.15, bf16[512,512]{1,0:T(8,128)(2,1)} %rows_ref.3), custom_call_target="tpu_custom_call" | custom-call | flops 536870912 | bytes 526336 | tf_op jit(solution)/shard_map/pack_born/pallas_call | solution.py:31
  20.7 16.0 %all-to-all-start = ((bf16[256,4,512]{2,1,0:T(4,128)(2,1)}), bf16[256,4,512]{2,1,0:T(4,128)(2,1)}, u32[]{:S(2)}, u32[]{:S(2)}) async-start(bf16[256,4,512]{2,1,0:T(4,128)(2,1)} %pack_born.1.after), calls=%async_computation | async-start | bytes 2097152 | tf_op jit(solution)/shard_map/all_to_all | solution.py:422
  36.7 0.0 collective-permute-done.lo
  36.7 0.0 collective-permute-done.1.up
  36.8 5.6 %sent_gram_1.1 = (f32[528,128]{1,0:T(8,128)}, f32[512,128]{1,0:T(8,128)}) custom-call(s32[1]{0:T(128)} %bitcast.rep_ref, bf16[512,2048]{1,0:T(8,128)(2,1)} %get-tuple-element.22.cols, bf16[512,1024]{1,0:T(8,128)(2,1)} %collective-permute-done.lo, bf16[512,1024]{1,0:T(8,128)(2,1)} %collective-permute-done.1.up, s32[1,2048]{1,0:T(1,128)} %bitcast.9, ...), custom_call_target="tpu_custom_call" | custom-call | flops 4831838208 | bytes 5259268 | tf_op jit(solution)/shard_map/sent_gram_1/pallas_call | solution.py:31
  42.4 2.7 %collective-permute-start.5 = (f32[512,128]{1,0:T(8,128)}, f32[512,128]{1,0:T(8,128)}, u32[]{:S(2)}, u32[]{:S(2)}) collective-permute-start(f32[512,128]{1,0:T(8,128)} %get-tuple-element.32), channel_id=1, source_target_pairs={{0,3},{1,2},{2,1},{3,0},{4,7},{5,6},{6,5},{7,4},{8,11},{9,10},{10,... | collective-permute-start | bytes 786440 | tf_op jit(solution)/shard_map/ppermute | solution.py:457
  45.1 0.0 collective-permute-start.4
  45.2 6.4 %sent_gram_2.1 = (f32[512,128]{1,0:T(8,128)}, f32[528,128]{1,0:T(8,128)}) custom-call(s32[1]{0:T(128)} %bitcast.rep_ref, bf16[512,2048]{1,0:T(8,128)(2,1)} %get-tuple-element.22.cols, bf16[512,1024]{1,0:T(8,128)(2,1)} %collective-permute-done.lo, bf16[512,1024]{1,0:T(8,128)(2,1)} %collective-permute-done.1.up, s32[1,2048]{1,0:T(1,128)} %bitcast.10, ...), custom_call_target="tpu_custom_call" | custom-call | flops 4831838208 | bytes 4481028 | tf_op jit(solution)/shard_map/sent_gram_2/pallas_call | solution.py:31
  51.6 1.6 %collective-permute-start.2 = (f32[512,128]{1,0:T(8,128)}, f32[512,128]{1,0:T(8,128)}, u32[]{:S(2)}, u32[]{:S(2)}) collective-permute-start(f32[512,128]{1,0:T(8,128)} %get-tuple-element.26.after), channel_id=1, source_target_pairs={{0,1},{1,0},{2,3},{3,2},{4,5},{5,4},{6,7},{7,6},{8,9},{9,8},{10,11... | collective-permute-start | bytes 786440 | tf_op jit(solution)/shard_map/ppermute | solution.py:457
  53.1 0.3 collective-permute-start.3
  53.4 7.9 %kept_gram.1 = (f32[528,128]{1,0:T(8,128)}, f32[512,128]{1,0:T(8,128)}, f32[512,128]{1,0:T(8,128)}, f32[528,128]{1,0:T(8,128)}) custom-call(s32[1]{0:T(128)} %bitcast.rep_ref, bf16[512,2048]{1,0:T(8,128)(2,1)} %get-tuple-element.22.cols, bf16[512,1024]{1,0:T(8,128)(2,1)} %collective-permute-done.lo, bf16[512,1024]{1,0:T(8,128)(2,1)} %collective-permute-done.1.up, ...), custom_call_target="tpu_custom_call" | custom-call | flops 9663676416 | bytes 4472836 | tf_op jit(solution)/shard_map/kept_gram/pallas_call | solution.py:31
  61.4 0.0 collective-permute-done.4.ra
  61.4 0.0 copy-start.6
  61.4 1.9 %onward_1.1 = (f32[264,128]{1,0:T(8,128)}, f32[256,128]{1,0:T(8,128)}) custom-call(f32[528,128]{1,0:T(8,128)} %get-tuple-element.30.ka, f32[528,128]{1,0:T(8,128)} %collective-permute-done.4.ra, f32[512,128]{1,0:T(8,128)} %get-tuple-element.31.kb, f32[512,128]{1,0:T(8,128)} %collective-permute-done.5.rb, f32[512,128]{1,0:T(8,128)} %get-tuple-element.27.after.ka), custom_call_target="tpu_custom_call" | custom-call | flops 1000000 | bytes 1327104 | tf_op jit(solution)/shard_map/onward_1/pallas_call | solution.py:31
  63.3 2.4 %collective-permute-start.8 = (f32[264,128]{1,0:T(8,128)}, f32[264,128]{1,0:T(8,128)S(1)}, u32[]{:S(2)}, u32[]{:S(2)}) collective-permute-start(f32[264,128]{1,0:T(8,128)} %get-tuple-element.33.after), channel_id=1, source_target_pairs={{0,3},{1,2},{2,1},{3,0},{4,7},{5,6},{6,5},{7,4},{8,11},{9,10},{10,... | collective-permute-start | bytes 405512 | tf_op jit(solution)/shard_map/ppermute | solution.py:477
  65.7 0.0 collective-permute-start.9
  65.7 0.0 copy-start.1
  65.7 0.7 copy-done.1
  66.4 1.9 %onward_2.1 = (f32[256,128]{1,0:T(8,128)}, f32[264,128]{1,0:T(8,128)}) custom-call(f32[512,128]{1,0:T(8,128)} %get-tuple-element.27.after.ka, f32[512,128]{1,0:T(8,128)} %collective-permute-done.2.ra, f32[528,128]{1,0:T(8,128)} %get-tuple-element.28.kb, f32[528,128]{1,0:T(8,128)} %copy-done.1, f32[264,128]{1,0:T(8,128)} %get-tuple-element.33.after), custom_call_target="tpu_custom_call" | custom-call | flops 1000000 | bytes 1200128 | tf_op jit(solution)/shard_map/onward_2/pallas_call | solution.py:31
  68.3 0.8 collective-permute-start.6
  69.1 1.0 %collective-permute-start.7 = (f32[264,128]{1,0:T(8,128)}, f32[264,128]{1,0:T(8,128)S(1)}, u32[]{:S(2)}, u32[]{:S(2)}) collective-permute-start(f32[264,128]{1,0:T(8,128)} %get-tuple-element.35), channel_id=1, source_target_pairs={{0,1},{1,0},{2,3},{3,2},{4,5},{5,4},{6,7},{7,6},{8,9},{9,8},{10,11... | collective-permute-start | bytes 405512 | tf_op jit(solution)/shard_map/ppermute | solution.py:478
  70.1 0.0 all-to-all-done.pool_ref
  70.1 2.0 %born_gram.1.born = f32[512,512]{1,0:T(8,128)S(1)} custom-call(bf16[256,4,512]{2,1,0:T(4,128)(2,1)} %all-to-all-done.pool_ref), custom_call_target="tpu_custom_call" | custom-call | flops 536870912 | bytes 1048576 | tf_op jit(solution)/shard_map/born_gram/pallas_call | solution.py:31
  72.1 0.0 copy-start.2
  72.1 0.0 collective-permute-done.9.b2
  72.1 4.5 %first_panel.1 = (f32[128,512]{1,0:T(8,128)S(1)}, f32[128,128]{1,0:T(8,128)S(1)}) custom-call(f32[528,128]{1,0:T(8,128)S(1)} %copy-done.4, f32[528,128]{1,0:T(8,128)} %collective-permute-done.4.ra, f32[264,128]{1,0:T(8,128)S(1)} %collective-permute-done.8.a2, f32[512,128]{1,0:T(8,128)S(1)} %copy-done.5, f32[512,128]{1,0:T(8,128)} %collective-permute-done.5.rb, ...), custom_call_target="tpu_custom_call" | custom-call | flops 1000000000 | bytes 2381824 | tf_op jit(solution)/shard_map/first_panel/pallas_call | solution.py:31
  76.7 0.0 collective-permute-done.6.a2
  76.7 0.0 collective-permute-done.7.b2
  76.7 11.8 %other_panels.1 = f32[512,512]{1,0:T(8,128)} custom-call(f32[512,128]{1,0:T(8,128)S(1)} %copy-done, f32[512,128]{1,0:T(8,128)} %collective-permute-done.2.ra, f32[256,128]{1,0:T(8,128)S(1)} %collective-permute-done.6.a2, f32[528,128]{1,0:T(8,128)S(1)} %copy-done.3, f32[528,128]{1,0:T(8,128)S(1)} %copy-done.2, f32[264,128]{1,0:T(8,128)S(1)} %collective-permute-done.7.b2, ...), custom_call_target="tpu_custom_call" | custom-call | flops 2000000000 | bytes 2709504 | tf_op jit(solution)/shard_map/other_panels/pallas_call | solution.py:31
  (14 shorter events, 0.0 us)
Async XLA Ops:
  10.2 26.5 %collective-permute-start = (bf16[512,1024]{1,0:T(8,128)(2,1)}, bf16[512,1024]{1,0:T(8,128)(2,1)}, u32[]{:S(2)}, u32[]{:S(2)}) collective-permute-start(bf16[512,1024]{1,0:T(8,128)(2,1)} %get-tuple-element.23), channel_id=1, source_target_pairs={{0,4},{4,8},{8,12},{12,16},{16,20},{20,24},{24,28},{28,32},{32,36}... | collective-permute-start | bytes 3145736 | tf_op jit(solution)/shard_map/ppermute | solution.py:410
  15.2 21.6 %collective-permute-start.1 = (bf16[512,1024]{1,0:T(8,128)(2,1)}, bf16[512,1024]{1,0:T(8,128)(2,1)}, u32[]{:S(2)}, u32[]{:S(2)}) collective-permute-start(bf16[512,1024]{1,0:T(8,128)(2,1)} %get-tuple-element.24), channel_id=1, source_target_pairs={{4,0},{8,4},{12,8},{16,12},{20,16},{24,20},{28,24},{32,28},{36,32}... | collective-permute-start | bytes 3145736 | tf_op jit(solution)/shard_map/ppermute | solution.py:411
  20.7 49.4 %all-to-all-start = ((bf16[256,4,512]{2,1,0:T(4,128)(2,1)}), bf16[256,4,512]{2,1,0:T(4,128)(2,1)}, u32[]{:S(2)}, u32[]{:S(2)}) async-start(bf16[256,4,512]{2,1,0:T(4,128)(2,1)} %pack_born.1.after), calls=%async_computation | async-start | bytes 2097152 | tf_op jit(solution)/shard_map/all_to_all | solution.py:422
  42.4 18.9 %collective-permute-start.5 = (f32[512,128]{1,0:T(8,128)}, f32[512,128]{1,0:T(8,128)}, u32[]{:S(2)}, u32[]{:S(2)}) collective-permute-start(f32[512,128]{1,0:T(8,128)} %get-tuple-element.32), channel_id=1, source_target_pairs={{0,3},{1,2},{2,1},{3,0},{4,7},{5,6},{6,5},{7,4},{8,11},{9,10},{10,... | collective-permute-start | bytes 786440 | tf_op jit(solution)/shard_map/ppermute | solution.py:457
  45.1 16.2 %collective-permute-start.4 = (f32[528,128]{1,0:T(8,128)}, f32[528,128]{1,0:T(8,128)}, u32[]{:S(2)}, u32[]{:S(2)}) collective-permute-start(f32[528,128]{1,0:T(8,128)} %get-tuple-element.25.after), channel_id=1, source_target_pairs={{0,1},{1,0},{2,3},{3,2},{4,5},{5,4},{6,7},{7,6},{8,9},{9,8},{10,11... | collective-permute-start | bytes 811016 | tf_op jit(solution)/shard_map/ppermute | solution.py:457
  51.6 14.1 %collective-permute-start.2 = (f32[512,128]{1,0:T(8,128)}, f32[512,128]{1,0:T(8,128)}, u32[]{:S(2)}, u32[]{:S(2)}) collective-permute-start(f32[512,128]{1,0:T(8,128)} %get-tuple-element.26.after), channel_id=1, source_target_pairs={{0,1},{1,0},{2,3},{3,2},{4,5},{5,4},{6,7},{7,6},{8,9},{9,8},{10,11... | collective-permute-start | bytes 786440 | tf_op jit(solution)/shard_map/ppermute | solution.py:457
  53.1 12.6 %collective-permute-start.3 = (f32[528,128]{1,0:T(8,128)}, f32[528,128]{1,0:T(8,128)S(1)}, u32[]{:S(2)}, u32[]{:S(2)}) collective-permute-start(f32[528,128]{1,0:T(8,128)} %get-tuple-element.29), channel_id=1, source_target_pairs={{0,3},{1,2},{2,1},{3,0},{4,7},{5,6},{6,5},{7,4},{8,11},{9,10},{10,... | collective-permute-start | bytes 811016 | tf_op jit(solution)/shard_map/ppermute | solution.py:457
  61.4 10.7 %copy-start.6 = (f32[512]{0:T(512)S(1)}, f32[512]{0:T(512)}, u32[]{:S(2)}) copy-start(f32[512]{0:T(512)} %param.13) | copy-start | bytes 6148
  63.3 8.8 %collective-permute-start.8 = (f32[264,128]{1,0:T(8,128)}, f32[264,128]{1,0:T(8,128)S(1)}, u32[]{:S(2)}, u32[]{:S(2)}) collective-permute-start(f32[264,128]{1,0:T(8,128)} %get-tuple-element.33.after), channel_id=1, source_target_pairs={{0,3},{1,2},{2,1},{3,0},{4,7},{5,6},{6,5},{7,4},{8,11},{9,10},{10,... | collective-permute-start | bytes 405512 | tf_op jit(solution)/shard_map/ppermute | solution.py:477
  65.7 6.4 %collective-permute-start.9 = (f32[256,128]{1,0:T(8,128)}, f32[256,128]{1,0:T(8,128)}, u32[]{:S(2)}, u32[]{:S(2)}) collective-permute-start(f32[256,128]{1,0:T(8,128)} %get-tuple-element.36), channel_id=1, source_target_pairs={{0,1},{1,0},{2,3},{3,2},{4,5},{5,4},{6,7},{7,6},{8,9},{9,8},{10,11... | collective-permute-start | bytes 393224 | tf_op jit(solution)/shard_map/ppermute | solution.py:478
  65.7 0.7 copy-start.1
  68.3 3.8 %copy-start.4 = (f32[528,128]{1,0:T(8,128)S(1)}, f32[528,128]{1,0:T(8,128)}, u32[]{:S(2)}) copy-start(f32[528,128]{1,0:T(8,128)} %get-tuple-element.30.ka) | copy-start | bytes 811012
  68.3 3.8 %copy-start.5 = (f32[512,128]{1,0:T(8,128)S(1)}, f32[512,128]{1,0:T(8,128)}, u32[]{:S(2)}) copy-start(f32[512,128]{1,0:T(8,128)} %get-tuple-element.31.kb) | copy-start | bytes 786436
  68.3 8.4 %collective-permute-start.6 = (f32[256,128]{1,0:T(8,128)}, f32[256,128]{1,0:T(8,128)S(1)}, u32[]{:S(2)}, u32[]{:S(2)}) collective-permute-start(f32[256,128]{1,0:T(8,128)} %get-tuple-element.34), channel_id=1, source_target_pairs={{0,3},{1,2},{2,1},{3,0},{4,7},{5,6},{6,5},{7,4},{8,11},{9,10},{10,... | collective-permute-start | bytes 393224 | tf_op jit(solution)/shard_map/ppermute | solution.py:477
  69.1 7.6 %collective-permute-start.7 = (f32[264,128]{1,0:T(8,128)}, f32[264,128]{1,0:T(8,128)S(1)}, u32[]{:S(2)}, u32[]{:S(2)}) collective-permute-start(f32[264,128]{1,0:T(8,128)} %get-tuple-element.35), channel_id=1, source_target_pairs={{0,1},{1,0},{2,3},{3,2},{4,5},{5,4},{6,7},{7,6},{8,9},{9,8},{10,11... | collective-permute-start | bytes 405512 | tf_op jit(solution)/shard_map/ppermute | solution.py:478
  72.1 4.7 %copy-start = (f32[512,128]{1,0:T(8,128)S(1)}, f32[512,128]{1,0:T(8,128)}, u32[]{:S(2)}) copy-start(f32[512,128]{1,0:T(8,128)} %get-tuple-element.27.after.ka) | copy-start | bytes 786436
  72.1 4.7 %copy-start.2 = (f32[528,128]{1,0:T(8,128)S(1)}, f32[528,128]{1,0:T(8,128)}, u32[]{:S(2)}) copy-start(f32[528,128]{1,0:T(8,128)} %copy-done.1) | copy-start | bytes 811012
  72.1 4.7 %copy-start.3 = (f32[528,128]{1,0:T(8,128)S(1)}, f32[528,128]{1,0:T(8,128)}, u32[]{:S(2)}) copy-start(f32[528,128]{1,0:T(8,128)} %get-tuple-element.28.kb) | copy-start | bytes 811012

commit v5 on v4

--- a/solution.py
+++ b/solution.py
@@ -12,14 +12,14 @@
 TILE = 128
 F32 = jnp.float32
 BF16 = jnp.bfloat16
-VMEM_LIMIT = 32 * 1024 * 1024
+VMEM_LIMIT = 24 * 1024 * 1024
 VMEM_WHOLE = 63 * 1024 * 1024 + 512 * 1024
 NT_DIMS = (((1,), (1,)), ((), ()))
 PLAIN = 2 * TILE
 MIXED = 2 * TILE + 8
 
 
-def call(kernel, outs, flops, *args, smem=(), anywhere=(), out_space=pltpu.VMEM, scratch=(), vmem=VMEM_WHOLE, name=None):
+def call(kernel, outs, flops, *args, smem=(), anywhere=(), out_space=pltpu.VMEM, scratch=(), vmem=VMEM_LIMIT, name=None):
     specs = [
         pl.BlockSpec(
             memory_space=pltpu.SMEM if i in smem else pltpu.HBM if i in anywhere else pltpu.VMEM
@@ -42,12 +42,6 @@
     )(*args)
 
 
-def transposed(rows):
-    order = lax.broadcasted_iota(jnp.int32, (W, W), 0) == lax.broadcasted_iota(jnp.int32, (W, W), 1)
-    eye = jnp.where(order, 1.0, 0.0).astype(BF16)
-    return lax.dot_general(eye, rows, NT_DIMS, preferred_element_type=F32).astype(BF16)
-
-
 def listed_kernel(
     rows_ref, list_ref, cols_out, lower_out, upper_out, rows, cols, lower, upper, in_sems, sems
 ):
@@ -70,7 +64,7 @@
     for i, copy in enumerate(copies):
         copy.wait()
         c = i * piece
-        cols[:, c : c + piece] = transposed(rows[c : c + piece, :])
+        cols[:, c : c + piece] = rows[c : c + piece, :].T
         send(cols, cols_out, c, piece)
     step, deep = 256, 256
     places = lax.broadcasted_iota(jnp.int32, (deep, step), 0).astype(BF16)
@@ -80,7 +74,7 @@
             hot = []
             for h in range(0, total, deep):
                 near = jnp.clip(names - h, -1, deep).astype(F32).astype(BF16)
-                hot.append(jnp.where(places == near, 1.0, 0.0).astype(BF16))
+                hot.append(jnp.maximum(1 - jnp.abs(places - near), 0).astype(BF16))
             buf[:, c : c + step] = jnp.dot(
                 cols[...], jnp.concatenate(hot, axis=0), preferred_element_type=F32
             ).astype(BF16)
@@ -121,8 +115,7 @@
     out_ref[at + 2 * TILE : at + MIXED, :] = jnp.broadcast_to(diagonal, (8, TILE))
 
 
-def gram_kernel(kept, parts, rep_ref, cols, lo, up, ids, halo_ids, after, *refs):
-    outs, (buf, sems) = refs[: 2 * len(parts)], refs[2 * len(parts) :]
+def gram_kernel(kept, parts, rep_ref, cols, lo, up, ids, halo_ids, after, *outs):
     me = rep_ref[0]
     pair, mirror, far = me ^ 1, 3 - me, me ^ 2
     blocks = {
@@ -130,29 +123,14 @@
         "b": (me, pair) if kept else (mirror, far),
     }
     half, own = lo.shape[1], cols.shape[1]
-    pieces = []
-    for ref, begin, widths in (
-        (cols, 0, (512, 512, 1024)),
-        (lo, own, (half,)),
-        (up, own + half, (half,)),
-    ):
-        at = 0
-        for width in widths:
-            copy = pltpu.make_async_copy(
-                ref.at[:, pl.ds(at, width)],
-                buf.at[:, pl.ds(begin + at, width)],
-                sems.at[len(pieces)],
-            )
-            copy.start()
-            pieces.append((copy, begin + at, width))
-            at += width
+    pieces = [(cols, ids, c) for c in range(0, own, 1024)]
+    pieces += [(lo, halo_ids.at[:, :half], 0), (up, halo_ids.at[:, half:], 0)]
     left_rows = [r for part in parts for r in LEFT[part]]
     right_rows = [r for part in parts for r in RIGHT[part]]
     left = right = None
-    for copy, c, width in pieces:
-        copy.wait()
-        span = slice(c, c + width)
-        names = ids[:, span] if c < own else halo_ids[:, c - own : c - own + width]
+    for buf, names_ref, c in pieces:
+        span = slice(c, c + 1024)
+        names = names_ref[:, span]
         masks = {
             k: [jnp.where(names == block, 1.0, 0.0).astype(BF16) for block in v]
             for k, v in blocks.items()
@@ -395,6 +373,7 @@
         lists,
         anywhere=(0,),
         out_space=pltpu.HBM,
+        vmem=VMEM_WHOLE,
         scratch=(
             pltpu.VMEM((rows, W), BF16),
             pltpu.VMEM((W, rows), BF16),
@@ -421,7 +400,7 @@
     )
     arrived = lax.all_to_all(packed, ("dom", "rep"), split_axis=0, concat_axis=0, tiled=True)
     born_gram = call(
-        born_gram_kernel, shape((W, W), F32), 2 * slots * CAP * W * W, arrived, vmem=VMEM_LIMIT, name="born_gram"
+        born_gram_kernel, shape((W, W), F32), 2 * slots * CAP * W * W, arrived, name="born_gram"
     )
 
     mixed, plain = shape((2 * MIXED, TILE), F32), shape((2 * PLAIN, TILE), F32)
@@ -440,11 +419,7 @@
             halo_block.reshape(1, -1),
             after,
             smem=(0,),
-            anywhere=(1, 2, 3, 6),
-            scratch=(
-                pltpu.VMEM((W, rows + 2 * listed), BF16),
-                pltpu.SemaphoreType.DMA((5,)),
-            ),
+            anywhere=(6,),
             name=name,
         )
 
@@ -485,7 +460,6 @@
         *pieces[1],
         born_gram,
         mass_row,
-        vmem=VMEM_LIMIT,
         name="first_panel",
     )
     return call(
@@ -498,7 +472,6 @@
         top,
         following,
         scratch=(pltpu.VMEM((W, W), F32),),
-        vmem=VMEM_LIMIT,
         name="other_panels",
     )
 

time: 90.3 us -> 83.4 us (0.924); the launches traced: 88.6 us -> 82.9 us
  Pallas kernels: 55.4 us -> 35.4 us
  waiting for transfers between devices: 0.03 us -> 12.6 us
  local copies, waits for them, and re-layouts: 0.73 us -> 5.82 us
  starting transfers between devices: 32.2 us -> 28.9 us
    pallas_call x10, Pallas kernels: 55.4 us -> 35.4 us  [call(): pl.pallas_call(kernel, out_shape=outs, in_specs=specs, out_specs=pl.Block...]
    ppermute x4, waiting for transfers between devices: 0.01 us -> 10.2 us  [local(): come[part] = (lax.ppermute(a, 'rep', pair), lax.ppermute(b, 'rep', mirror))]
    unnamed x14 -> x20, local copies, waits for them, and re-layouts: 0.73 us -> 5.82 us
    all_to_all x1, waiting for transfers between devices: 0.01 us -> 2.38 us  [local(): lax.all_to_all(packed, ('dom', 'rep'), split_axis=0, concat_axis=0, tiled...]
    ppermute x2, starting transfers between devices: 3.2 us -> 2.05 us  [local(): a2 = lax.ppermute(a_next, 'rep', mirror)]
    ppermute x2, starting transfers between devices: 0.98 us -> 0.01 us  [local(): b2 = lax.ppermute(b_next, 'rep', pair)]
  transfers between devices with their start and end apart: 11 -> 11, of which waited for: 0 -> 3; matrix products, arithmetic and copies ran while one was open for 0% -> 0% of each run, Pallas kernels for 38% -> 19%
where the time goes in v5:
time: 83.4 us; the launch traced here: 82.9 us
  Pallas kernels  35.4 us (42%)
  starting transfers between devices  28.9 us (35%)
  waiting for transfers between devices  12.6 us (15%)
  local copies, waits for them, and re-layouts  5.82 us (7%)
    pallas_call x10, Pallas kernels, call(): pl.pallas_call(kernel, out_shape=outs, in_specs=specs, out_specs=pl.Block...  35.4 us
    all_to_all x1, starting transfers between devices, local(): lax.all_to_all(packed, ('dom', 'rep'), split_axis=0, concat_axis=0, tiled...  15.6 us
    ppermute x4, waiting for transfers between devices, local(): come[part] = (lax.ppermute(a, 'rep', pair), lax.ppermute(b, 'rep', mirror))  10.2 us
    unnamed x20, local copies, waits for them, and re-layouts  5.82 us
    ppermute x1, starting transfers between devices, local(): from_lower = lax.ppermute(to_upper, 'dom', up)  4.93 us
    ppermute x4, starting transfers between devices, local(): come[part] = (lax.ppermute(a, 'rep', pair), lax.ppermute(b, 'rep', mirror))  4.39 us
    all_to_all x1, waiting for transfers between devices, local(): lax.all_to_all(packed, ('dom', 'rep'), split_axis=0, concat_axis=0, tiled...  2.38 us
    ppermute x2, starting transfers between devices, local(): a2 = lax.ppermute(a_next, 'rep', mirror)  2.05 us
  transfers between devices with their start and end apart: 11, of which 3 were waited for; matrix products, arithmetic and copies ran while one was open for 0% of the time, Pallas kernels for 19%

profile of v5, /device:TPU:1, one launch (start us, length us, event | category | flops | bytes accessed | tf_op | source)
XLA Modules:
  0.0 82.9 jit_solution(17294953750898725164)
XLA Ops:
  0.0 8.0 %listed.1 = (bf16[512,2048]{1,0:T(8,128)(2,1)}, bf16[512,1024]{1,0:T(8,128)(2,1)}, bf16[512,1024]{1,0:T(8,128)(2,1)}) custom-call(bf16[2048,512]{1,0:T(8,128)(2,1)} %rows_ref.2, s32[1,2048]{1,0:T(1,128)} %bitcast.15), custom_call_target="tpu_custom_call" | custom-call | flops 5368709120 | bytes 2105344 | tf_op jit(solution)/shard_map/listed/pallas_call | solution.py:31
  8.0 4.9 %collective-permute-start = (bf16[512,1024]{1,0:T(8,128)(2,1)}, bf16[512,1024]{1,0:T(8,128)(2,1)S(1)}, u32[]{:S(2)}, u32[]{:S(2)}) collective-permute-start(bf16[512,1024]{1,0:T(8,128)(2,1)} %get-tuple-element.23), channel_id=1, source_target_pairs={{0,4},{4,8},{8,12},{12,16},{16,20},{20,24},{24,28},{28,32},{32,36}... | collective-permute-start | bytes 3145736 | tf_op jit(solution)/shard_map/ppermute | solution.py:389
  13.0 1.9 %collective-permute-start.1 = (bf16[512,1024]{1,0:T(8,128)(2,1)}, bf16[512,1024]{1,0:T(8,128)(2,1)S(1)}, u32[]{:S(2)}, u32[]{:S(2)}) collective-permute-start(bf16[512,1024]{1,0:T(8,128)(2,1)} %get-tuple-element.24), channel_id=1, source_target_pairs={{4,0},{8,4},{12,8},{16,12},{20,16},{24,20},{28,24},{32,28},{36,32}... | collective-permute-start | bytes 3145736 | tf_op jit(solution)/shard_map/ppermute | solution.py:390
  14.9 0.0 copy-start.4
  14.9 1.0 %copy-done.4 = bf16[512,512]{1,0:T(8,128)(2,1)S(1)} copy-done((bf16[512,512]{1,0:T(8,128)(2,1)S(1)}, bf16[512,512]{1,0:T(8,128)(2,1)}, u32[]{:S(2)}) %copy-start.4) | copy-done | bytes 524312
  16.0 2.0 %pack_born.1.after = bf16[256,4,512]{2,1,0:T(4,128)(2,1)} custom-call(s32[1,512]{1,0:T(1,128)S(1)} %bitcast.12, bf16[512,512]{1,0:T(8,128)(2,1)S(1)} %copy-done.4), custom_call_target="tpu_custom_call" | custom-call | flops 536870912 | bytes 526336 | tf_op jit(solution)/shard_map/pack_born/pallas_call | solution.py:31
  18.0 15.6 %all-to-all-start = ((bf16[256,4,512]{2,1,0:T(4,128)(2,1)}), bf16[256,4,512]{2,1,0:T(4,128)(2,1)S(1)}, u32[]{:S(2)}, u32[]{:S(2)}) async-start(bf16[256,4,512]{2,1,0:T(4,128)(2,1)} %pack_born.1.after), calls=%async_computation | async-start | bytes 2097152 | tf_op jit(solution)/shard_map/all_to_all | solution.py:401
  33.5 0.0 collective-permute-done.lo
  33.6 0.0 copy-start.2
  33.6 2.3 %copy-done.9 = bf16[512,2048]{1,0:T(8,128)(2,1)S(1)} copy-done((bf16[512,2048]{1,0:T(8,128)(2,1)S(1)}, bf16[512,2048]{1,0:T(8,128)(2,1)}, u32[]{:S(2)}) %copy-start.9) | copy-done | bytes 2097176
  35.9 1.8 %sent_gram_1.1 = (f32[528,128]{1,0:T(8,128)S(1)}, f32[512,128]{1,0:T(8,128)S(1)}) custom-call(s32[1]{0:T(128)} %bitcast.rep_ref, bf16[512,2048]{1,0:T(8,128)(2,1)S(1)} %copy-done.9, bf16[512,1024]{1,0:T(8,128)(2,1)S(1)} %collective-permute-done.lo, bf16[512,1024]{1,0:T(8,128)(2,1)S(1)} %collective-permute-done.1.up, s32[1,2048]{1,0:T(1,128)S(1)} %bitcast.6, ...), custom_call_target="tpu_custom_call" | custom-call | flops 4831838208 | bytes 5259268 | tf_op jit(solution)/shard_map/sent_gram_1/pallas_call | solution.py:31
  37.8 2.7 %collective-permute-start.5 = (f32[512,128]{1,0:T(8,128)S(1)}, f32[512,128]{1,0:T(8,128)S(1)}, u32[]{:S(2)}, u32[]{:S(2)}) collective-permute-start(f32[512,128]{1,0:T(8,128)S(1)} %get-tuple-element.32), channel_id=1, source_target_pairs={{0,3},{1,2},{2,1},{3,0},{4,7},{5,6},{6,5},{7,4},{8,11},{9,10},{10,... | collective-permute-start | bytes 786440 | tf_op jit(solution)/shard_map/ppermute | solution.py:432
  40.5 0.0 collective-permute-start.4
  40.5 1.2 %copy-done.1 = bf16[512,1024]{1,0:T(8,128)(2,1)S(1)} copy-done((bf16[512,1024]{1,0:T(8,128)(2,1)S(1)}, bf16[512,1024]{1,0:T(8,128)(2,1)}, u32[]{:S(2)}) %copy-start.1) | copy-done | bytes 1048600
  41.7 1.2 %copy-done.3 = bf16[512,1024]{1,0:T(8,128)(2,1)S(1)} copy-done((bf16[512,1024]{1,0:T(8,128)(2,1)S(1)}, bf16[512,1024]{1,0:T(8,128)(2,1)}, u32[]{:S(2)}) %copy-start.3) | copy-done | bytes 1048600
  43.0 1.8 %sent_gram_2.1 = (f32[512,128]{1,0:T(8,128)S(1)}, f32[528,128]{1,0:T(8,128)S(1)}) custom-call(s32[1]{0:T(128)} %bitcast.rep_ref, bf16[512,2048]{1,0:T(8,128)(2,1)S(1)} %copy-done.9, bf16[512,1024]{1,0:T(8,128)(2,1)S(1)} %copy-done.1, bf16[512,1024]{1,0:T(8,128)(2,1)S(1)} %copy-done.3, s32[1,2048]{1,0:T(1,128)S(1)} %bitcast.7, s32[1,2048]{1,0:T(1,128)S(1)} %bitcast.10, ...), custom_call_target="tpu_custom_call" | custom-call | flops 4831838208 | bytes 4481028 | tf_op jit(solution)/shard_map/sent_gram_2/pallas_call | solution.py:31
  44.8 1.6 %collective-permute-start.2 = (f32[512,128]{1,0:T(8,128)S(1)}, f32[512,128]{1,0:T(8,128)S(1)}, u32[]{:S(2)}, u32[]{:S(2)}) collective-permute-start(f32[512,128]{1,0:T(8,128)S(1)} %get-tuple-element.26.after), channel_id=1, source_target_pairs={{0,1},{1,0},{2,3},{3,2},{4,5},{5,4},{6,7},{7,6},{8,9},{9,8},{10,11... | collective-permute-start | bytes 786440 | tf_op jit(solution)/shard_map/ppermute | solution.py:432
  46.4 0.1 collective-permute-start.3
  46.5 3.5 %kept_gram.1 = (f32[528,128]{1,0:T(8,128)S(1)}, f32[512,128]{1,0:T(8,128)S(1)}, f32[512,128]{1,0:T(8,128)S(1)}, f32[528,128]{1,0:T(8,128)S(1)}) custom-call(s32[1]{0:T(128)} %bitcast.rep_ref, bf16[512,2048]{1,0:T(8,128)(2,1)S(1)} %copy-done.9, bf16[512,1024]{1,0:T(8,128)(2,1)S(1)} %copy-done.1, bf16[512,1024]{1,0:T(8,128)(2,1)S(1)} %copy-done.3, ...), custom_call_target="tpu_custom_call" | custom-call | flops 9663676416 | bytes 4472836 | tf_op jit(solution)/shard_map/kept_gram/pallas_call | solution.py:31
  49.9 0.0 collective-permute-done.5.rb
  49.9 2.8 %collective-permute-done.4.ra = f32[528,128]{1,0:T(8,128)S(1)} collective-permute-done((f32[528,128]{1,0:T(8,128)S(1)}, f32[528,128]{1,0:T(8,128)S(1)}, u32[]{:S(2)}, u32[]{:S(2)}) %collective-permute-start.4) | collective-permute-done | bytes 270368 | tf_op jit(solution)/shard_map/ppermute | solution.py:432
  52.7 0.7 onward_1.1
  53.4 0.8 collective-permute-start.8
  54.2 7.4 %collective-permute-done.2.ra = f32[512,128]{1,0:T(8,128)S(1)} collective-permute-done((f32[512,128]{1,0:T(8,128)S(1)}, f32[512,128]{1,0:T(8,128)S(1)}, u32[]{:S(2)}, u32[]{:S(2)}) %collective-permute-start.2) | collective-permute-done | bytes 262176 | tf_op jit(solution)/shard_map/ppermute | solution.py:432
  61.6 0.7 onward_2.1
  62.3 1.3 %collective-permute-start.6 = (f32[256,128]{1,0:T(8,128)}, f32[256,128]{1,0:T(8,128)}, u32[]{:S(2)}, u32[]{:S(2)}) collective-permute-start(f32[256,128]{1,0:T(8,128)} %get-tuple-element.34), channel_id=1, source_target_pairs={{0,3},{1,2},{2,1},{3,0},{4,7},{5,6},{6,5},{7,4},{8,11},{9,10},{10,... | collective-permute-start | bytes 393224 | tf_op jit(solution)/shard_map/ppermute | solution.py:452
  63.6 2.4 %all-to-all-done.pool_ref = bf16[256,4,512]{2,1,0:T(4,128)(2,1)S(1)} async-done(((bf16[256,4,512]{2,1,0:T(4,128)(2,1)}), bf16[256,4,512]{2,1,0:T(4,128)(2,1)S(1)}, u32[]{:S(2)}, u32[]{:S(2)}) %all-to-all-start) | async-done | bytes 1048608 | tf_op jit(solution)/shard_map/all_to_all | solution.py:401
  66.0 0.7 born_gram.1.born
  66.7 0.0 collective-permute-done.9.b2
  66.7 0.0 collective-permute-done.8.a2
  66.8 4.3 %first_panel.1 = (f32[128,512]{1,0:T(8,128)S(1)}, f32[128,128]{1,0:T(8,128)S(1)}) custom-call(f32[528,128]{1,0:T(8,128)S(1)} %get-tuple-element.30.ka, f32[528,128]{1,0:T(8,128)S(1)} %collective-permute-done.4.ra, f32[264,128]{1,0:T(8,128)S(1)} %collective-permute-done.8.a2, f32[512,128]{1,0:T(8,128)S(1)} %get-tuple-element.31.kb, ...), custom_call_target="tpu_custom_call" | custom-call | flops 1000000000 | bytes 2381824 | tf_op jit(solution)/shard_map/first_panel/pallas_call | solution.py:31
  71.1 11.8 %other_panels.1 = f32[512,512]{1,0:T(8,128)} custom-call(f32[512,128]{1,0:T(8,128)S(1)} %get-tuple-element.27.after.ka, f32[512,128]{1,0:T(8,128)S(1)} %collective-permute-done.2.ra, f32[256,128]{1,0:T(8,128)} %collective-permute-done.6.a2, f32[528,128]{1,0:T(8,128)S(1)} %get-tuple-element.28.kb, f32[528,128]{1,0:T(8,128)S(1)} %collective-permute-done.3.rb, ...), custom_call_target="tpu_custom_call" | custom-call | flops 2000000000 | bytes 2709504 | tf_op jit(solution)/shard_map/other_panels/pallas_call | solution.py:31
  (20 shorter events, 0.0 us)
Async XLA Ops:
  0.0 14.9 %copy-start.7 = (s32[512,1]{0,1:T(1,128)S(1)}, s32[512,1]{0,1:T(1,128)}, u32[]{:S(2)}) copy-start(s32[512,1]{0,1:T(1,128)} %param.12) | copy-start | bytes 6148
  0.0 33.6 %copy-start.5 = (s32[2048]{0:T(1024)S(1)}, s32[2048]{0:T(1024)}, u32[]{:S(2)}) copy-start(s32[2048]{0:T(1024)} %param.8) | copy-start | bytes 24580
  0.0 33.6 %copy-start.6 = (s32[2048]{0:T(1024)S(1)}, s32[2048]{0:T(1024)}, u32[]{:S(2)}) copy-start(s32[2048]{0:T(1024)} %param.10) | copy-start | bytes 24580
  8.0 25.5 %collective-permute-start = (bf16[512,1024]{1,0:T(8,128)(2,1)}, bf16[512,1024]{1,0:T(8,128)(2,1)S(1)}, u32[]{:S(2)}, u32[]{:S(2)}) collective-permute-start(bf16[512,1024]{1,0:T(8,128)(2,1)} %get-tuple-element.23), channel_id=1, source_target_pairs={{0,4},{4,8},{8,12},{12,16},{16,20},{20,24},{24,28},{28,32},{32,36}... | collective-permute-start | bytes 3145736 | tf_op jit(solution)/shard_map/ppermute | solution.py:389
  13.0 20.6 %collective-permute-start.1 = (bf16[512,1024]{1,0:T(8,128)(2,1)}, bf16[512,1024]{1,0:T(8,128)(2,1)S(1)}, u32[]{:S(2)}, u32[]{:S(2)}) collective-permute-start(bf16[512,1024]{1,0:T(8,128)(2,1)} %get-tuple-element.24), channel_id=1, source_target_pairs={{4,0},{8,4},{12,8},{16,12},{20,16},{24,20},{28,24},{32,28},{36,32}... | collective-permute-start | bytes 3145736 | tf_op jit(solution)/shard_map/ppermute | solution.py:390
  14.9 1.0 %copy-start.4 = (bf16[512,512]{1,0:T(8,128)(2,1)S(1)}, bf16[512,512]{1,0:T(8,128)(2,1)}, u32[]{:S(2)}) copy-start(bf16[512,512]{1,0:T(8,128)(2,1)} %rows_ref.3) | copy-start | bytes 1572868
  18.0 48.0 %all-to-all-start = ((bf16[256,4,512]{2,1,0:T(4,128)(2,1)}), bf16[256,4,512]{2,1,0:T(4,128)(2,1)S(1)}, u32[]{:S(2)}, u32[]{:S(2)}) async-start(bf16[256,4,512]{2,1,0:T(4,128)(2,1)} %pack_born.1.after), calls=%async_computation | async-start | bytes 2097152 | tf_op jit(solution)/shard_map/all_to_all | solution.py:401
  33.5 4.2 %copy-start = (bf16[512,1024]{1,0:T(8,128)(2,1)}, bf16[512,1024]{1,0:T(8,128)(2,1)S(1)}, u32[]{:S(2)}) copy-start(bf16[512,1024]{1,0:T(8,128)(2,1)S(1)} %collective-permute-done.lo) | copy-start | bytes 3145732
  33.6 4.2 %copy-start.2 = (bf16[512,1024]{1,0:T(8,128)(2,1)}, bf16[512,1024]{1,0:T(8,128)(2,1)S(1)}, u32[]{:S(2)}) copy-start(bf16[512,1024]{1,0:T(8,128)(2,1)S(1)} %collective-permute-done.1.up) | copy-start | bytes 3145732
  33.6 2.3 %copy-start.9 = (bf16[512,2048]{1,0:T(8,128)(2,1)S(1)}, bf16[512,2048]{1,0:T(8,128)(2,1)}, u32[]{:S(2)}) copy-start(bf16[512,2048]{1,0:T(8,128)(2,1)} %get-tuple-element.22.cols) | copy-start | bytes 6291460
  37.8 12.2 %collective-permute-start.5 = (f32[512,128]{1,0:T(8,128)S(1)}, f32[512,128]{1,0:T(8,128)S(1)}, u32[]{:S(2)}, u32[]{:S(2)}) collective-permute-start(f32[512,128]{1,0:T(8,128)S(1)} %get-tuple-element.32), channel_id=1, source_target_pairs={{0,3},{1,2},{2,1},{3,0},{4,7},{5,6},{6,5},{7,4},{8,11},{9,10},{10,... | collective-permute-start | bytes 786440 | tf_op jit(solution)/shard_map/ppermute | solution.py:432
  40.5 12.2 %collective-permute-start.4 = (f32[528,128]{1,0:T(8,128)S(1)}, f32[528,128]{1,0:T(8,128)S(1)}, u32[]{:S(2)}, u32[]{:S(2)}) collective-permute-start(f32[528,128]{1,0:T(8,128)S(1)} %get-tuple-element.25.after), channel_id=1, source_target_pairs={{0,1},{1,0},{2,3},{3,2},{4,5},{5,4},{6,7},{7,6},{8,9},{9,8},{10,11... | collective-permute-start | bytes 811016 | tf_op jit(solution)/shard_map/ppermute | solution.py:432
  40.5 1.2 %copy-start.1 = (bf16[512,1024]{1,0:T(8,128)(2,1)S(1)}, bf16[512,1024]{1,0:T(8,128)(2,1)}, u32[]{:S(2)}) copy-start(bf16[512,1024]{1,0:T(8,128)(2,1)} %copy-done) | copy-start | bytes 3145732
  41.7 1.2 %copy-start.3 = (bf16[512,1024]{1,0:T(8,128)(2,1)S(1)}, bf16[512,1024]{1,0:T(8,128)(2,1)}, u32[]{:S(2)}) copy-start(bf16[512,1024]{1,0:T(8,128)(2,1)} %copy-done.2) | copy-start | bytes 3145732
  44.8 16.8 %collective-permute-start.2 = (f32[512,128]{1,0:T(8,128)S(1)}, f32[512,128]{1,0:T(8,128)S(1)}, u32[]{:S(2)}, u32[]{:S(2)}) collective-permute-start(f32[512,128]{1,0:T(8,128)S(1)} %get-tuple-element.26.after), channel_id=1, source_target_pairs={{0,1},{1,0},{2,3},{3,2},{4,5},{5,4},{6,7},{7,6},{8,9},{9,8},{10,11... | collective-permute-start | bytes 786440 | tf_op jit(solution)/shard_map/ppermute | solution.py:432
  46.4 15.2 %collective-permute-start.3 = (f32[528,128]{1,0:T(8,128)S(1)}, f32[528,128]{1,0:T(8,128)S(1)}, u32[]{:S(2)}, u32[]{:S(2)}) collective-permute-start(f32[528,128]{1,0:T(8,128)S(1)} %get-tuple-element.29), channel_id=1, source_target_pairs={{0,3},{1,2},{2,1},{3,0},{4,7},{5,6},{6,5},{7,4},{8,11},{9,10},{10,... | collective-permute-start | bytes 811016 | tf_op jit(solution)/shard_map/ppermute | solution.py:432
  52.7 14.0 %copy-start.8 = (f32[512]{0:T(512)S(1)}, f32[512]{0:T(512)}, u32[]{:S(2)}) copy-start(f32[512]{0:T(512)} %param.13) | copy-start | bytes 6148
  53.4 13.3 %collective-permute-start.8 = (f32[264,128]{1,0:T(8,128)S(1)}, f32[264,128]{1,0:T(8,128)S(1)}, u32[]{:S(2)}, u32[]{:S(2)}) collective-permute-start(f32[264,128]{1,0:T(8,128)S(1)} %get-tuple-element.33.after), channel_id=1, source_target_pairs={{0,3},{1,2},{2,1},{3,0},{4,7},{5,6},{6,5},{7,4},{8,11},{9,10},{10,... | collective-permute-start | bytes 405512 | tf_op jit(solution)/shard_map/ppermute | solution.py:452
  54.2 12.6 %collective-permute-start.9 = (f32[256,128]{1,0:T(8,128)}, f32[256,128]{1,0:T(8,128)}, u32[]{:S(2)}, u32[]{:S(2)}) collective-permute-start(f32[256,128]{1,0:T(8,128)} %get-tuple-element.36), channel_id=1, source_target_pairs={{0,1},{1,0},{2,3},{3,2},{4,5},{5,4},{6,7},{7,6},{8,9},{9,8},{10,11... | collective-permute-start | bytes 393224 | tf_op jit(solution)/shard_map/ppermute | solution.py:453
  62.3 8.8 %collective-permute-start.6 = (f32[256,128]{1,0:T(8,128)}, f32[256,128]{1,0:T(8,128)}, u32[]{:S(2)}, u32[]{:S(2)}) collective-permute-start(f32[256,128]{1,0:T(8,128)} %get-tuple-element.34), channel_id=1, source_target_pairs={{0,3},{1,2},{2,1},{3,0},{4,7},{5,6},{6,5},{7,4},{8,11},{9,10},{10,... | collective-permute-start | bytes 393224 | tf_op jit(solution)/shard_map/ppermute | solution.py:452
  63.6 7.5 %collective-permute-start.7 = (f32[264,128]{1,0:T(8,128)}, f32[264,128]{1,0:T(8,128)}, u32[]{:S(2)}, u32[]{:S(2)}) collective-permute-start(f32[264,128]{1,0:T(8,128)} %get-tuple-element.35), channel_id=1, source_target_pairs={{0,1},{1,0},{2,3},{3,2},{4,5},{5,4},{6,7},{7,6},{8,9},{9,8},{10,11... | collective-permute-start | bytes 405512 | tf_op jit(solution)/shard_map/ppermute | solution.py:453

commit v6 on v5

--- a/solution.py
+++ b/solution.py
@@ -13,6 +13,7 @@
 F32 = jnp.float32
 BF16 = jnp.bfloat16
 VMEM_LIMIT = 24 * 1024 * 1024
+VMEM_MOST = 64 * 1024 * 1024 - 2304 * 1024
 VMEM_WHOLE = 63 * 1024 * 1024 + 512 * 1024
 NT_DIMS = (((1,), (1,)), ((), ()))
 PLAIN = 2 * TILE
@@ -83,7 +84,9 @@
         copy.wait()
 
 
-def pack_kernel(owner_ref, rows_ref, out_ref):
+def pack_kernel(owner_ref, rows_ref, out_ref, rows, sem):
+    copy = pltpu.make_async_copy(rows_ref, rows, sem)
+    copy.start()
     owner = owner_ref[...]
     count = owner.shape[1]
     blocks = out_ref.shape[0]
@@ -98,7 +101,8 @@
     place = owner * CAP + rank.astype(jnp.int32)
     hot = lax.broadcasted_iota(jnp.int32, (blocks * CAP, count), 0) == place
     hot = jnp.where(hot, 1.0, 0.0).astype(BF16)
-    packed = jnp.dot(hot, rows_ref[...], preferred_element_type=F32).astype(BF16)
+    copy.wait()
+    packed = jnp.dot(hot, rows[...], preferred_element_type=F32).astype(BF16)
     out_ref[...] = packed.reshape(out_ref.shape)
 
 
@@ -396,6 +400,9 @@
         2 * slots * CAP * W * W,
         born_owner.reshape(1, -1),
         born_rows,
+        anywhere=(1,),
+        scratch=(pltpu.VMEM(born_rows.shape, BF16), pltpu.SemaphoreType.DMA),
+        vmem=VMEM_MOST,
         name="pack_born",
     )
     arrived = lax.all_to_all(packed, ("dom", "rep"), split_axis=0, concat_axis=0, tiled=True)

time: 83.4 us -> 83.9 us (level)
  Pallas kernels: 35.4 us -> 40.5 us
  waiting for transfers between devices: 12.6 us -> 9.39 us
  local copies, waits for them, and re-layouts: 5.82 us -> 3.18 us
  starting transfers between devices: 28.9 us -> 30.1 us
    pallas_call x10, Pallas kernels: 35.4 us -> 40.5 us  [call(): pl.pallas_call(kernel, out_shape=outs, in_specs=specs, out_specs=pl.Block...]
    unnamed x20 -> x14, local copies, waits for them, and re-layouts: 5.82 us -> 3.18 us
    ppermute x4, waiting for transfers between devices: 10.2 us -> 7.83 us  [local(): come[part] = (lax.ppermute(a, 'rep', pair), lax.ppermute(b, 'rep', mirror))]
    ppermute x2, starting transfers between devices: 2.05 us -> 3.22 us  [local(): a2 = lax.ppermute(a_next, 'rep', mirror)]
  transfers between devices with their start and end apart: 11 -> 11, of which waited for: 3 -> 3; matrix products, arithmetic and copies ran while one was open for 0% -> 0% of each run, Pallas kernels for 19% -> 25%
where the time goes in v6:
time: 83.9 us; the launch traced here: 83.3 us
  Pallas kernels  40.5 us (48%)
  starting transfers between devices  30.1 us (36%)
  waiting for transfers between devices  9.39 us (11%)
  local copies, waits for them, and re-layouts  3.18 us (4%)
    pallas_call x10, Pallas kernels, call(): pl.pallas_call(kernel, out_shape=outs, in_specs=specs, out_specs=pl.Block...  40.5 us
    all_to_all x1, starting transfers between devices, local(): lax.all_to_all(packed, ('dom', 'rep'), split_axis=0, concat_axis=0, tiled...  15.6 us
    ppermute x4, waiting for transfers between devices, local(): come[part] = (lax.ppermute(a, 'rep', pair), lax.ppermute(b, 'rep', mirror))  7.83 us
    ppermute x1, starting transfers between devices, local(): from_lower = lax.ppermute(to_upper, 'dom', up)  4.94 us
    ppermute x4, starting transfers between devices, local(): come[part] = (lax.ppermute(a, 'rep', pair), lax.ppermute(b, 'rep', mirror))  4.39 us
    ppermute x2, starting transfers between devices, local(): a2 = lax.ppermute(a_next, 'rep', mirror)  3.22 us
    unnamed x14, local copies, waits for them, and re-layouts  3.18 us
    ppermute x1, starting transfers between devices, local(): from_upper = lax.ppermute(to_lower, 'dom', down)  1.92 us
  transfers between devices with their start and end apart: 11, of which 3 were waited for; matrix products, arithmetic and copies ran while one was open for 0% of the time, Pallas kernels for 25%

profile of v6, /device:TPU:1, one launch (start us, length us, event | category | flops | bytes accessed | tf_op | source)
XLA Modules:
  0.0 83.3 jit_solution(10550118124536928086)
XLA Ops:
  0.0 8.0 %listed.1 = (bf16[512,2048]{1,0:T(8,128)(2,1)}, bf16[512,1024]{1,0:T(8,128)(2,1)}, bf16[512,1024]{1,0:T(8,128)(2,1)}) custom-call(bf16[2048,512]{1,0:T(8,128)(2,1)} %rows_ref.2, s32[1,2048]{1,0:T(1,128)} %bitcast.14), custom_call_target="tpu_custom_call" | custom-call | flops 5368709120 | bytes 2105344 | tf_op jit(solution)/shard_map/listed/pallas_call | solution.py:32
  8.0 0.0 copy-start.3
  8.0 0.0 copy-start.4
  8.0 4.9 %collective-permute-start = (bf16[512,1024]{1,0:T(8,128)(2,1)}, bf16[512,1024]{1,0:T(8,128)(2,1)S(1)}, u32[]{:S(2)}, u32[]{:S(2)}) collective-permute-start(bf16[512,1024]{1,0:T(8,128)(2,1)} %get-tuple-element.23), channel_id=1, source_target_pairs={{0,4},{4,8},{8,12},{12,16},{16,20},{20,24},{24,28},{28,32},{32,36}... | collective-permute-start | bytes 3145736 | tf_op jit(solution)/shard_map/ppermute | solution.py:393
  13.0 1.9 %collective-permute-start.1 = (bf16[512,1024]{1,0:T(8,128)(2,1)}, bf16[512,1024]{1,0:T(8,128)(2,1)}, u32[]{:S(2)}, u32[]{:S(2)}) collective-permute-start(bf16[512,1024]{1,0:T(8,128)(2,1)} %get-tuple-element.24), channel_id=1, source_target_pairs={{4,0},{8,4},{12,8},{16,12},{20,16},{24,20},{28,24},{32,28},{36,32}... | collective-permute-start | bytes 3145736 | tf_op jit(solution)/shard_map/ppermute | solution.py:394
  14.9 3.4 %pack_born.1.after = bf16[256,4,512]{2,1,0:T(4,128)(2,1)} custom-call(s32[1,512]{1,0:T(1,128)} %bitcast.15, bf16[512,512]{1,0:T(8,128)(2,1)} %rows_ref.3), custom_call_target="tpu_custom_call" | custom-call | flops 536870912 | bytes 526336 | tf_op jit(solution)/shard_map/pack_born/pallas_call | solution.py:32
  18.3 15.6 %all-to-all-start = ((bf16[256,4,512]{2,1,0:T(4,128)(2,1)}), bf16[256,4,512]{2,1,0:T(4,128)(2,1)S(1)}, u32[]{:S(2)}, u32[]{:S(2)}) async-start(bf16[256,4,512]{2,1,0:T(4,128)(2,1)} %pack_born.1.after), calls=%async_computation | async-start | bytes 2097152 | tf_op jit(solution)/shard_map/all_to_all | solution.py:408
  34.0 0.0 collective-permute-done.1.up
  34.0 1.9 %copy-done.6 = bf16[512,2048]{1,0:T(8,128)(2,1)S(1)} copy-done((bf16[512,2048]{1,0:T(8,128)(2,1)S(1)}, bf16[512,2048]{1,0:T(8,128)(2,1)}, u32[]{:S(2)}) %copy-start.6) | copy-done | bytes 2097176
  35.9 3.1 %sent_gram_1.1 = (f32[528,128]{1,0:T(8,128)S(1)}, f32[512,128]{1,0:T(8,128)S(1)}) custom-call(s32[1]{0:T(128)} %bitcast.rep_ref, bf16[512,2048]{1,0:T(8,128)(2,1)S(1)} %copy-done.6, bf16[512,1024]{1,0:T(8,128)(2,1)S(1)} %collective-permute-done.lo, bf16[512,1024]{1,0:T(8,128)(2,1)} %collective-permute-done.1.up, s32[1,2048]{1,0:T(1,128)S(1)} %bitcast.6, ...), custom_call_target="tpu_custom_call" | custom-call | flops 4831838208 | bytes 5259268 | tf_op jit(solution)/shard_map/sent_gram_1/pallas_call | solution.py:32
  39.0 2.7 %collective-permute-start.5 = (f32[512,128]{1,0:T(8,128)S(1)}, f32[512,128]{1,0:T(8,128)S(1)}, u32[]{:S(2)}, u32[]{:S(2)}) collective-permute-start(f32[512,128]{1,0:T(8,128)S(1)} %get-tuple-element.32), channel_id=1, source_target_pairs={{0,3},{1,2},{2,1},{3,0},{4,7},{5,6},{6,5},{7,4},{8,11},{9,10},{10,... | collective-permute-start | bytes 786440 | tf_op jit(solution)/shard_map/ppermute | solution.py:439
  41.7 0.0 collective-permute-start.4
  41.7 1.2 %copy-done.2 = bf16[512,1024]{1,0:T(8,128)(2,1)S(1)} copy-done((bf16[512,1024]{1,0:T(8,128)(2,1)S(1)}, bf16[512,1024]{1,0:T(8,128)(2,1)}, u32[]{:S(2)}) %copy-start.2) | copy-done | bytes 1048600
  43.0 3.0 %sent_gram_2.1 = (f32[512,128]{1,0:T(8,128)S(1)}, f32[528,128]{1,0:T(8,128)S(1)}) custom-call(s32[1]{0:T(128)} %bitcast.rep_ref, bf16[512,2048]{1,0:T(8,128)(2,1)S(1)} %copy-done.6, bf16[512,1024]{1,0:T(8,128)(2,1)S(1)} %copy-done.2, bf16[512,1024]{1,0:T(8,128)(2,1)} %collective-permute-done.1.up, s32[1,2048]{1,0:T(1,128)S(1)} %bitcast.7, ...), custom_call_target="tpu_custom_call" | custom-call | flops 4831838208 | bytes 4481028 | tf_op jit(solution)/shard_map/sent_gram_2/pallas_call | solution.py:32
  46.0 1.6 %collective-permute-start.2 = (f32[512,128]{1,0:T(8,128)S(1)}, f32[512,128]{1,0:T(8,128)S(1)}, u32[]{:S(2)}, u32[]{:S(2)}) collective-permute-start(f32[512,128]{1,0:T(8,128)S(1)} %get-tuple-element.26.after), channel_id=1, source_target_pairs={{0,1},{1,0},{2,3},{3,2},{4,5},{5,4},{6,7},{7,6},{8,9},{9,8},{10,11... | collective-permute-start | bytes 786440 | tf_op jit(solution)/shard_map/ppermute | solution.py:439
  47.6 0.1 collective-permute-start.3
  47.7 4.7 %kept_gram.1 = (f32[528,128]{1,0:T(8,128)S(1)}, f32[512,128]{1,0:T(8,128)S(1)}, f32[512,128]{1,0:T(8,128)S(1)}, f32[528,128]{1,0:T(8,128)S(1)}) custom-call(s32[1]{0:T(128)} %bitcast.rep_ref, bf16[512,2048]{1,0:T(8,128)(2,1)S(1)} %copy-done.6, bf16[512,1024]{1,0:T(8,128)(2,1)S(1)} %copy-done.2, bf16[512,1024]{1,0:T(8,128)(2,1)} %collective-permute-done.1.up, ...), custom_call_target="tpu_custom_call" | custom-call | flops 9663676416 | bytes 4472836 | tf_op jit(solution)/shard_map/kept_gram/pallas_call | solution.py:32
  52.4 1.2 %collective-permute-done.4.ra = f32[528,128]{1,0:T(8,128)S(1)} collective-permute-done((f32[528,128]{1,0:T(8,128)S(1)}, f32[528,128]{1,0:T(8,128)S(1)}, u32[]{:S(2)}, u32[]{:S(2)}) %collective-permute-start.4) | collective-permute-done | bytes 270368 | tf_op jit(solution)/shard_map/ppermute | solution.py:439
  53.5 0.7 onward_1.1
  54.2 1.4 %collective-permute-start.8 = (f32[264,128]{1,0:T(8,128)S(1)}, f32[264,128]{1,0:T(8,128)S(1)}, u32[]{:S(2)}, u32[]{:S(2)}) collective-permute-start(f32[264,128]{1,0:T(8,128)S(1)} %get-tuple-element.33.after), channel_id=1, source_target_pairs={{0,3},{1,2},{2,1},{3,0},{4,7},{5,6},{6,5},{7,4},{8,11},{9,10},{10,... | collective-permute-start | bytes 405512 | tf_op jit(solution)/shard_map/ppermute | solution.py:459
  55.6 0.0 collective-permute-start.9
  55.6 6.6 %collective-permute-done.2.ra = f32[512,128]{1,0:T(8,128)S(1)} collective-permute-done((f32[512,128]{1,0:T(8,128)S(1)}, f32[512,128]{1,0:T(8,128)S(1)}, u32[]{:S(2)}, u32[]{:S(2)}) %collective-permute-start.2) | collective-permute-done | bytes 262176 | tf_op jit(solution)/shard_map/ppermute | solution.py:439
  62.3 0.7 onward_2.1
  63.0 1.8 %collective-permute-start.6 = (f32[256,128]{1,0:T(8,128)}, f32[256,128]{1,0:T(8,128)}, u32[]{:S(2)}, u32[]{:S(2)}) collective-permute-start(f32[256,128]{1,0:T(8,128)} %get-tuple-element.34), channel_id=1, source_target_pairs={{0,3},{1,2},{2,1},{3,0},{4,7},{5,6},{6,5},{7,4},{8,11},{9,10},{10,... | collective-permute-start | bytes 393224 | tf_op jit(solution)/shard_map/ppermute | solution.py:459
  64.8 0.0 collective-permute-start.7
  64.8 1.5 %all-to-all-done.pool_ref = bf16[256,4,512]{2,1,0:T(4,128)(2,1)S(1)} async-done(((bf16[256,4,512]{2,1,0:T(4,128)(2,1)}), bf16[256,4,512]{2,1,0:T(4,128)(2,1)S(1)}, u32[]{:S(2)}, u32[]{:S(2)}) %all-to-all-start) | async-done | bytes 1048608 | tf_op jit(solution)/shard_map/all_to_all | solution.py:408
  66.4 0.7 born_gram.1.born
  67.1 0.0 collective-permute-done.8.a2
  67.2 4.3 %first_panel.1 = (f32[128,512]{1,0:T(8,128)S(1)}, f32[128,128]{1,0:T(8,128)S(1)}) custom-call(f32[528,128]{1,0:T(8,128)S(1)} %get-tuple-element.30.ka, f32[528,128]{1,0:T(8,128)S(1)} %collective-permute-done.4.ra, f32[264,128]{1,0:T(8,128)S(1)} %collective-permute-done.8.a2, f32[512,128]{1,0:T(8,128)S(1)} %get-tuple-element.31.kb, ...), custom_call_target="tpu_custom_call" | custom-call | flops 1000000000 | bytes 2381824 | tf_op jit(solution)/shard_map/first_panel/pallas_call | solution.py:32
  71.5 0.0 collective-permute-done.6.a2
  71.5 0.0 collective-permute-done.7.b2
  71.5 11.8 %other_panels.1 = f32[512,512]{1,0:T(8,128)} custom-call(f32[512,128]{1,0:T(8,128)S(1)} %get-tuple-element.27.after.ka, f32[512,128]{1,0:T(8,128)S(1)} %collective-permute-done.2.ra, f32[256,128]{1,0:T(8,128)} %collective-permute-done.6.a2, f32[528,128]{1,0:T(8,128)S(1)} %get-tuple-element.28.kb, f32[528,128]{1,0:T(8,128)S(1)} %collective-permute-done.3.rb, ...), custom_call_target="tpu_custom_call" | custom-call | flops 2000000000 | bytes 2709504 | tf_op jit(solution)/shard_map/other_panels/pallas_call | solution.py:32
  (14 shorter events, 0.0 us)
Async XLA Ops:
  8.0 26.0 %copy-start.3 = (s32[2048]{0:T(1024)S(1)}, s32[2048]{0:T(1024)}, u32[]{:S(2)}) copy-start(s32[2048]{0:T(1024)} %param.8) | copy-start | bytes 24580
  8.0 26.0 %copy-start.4 = (s32[2048]{0:T(1024)S(1)}, s32[2048]{0:T(1024)}, u32[]{:S(2)}) copy-start(s32[2048]{0:T(1024)} %param.10) | copy-start | bytes 24580
  8.0 25.9 %collective-permute-start = (bf16[512,1024]{1,0:T(8,128)(2,1)}, bf16[512,1024]{1,0:T(8,128)(2,1)S(1)}, u32[]{:S(2)}, u32[]{:S(2)}) collective-permute-start(bf16[512,1024]{1,0:T(8,128)(2,1)} %get-tuple-element.23), channel_id=1, source_target_pairs={{0,4},{4,8},{8,12},{12,16},{16,20},{20,24},{24,28},{28,32},{32,36}... | collective-permute-start | bytes 3145736 | tf_op jit(solution)/shard_map/ppermute | solution.py:393
  13.0 21.0 %collective-permute-start.1 = (bf16[512,1024]{1,0:T(8,128)(2,1)}, bf16[512,1024]{1,0:T(8,128)(2,1)}, u32[]{:S(2)}, u32[]{:S(2)}) collective-permute-start(bf16[512,1024]{1,0:T(8,128)(2,1)} %get-tuple-element.24), channel_id=1, source_target_pairs={{4,0},{8,4},{12,8},{16,12},{20,16},{24,20},{28,24},{32,28},{36,32}... | collective-permute-start | bytes 3145736 | tf_op jit(solution)/shard_map/ppermute | solution.py:394
  18.3 15.6 %copy-start = (bf16[256,4,512]{2,1,0:T(4,128)(2,1)S(1)}, bf16[256,4,512]{2,1,0:T(4,128)(2,1)}, u32[]{:S(2)}) copy-start(bf16[256,4,512]{2,1,0:T(4,128)(2,1)} %pack_born.1.after) | copy-start | bytes 3145732
  18.3 48.0 %all-to-all-start = ((bf16[256,4,512]{2,1,0:T(4,128)(2,1)}), bf16[256,4,512]{2,1,0:T(4,128)(2,1)S(1)}, u32[]{:S(2)}, u32[]{:S(2)}) async-start(bf16[256,4,512]{2,1,0:T(4,128)(2,1)} %pack_born.1.after), calls=%async_computation | async-start | bytes 2097152 | tf_op jit(solution)/shard_map/all_to_all | solution.py:408
  33.9 5.0 %copy-start.1 = (bf16[512,1024]{1,0:T(8,128)(2,1)}, bf16[512,1024]{1,0:T(8,128)(2,1)S(1)}, u32[]{:S(2)}) copy-start(bf16[512,1024]{1,0:T(8,128)(2,1)S(1)} %collective-permute-done.lo) | copy-start | bytes 3145732
  34.0 1.9 %copy-start.6 = (bf16[512,2048]{1,0:T(8,128)(2,1)S(1)}, bf16[512,2048]{1,0:T(8,128)(2,1)}, u32[]{:S(2)}) copy-start(bf16[512,2048]{1,0:T(8,128)(2,1)} %get-tuple-element.22.cols) | copy-start | bytes 6291460
  39.0 13.4 %collective-permute-start.5 = (f32[512,128]{1,0:T(8,128)S(1)}, f32[512,128]{1,0:T(8,128)S(1)}, u32[]{:S(2)}, u32[]{:S(2)}) collective-permute-start(f32[512,128]{1,0:T(8,128)S(1)} %get-tuple-element.32), channel_id=1, source_target_pairs={{0,3},{1,2},{2,1},{3,0},{4,7},{5,6},{6,5},{7,4},{8,11},{9,10},{10,... | collective-permute-start | bytes 786440 | tf_op jit(solution)/shard_map/ppermute | solution.py:439
  41.7 11.8 %collective-permute-start.4 = (f32[528,128]{1,0:T(8,128)S(1)}, f32[528,128]{1,0:T(8,128)S(1)}, u32[]{:S(2)}, u32[]{:S(2)}) collective-permute-start(f32[528,128]{1,0:T(8,128)S(1)} %get-tuple-element.25.after), channel_id=1, source_target_pairs={{0,1},{1,0},{2,3},{3,2},{4,5},{5,4},{6,7},{7,6},{8,9},{9,8},{10,11... | collective-permute-start | bytes 811016 | tf_op jit(solution)/shard_map/ppermute | solution.py:439
  41.7 1.2 %copy-start.2 = (bf16[512,1024]{1,0:T(8,128)(2,1)S(1)}, bf16[512,1024]{1,0:T(8,128)(2,1)}, u32[]{:S(2)}) copy-start(bf16[512,1024]{1,0:T(8,128)(2,1)} %copy-done.1) | copy-start | bytes 3145732
  46.0 16.3 %collective-permute-start.2 = (f32[512,128]{1,0:T(8,128)S(1)}, f32[512,128]{1,0:T(8,128)S(1)}, u32[]{:S(2)}, u32[]{:S(2)}) collective-permute-start(f32[512,128]{1,0:T(8,128)S(1)} %get-tuple-element.26.after), channel_id=1, source_target_pairs={{0,1},{1,0},{2,3},{3,2},{4,5},{5,4},{6,7},{7,6},{8,9},{9,8},{10,11... | collective-permute-start | bytes 786440 | tf_op jit(solution)/shard_map/ppermute | solution.py:439
  47.6 14.7 %collective-permute-start.3 = (f32[528,128]{1,0:T(8,128)S(1)}, f32[528,128]{1,0:T(8,128)S(1)}, u32[]{:S(2)}, u32[]{:S(2)}) collective-permute-start(f32[528,128]{1,0:T(8,128)S(1)} %get-tuple-element.29), channel_id=1, source_target_pairs={{0,3},{1,2},{2,1},{3,0},{4,7},{5,6},{6,5},{7,4},{8,11},{9,10},{10,... | collective-permute-start | bytes 811016 | tf_op jit(solution)/shard_map/ppermute | solution.py:439
  53.5 13.6 %copy-start.5 = (f32[512]{0:T(512)S(1)}, f32[512]{0:T(512)}, u32[]{:S(2)}) copy-start(f32[512]{0:T(512)} %param.13) | copy-start | bytes 6148
  54.2 12.9 %collective-permute-start.8 = (f32[264,128]{1,0:T(8,128)S(1)}, f32[264,128]{1,0:T(8,128)S(1)}, u32[]{:S(2)}, u32[]{:S(2)}) collective-permute-start(f32[264,128]{1,0:T(8,128)S(1)} %get-tuple-element.33.after), channel_id=1, source_target_pairs={{0,3},{1,2},{2,1},{3,0},{4,7},{5,6},{6,5},{7,4},{8,11},{9,10},{10,... | collective-permute-start | bytes 405512 | tf_op jit(solution)/shard_map/ppermute | solution.py:459
  55.6 11.5 %collective-permute-start.9 = (f32[256,128]{1,0:T(8,128)}, f32[256,128]{1,0:T(8,128)}, u32[]{:S(2)}, u32[]{:S(2)}) collective-permute-start(f32[256,128]{1,0:T(8,128)} %get-tuple-element.36), channel_id=1, source_target_pairs={{0,1},{1,0},{2,3},{3,2},{4,5},{5,4},{6,7},{7,6},{8,9},{9,8},{10,11... | collective-permute-start | bytes 393224 | tf_op jit(solution)/shard_map/ppermute | solution.py:460
  63.0 8.4 %collective-permute-start.6 = (f32[256,128]{1,0:T(8,128)}, f32[256,128]{1,0:T(8,128)}, u32[]{:S(2)}, u32[]{:S(2)}) collective-permute-start(f32[256,128]{1,0:T(8,128)} %get-tuple-element.34), channel_id=1, source_target_pairs={{0,3},{1,2},{2,1},{3,0},{4,7},{5,6},{6,5},{7,4},{8,11},{9,10},{10,... | collective-permute-start | bytes 393224 | tf_op jit(solution)/shard_map/ppermute | solution.py:459
  64.8 6.6 %collective-permute-start.7 = (f32[264,128]{1,0:T(8,128)}, f32[264,128]{1,0:T(8,128)}, u32[]{:S(2)}, u32[]{:S(2)}) collective-permute-start(f32[264,128]{1,0:T(8,128)} %get-tuple-element.35), channel_id=1, source_target_pairs={{0,1},{1,0},{2,3},{3,2},{4,5},{5,4},{6,7},{7,6},{8,9},{9,8},{10,11... | collective-permute-start | bytes 405512 | tf_op jit(solution)/shard_map/ppermute | solution.py:460

commit v7 on v5

--- a/solution.py
+++ b/solution.py
@@ -96,8 +96,13 @@
     earlier = jnp.dot(named.astype(BF16), before, preferred_element_type=F32)
     rank = jnp.sum(named * earlier, axis=0, keepdims=True)
     place = owner * CAP + rank.astype(jnp.int32)
-    hot = lax.broadcasted_iota(jnp.int32, (blocks * CAP, count), 0) == place
-    hot = jnp.where(hot, 1.0, 0.0).astype(BF16)
+    deep = 256
+    slots = lax.broadcasted_iota(jnp.int32, (deep, count), 0).astype(BF16)
+    hot = []
+    for h in range(0, blocks * CAP, deep):
+        near = jnp.clip(place - h, -1, deep).astype(F32).astype(BF16)
+        hot.append(jnp.maximum(1 - jnp.abs(slots - near), 0).astype(BF16))
+    hot = jnp.concatenate(hot, axis=0)
     packed = jnp.dot(hot, rows_ref[...], preferred_element_type=F32).astype(BF16)
     out_ref[...] = packed.reshape(out_ref.shape)
 

time: 83.4 us -> 83.4 us (level)
  no operation moved by 1% of the time
where the time goes in v7:
time: 83.4 us; the launch traced here: 82.9 us
  Pallas kernels  35.4 us (42%)
  starting transfers between devices  28.8 us (35%)
  waiting for transfers between devices  12.6 us (15%)
  local copies, waits for them, and re-layouts  5.82 us (7%)
    pallas_call x10, Pallas kernels, call(): pl.pallas_call(kernel, out_shape=outs, in_specs=specs, out_specs=pl.Block...  35.4 us
    all_to_all x1, starting transfers between devices, local(): lax.all_to_all(packed, ('dom', 'rep'), split_axis=0, concat_axis=0, tiled...  15.6 us
    ppermute x4, waiting for transfers between devices, local(): come[part] = (lax.ppermute(a, 'rep', pair), lax.ppermute(b, 'rep', mirror))  10.2 us
    unnamed x20, local copies, waits for them, and re-layouts  5.82 us
    ppermute x1, starting transfers between devices, local(): from_lower = lax.ppermute(to_upper, 'dom', up)  4.93 us
    ppermute x4, starting transfers between devices, local(): come[part] = (lax.ppermute(a, 'rep', pair), lax.ppermute(b, 'rep', mirror))  4.39 us
    all_to_all x1, waiting for transfers between devices, local(): lax.all_to_all(packed, ('dom', 'rep'), split_axis=0, concat_axis=0, tiled...  2.39 us
    ppermute x2, starting transfers between devices, local(): a2 = lax.ppermute(a_next, 'rep', mirror)  2.02 us
  transfers between devices with their start and end apart: 11, of which 3 were waited for; matrix products, arithmetic and copies ran while one was open for 0% of the time, Pallas kernels for 19%

profile of v7, /device:TPU:1, one launch (start us, length us, event | category | flops | bytes accessed | tf_op | source)
XLA Modules:
  0.0 82.9 jit_solution(1924829451362334595)
XLA Ops:
  0.0 8.0 %listed.1 = (bf16[512,2048]{1,0:T(8,128)(2,1)}, bf16[512,1024]{1,0:T(8,128)(2,1)}, bf16[512,1024]{1,0:T(8,128)(2,1)}) custom-call(bf16[2048,512]{1,0:T(8,128)(2,1)} %rows_ref.2, s32[1,2048]{1,0:T(1,128)} %bitcast.15), custom_call_target="tpu_custom_call" | custom-call | flops 5368709120 | bytes 2105344 | tf_op jit(solution)/shard_map/listed/pallas_call | solution.py:31
  8.0 4.9 %collective-permute-start = (bf16[512,1024]{1,0:T(8,128)(2,1)}, bf16[512,1024]{1,0:T(8,128)(2,1)S(1)}, u32[]{:S(2)}, u32[]{:S(2)}) collective-permute-start(bf16[512,1024]{1,0:T(8,128)(2,1)} %get-tuple-element.23), channel_id=1, source_target_pairs={{0,4},{4,8},{8,12},{12,16},{16,20},{20,24},{24,28},{28,32},{32,36}... | collective-permute-start | bytes 3145736 | tf_op jit(solution)/shard_map/ppermute | solution.py:394
  13.0 1.9 %collective-permute-start.1 = (bf16[512,1024]{1,0:T(8,128)(2,1)}, bf16[512,1024]{1,0:T(8,128)(2,1)S(1)}, u32[]{:S(2)}, u32[]{:S(2)}) collective-permute-start(bf16[512,1024]{1,0:T(8,128)(2,1)} %get-tuple-element.24), channel_id=1, source_target_pairs={{4,0},{8,4},{12,8},{16,12},{20,16},{24,20},{28,24},{32,28},{36,32}... | collective-permute-start | bytes 3145736 | tf_op jit(solution)/shard_map/ppermute | solution.py:395
  14.9 0.0 copy-start.4
  14.9 1.0 %copy-done.4 = bf16[512,512]{1,0:T(8,128)(2,1)S(1)} copy-done((bf16[512,512]{1,0:T(8,128)(2,1)S(1)}, bf16[512,512]{1,0:T(8,128)(2,1)}, u32[]{:S(2)}) %copy-start.4) | copy-done | bytes 524312
  16.0 2.0 %pack_born.1.after = bf16[256,4,512]{2,1,0:T(4,128)(2,1)} custom-call(s32[1,512]{1,0:T(1,128)S(1)} %bitcast.12, bf16[512,512]{1,0:T(8,128)(2,1)S(1)} %copy-done.4), custom_call_target="tpu_custom_call" | custom-call | flops 536870912 | bytes 526336 | tf_op jit(solution)/shard_map/pack_born/pallas_call | solution.py:31
  18.0 15.6 %all-to-all-start = ((bf16[256,4,512]{2,1,0:T(4,128)(2,1)}), bf16[256,4,512]{2,1,0:T(4,128)(2,1)S(1)}, u32[]{:S(2)}, u32[]{:S(2)}) async-start(bf16[256,4,512]{2,1,0:T(4,128)(2,1)} %pack_born.1.after), calls=%async_computation | async-start | bytes 2097152 | tf_op jit(solution)/shard_map/all_to_all | solution.py:406
  33.6 0.0 collective-permute-done.lo
  33.6 0.0 collective-permute-done.1.up
  33.6 0.0 copy-start.2
  33.6 2.3 %copy-done.9 = bf16[512,2048]{1,0:T(8,128)(2,1)S(1)} copy-done((bf16[512,2048]{1,0:T(8,128)(2,1)S(1)}, bf16[512,2048]{1,0:T(8,128)(2,1)}, u32[]{:S(2)}) %copy-start.9) | copy-done | bytes 2097176
  35.9 1.8 %sent_gram_1.1 = (f32[528,128]{1,0:T(8,128)S(1)}, f32[512,128]{1,0:T(8,128)S(1)}) custom-call(s32[1]{0:T(128)} %bitcast.rep_ref, bf16[512,2048]{1,0:T(8,128)(2,1)S(1)} %copy-done.9, bf16[512,1024]{1,0:T(8,128)(2,1)S(1)} %collective-permute-done.lo, bf16[512,1024]{1,0:T(8,128)(2,1)S(1)} %collective-permute-done.1.up, s32[1,2048]{1,0:T(1,128)S(1)} %bitcast.6, ...), custom_call_target="tpu_custom_call" | custom-call | flops 4831838208 | bytes 5259268 | tf_op jit(solution)/shard_map/sent_gram_1/pallas_call | solution.py:31
  37.8 2.7 %collective-permute-start.5 = (f32[512,128]{1,0:T(8,128)S(1)}, f32[512,128]{1,0:T(8,128)S(1)}, u32[]{:S(2)}, u32[]{:S(2)}) collective-permute-start(f32[512,128]{1,0:T(8,128)S(1)} %get-tuple-element.32), channel_id=1, source_target_pairs={{0,3},{1,2},{2,1},{3,0},{4,7},{5,6},{6,5},{7,4},{8,11},{9,10},{10,... | collective-permute-start | bytes 786440 | tf_op jit(solution)/shard_map/ppermute | solution.py:437
  40.5 0.0 collective-permute-start.4
  40.5 1.2 %copy-done.1 = bf16[512,1024]{1,0:T(8,128)(2,1)S(1)} copy-done((bf16[512,1024]{1,0:T(8,128)(2,1)S(1)}, bf16[512,1024]{1,0:T(8,128)(2,1)}, u32[]{:S(2)}) %copy-start.1) | copy-done | bytes 1048600
  41.8 1.2 %copy-done.3 = bf16[512,1024]{1,0:T(8,128)(2,1)S(1)} copy-done((bf16[512,1024]{1,0:T(8,128)(2,1)S(1)}, bf16[512,1024]{1,0:T(8,128)(2,1)}, u32[]{:S(2)}) %copy-start.3) | copy-done | bytes 1048600
  43.0 1.8 %sent_gram_2.1 = (f32[512,128]{1,0:T(8,128)S(1)}, f32[528,128]{1,0:T(8,128)S(1)}) custom-call(s32[1]{0:T(128)} %bitcast.rep_ref, bf16[512,2048]{1,0:T(8,128)(2,1)S(1)} %copy-done.9, bf16[512,1024]{1,0:T(8,128)(2,1)S(1)} %copy-done.1, bf16[512,1024]{1,0:T(8,128)(2,1)S(1)} %copy-done.3, s32[1,2048]{1,0:T(1,128)S(1)} %bitcast.7, s32[1,2048]{1,0:T(1,128)S(1)} %bitcast.10, ...), custom_call_target="tpu_custom_call" | custom-call | flops 4831838208 | bytes 4481028 | tf_op jit(solution)/shard_map/sent_gram_2/pallas_call | solution.py:31
  44.8 1.6 %collective-permute-start.2 = (f32[512,128]{1,0:T(8,128)S(1)}, f32[512,128]{1,0:T(8,128)S(1)}, u32[]{:S(2)}, u32[]{:S(2)}) collective-permute-start(f32[512,128]{1,0:T(8,128)S(1)} %get-tuple-element.26.after), channel_id=1, source_target_pairs={{0,1},{1,0},{2,3},{3,2},{4,5},{5,4},{6,7},{7,6},{8,9},{9,8},{10,11... | collective-permute-start | bytes 786440 | tf_op jit(solution)/shard_map/ppermute | solution.py:437
  46.4 0.1 collective-permute-start.3
  46.5 3.5 %kept_gram.1 = (f32[528,128]{1,0:T(8,128)S(1)}, f32[512,128]{1,0:T(8,128)S(1)}, f32[512,128]{1,0:T(8,128)S(1)}, f32[528,128]{1,0:T(8,128)S(1)}) custom-call(s32[1]{0:T(128)} %bitcast.rep_ref, bf16[512,2048]{1,0:T(8,128)(2,1)S(1)} %copy-done.9, bf16[512,1024]{1,0:T(8,128)(2,1)S(1)} %copy-done.1, bf16[512,1024]{1,0:T(8,128)(2,1)S(1)} %copy-done.3, ...), custom_call_target="tpu_custom_call" | custom-call | flops 9663676416 | bytes 4472836 | tf_op jit(solution)/shard_map/kept_gram/pallas_call | solution.py:31
  50.0 0.0 collective-permute-done.5.rb
  50.0 2.8 %collective-permute-done.4.ra = f32[528,128]{1,0:T(8,128)S(1)} collective-permute-done((f32[528,128]{1,0:T(8,128)S(1)}, f32[528,128]{1,0:T(8,128)S(1)}, u32[]{:S(2)}, u32[]{:S(2)}) %collective-permute-start.4) | collective-permute-done | bytes 270368 | tf_op jit(solution)/shard_map/ppermute | solution.py:437
  52.8 0.7 onward_1.1
  53.4 0.8 collective-permute-start.8
  54.2 0.0 collective-permute-start.9
  54.2 7.4 %collective-permute-done.2.ra = f32[512,128]{1,0:T(8,128)S(1)} collective-permute-done((f32[512,128]{1,0:T(8,128)S(1)}, f32[512,128]{1,0:T(8,128)S(1)}, u32[]{:S(2)}, u32[]{:S(2)}) %collective-permute-start.2) | collective-permute-done | bytes 262176 | tf_op jit(solution)/shard_map/ppermute | solution.py:437
  61.6 0.7 onward_2.1
  62.4 1.3 %collective-permute-start.6 = (f32[256,128]{1,0:T(8,128)}, f32[256,128]{1,0:T(8,128)}, u32[]{:S(2)}, u32[]{:S(2)}) collective-permute-start(f32[256,128]{1,0:T(8,128)} %get-tuple-element.34), channel_id=1, source_target_pairs={{0,3},{1,2},{2,1},{3,0},{4,7},{5,6},{6,5},{7,4},{8,11},{9,10},{10,... | collective-permute-start | bytes 393224 | tf_op jit(solution)/shard_map/ppermute | solution.py:457
  63.6 2.4 %all-to-all-done.pool_ref = bf16[256,4,512]{2,1,0:T(4,128)(2,1)S(1)} async-done(((bf16[256,4,512]{2,1,0:T(4,128)(2,1)}), bf16[256,4,512]{2,1,0:T(4,128)(2,1)S(1)}, u32[]{:S(2)}, u32[]{:S(2)}) %all-to-all-start) | async-done | bytes 1048608 | tf_op jit(solution)/shard_map/all_to_all | solution.py:406
  66.0 0.7 born_gram.1.born
  66.8 4.3 %first_panel.1 = (f32[128,512]{1,0:T(8,128)S(1)}, f32[128,128]{1,0:T(8,128)S(1)}) custom-call(f32[528,128]{1,0:T(8,128)S(1)} %get-tuple-element.30.ka, f32[528,128]{1,0:T(8,128)S(1)} %collective-permute-done.4.ra, f32[264,128]{1,0:T(8,128)S(1)} %collective-permute-done.8.a2, f32[512,128]{1,0:T(8,128)S(1)} %get-tuple-element.31.kb, ...), custom_call_target="tpu_custom_call" | custom-call | flops 1000000000 | bytes 2381824 | tf_op jit(solution)/shard_map/first_panel/pallas_call | solution.py:31
  71.1 11.8 %other_panels.1 = f32[512,512]{1,0:T(8,128)} custom-call(f32[512,128]{1,0:T(8,128)S(1)} %get-tuple-element.27.after.ka, f32[512,128]{1,0:T(8,128)S(1)} %collective-permute-done.2.ra, f32[256,128]{1,0:T(8,128)} %collective-permute-done.6.a2, f32[528,128]{1,0:T(8,128)S(1)} %get-tuple-element.28.kb, f32[528,128]{1,0:T(8,128)S(1)} %collective-permute-done.3.rb, ...), custom_call_target="tpu_custom_call" | custom-call | flops 2000000000 | bytes 2709504 | tf_op jit(solution)/shard_map/other_panels/pallas_call | solution.py:31
  (20 shorter events, 0.0 us)
Async XLA Ops:
  0.0 14.9 %copy-start.7 = (s32[512,1]{0,1:T(1,128)S(1)}, s32[512,1]{0,1:T(1,128)}, u32[]{:S(2)}) copy-start(s32[512,1]{0,1:T(1,128)} %param.12) | copy-start | bytes 6148
  0.0 33.6 %copy-start.5 = (s32[2048]{0:T(1024)S(1)}, s32[2048]{0:T(1024)}, u32[]{:S(2)}) copy-start(s32[2048]{0:T(1024)} %param.8) | copy-start | bytes 24580
  0.0 33.6 %copy-start.6 = (s32[2048]{0:T(1024)S(1)}, s32[2048]{0:T(1024)}, u32[]{:S(2)}) copy-start(s32[2048]{0:T(1024)} %param.10) | copy-start | bytes 24580
  8.0 25.5 %collective-permute-start = (bf16[512,1024]{1,0:T(8,128)(2,1)}, bf16[512,1024]{1,0:T(8,128)(2,1)S(1)}, u32[]{:S(2)}, u32[]{:S(2)}) collective-permute-start(bf16[512,1024]{1,0:T(8,128)(2,1)} %get-tuple-element.23), channel_id=1, source_target_pairs={{0,4},{4,8},{8,12},{12,16},{16,20},{20,24},{24,28},{28,32},{32,36}... | collective-permute-start | bytes 3145736 | tf_op jit(solution)/shard_map/ppermute | solution.py:394
  13.0 20.6 %collective-permute-start.1 = (bf16[512,1024]{1,0:T(8,128)(2,1)}, bf16[512,1024]{1,0:T(8,128)(2,1)S(1)}, u32[]{:S(2)}, u32[]{:S(2)}) collective-permute-start(bf16[512,1024]{1,0:T(8,128)(2,1)} %get-tuple-element.24), channel_id=1, source_target_pairs={{4,0},{8,4},{12,8},{16,12},{20,16},{24,20},{28,24},{32,28},{36,32}... | collective-permute-start | bytes 3145736 | tf_op jit(solution)/shard_map/ppermute | solution.py:395
  14.9 1.0 %copy-start.4 = (bf16[512,512]{1,0:T(8,128)(2,1)S(1)}, bf16[512,512]{1,0:T(8,128)(2,1)}, u32[]{:S(2)}) copy-start(bf16[512,512]{1,0:T(8,128)(2,1)} %rows_ref.3) | copy-start | bytes 1572868
  18.0 48.0 %all-to-all-start = ((bf16[256,4,512]{2,1,0:T(4,128)(2,1)}), bf16[256,4,512]{2,1,0:T(4,128)(2,1)S(1)}, u32[]{:S(2)}, u32[]{:S(2)}) async-start(bf16[256,4,512]{2,1,0:T(4,128)(2,1)} %pack_born.1.after), calls=%async_computation | async-start | bytes 2097152 | tf_op jit(solution)/shard_map/all_to_all | solution.py:406
  33.6 4.2 %copy-start = (bf16[512,1024]{1,0:T(8,128)(2,1)}, bf16[512,1024]{1,0:T(8,128)(2,1)S(1)}, u32[]{:S(2)}) copy-start(bf16[512,1024]{1,0:T(8,128)(2,1)S(1)} %collective-permute-done.lo) | copy-start | bytes 3145732
  33.6 4.2 %copy-start.2 = (bf16[512,1024]{1,0:T(8,128)(2,1)}, bf16[512,1024]{1,0:T(8,128)(2,1)S(1)}, u32[]{:S(2)}) copy-start(bf16[512,1024]{1,0:T(8,128)(2,1)S(1)} %collective-permute-done.1.up) | copy-start | bytes 3145732
  33.6 2.3 %copy-start.9 = (bf16[512,2048]{1,0:T(8,128)(2,1)S(1)}, bf16[512,2048]{1,0:T(8,128)(2,1)}, u32[]{:S(2)}) copy-start(bf16[512,2048]{1,0:T(8,128)(2,1)} %get-tuple-element.22.cols) | copy-start | bytes 6291460
  37.8 12.2 %collective-permute-start.5 = (f32[512,128]{1,0:T(8,128)S(1)}, f32[512,128]{1,0:T(8,128)S(1)}, u32[]{:S(2)}, u32[]{:S(2)}) collective-permute-start(f32[512,128]{1,0:T(8,128)S(1)} %get-tuple-element.32), channel_id=1, source_target_pairs={{0,3},{1,2},{2,1},{3,0},{4,7},{5,6},{6,5},{7,4},{8,11},{9,10},{10,... | collective-permute-start | bytes 786440 | tf_op jit(solution)/shard_map/ppermute | solution.py:437
  40.5 12.2 %collective-permute-start.4 = (f32[528,128]{1,0:T(8,128)S(1)}, f32[528,128]{1,0:T(8,128)S(1)}, u32[]{:S(2)}, u32[]{:S(2)}) collective-permute-start(f32[528,128]{1,0:T(8,128)S(1)} %get-tuple-element.25.after), channel_id=1, source_target_pairs={{0,1},{1,0},{2,3},{3,2},{4,5},{5,4},{6,7},{7,6},{8,9},{9,8},{10,11... | collective-permute-start | bytes 811016 | tf_op jit(solution)/shard_map/ppermute | solution.py:437
  40.5 1.2 %copy-start.1 = (bf16[512,1024]{1,0:T(8,128)(2,1)S(1)}, bf16[512,1024]{1,0:T(8,128)(2,1)}, u32[]{:S(2)}) copy-start(bf16[512,1024]{1,0:T(8,128)(2,1)} %copy-done) | copy-start | bytes 3145732
  41.8 1.2 %copy-start.3 = (bf16[512,1024]{1,0:T(8,128)(2,1)S(1)}, bf16[512,1024]{1,0:T(8,128)(2,1)}, u32[]{:S(2)}) copy-start(bf16[512,1024]{1,0:T(8,128)(2,1)} %copy-done.2) | copy-start | bytes 3145732
  44.8 16.8 %collective-permute-start.2 = (f32[512,128]{1,0:T(8,128)S(1)}, f32[512,128]{1,0:T(8,128)S(1)}, u32[]{:S(2)}, u32[]{:S(2)}) collective-permute-start(f32[512,128]{1,0:T(8,128)S(1)} %get-tuple-element.26.after), channel_id=1, source_target_pairs={{0,1},{1,0},{2,3},{3,2},{4,5},{5,4},{6,7},{7,6},{8,9},{9,8},{10,11... | collective-permute-start | bytes 786440 | tf_op jit(solution)/shard_map/ppermute | solution.py:437
  46.4 15.2 %collective-permute-start.3 = (f32[528,128]{1,0:T(8,128)S(1)}, f32[528,128]{1,0:T(8,128)S(1)}, u32[]{:S(2)}, u32[]{:S(2)}) collective-permute-start(f32[528,128]{1,0:T(8,128)S(1)} %get-tuple-element.29), channel_id=1, source_target_pairs={{0,3},{1,2},{2,1},{3,0},{4,7},{5,6},{6,5},{7,4},{8,11},{9,10},{10,... | collective-permute-start | bytes 811016 | tf_op jit(solution)/shard_map/ppermute | solution.py:437
  52.8 14.0 %copy-start.8 = (f32[512]{0:T(512)S(1)}, f32[512]{0:T(512)}, u32[]{:S(2)}) copy-start(f32[512]{0:T(512)} %param.13) | copy-start | bytes 6148
  53.4 13.3 %collective-permute-start.8 = (f32[264,128]{1,0:T(8,128)S(1)}, f32[264,128]{1,0:T(8,128)S(1)}, u32[]{:S(2)}, u32[]{:S(2)}) collective-permute-start(f32[264,128]{1,0:T(8,128)S(1)} %get-tuple-element.33.after), channel_id=1, source_target_pairs={{0,3},{1,2},{2,1},{3,0},{4,7},{5,6},{6,5},{7,4},{8,11},{9,10},{10,... | collective-permute-start | bytes 405512 | tf_op jit(solution)/shard_map/ppermute | solution.py:457
  54.2 12.6 %collective-permute-start.9 = (f32[256,128]{1,0:T(8,128)}, f32[256,128]{1,0:T(8,128)}, u32[]{:S(2)}, u32[]{:S(2)}) collective-permute-start(f32[256,128]{1,0:T(8,128)} %get-tuple-element.36), channel_id=1, source_target_pairs={{0,1},{1,0},{2,3},{3,2},{4,5},{5,4},{6,7},{7,6},{8,9},{9,8},{10,11... | collective-permute-start | bytes 393224 | tf_op jit(solution)/shard_map/ppermute | solution.py:458
  62.4 8.7 %collective-permute-start.6 = (f32[256,128]{1,0:T(8,128)}, f32[256,128]{1,0:T(8,128)}, u32[]{:S(2)}, u32[]{:S(2)}) collective-permute-start(f32[256,128]{1,0:T(8,128)} %get-tuple-element.34), channel_id=1, source_target_pairs={{0,3},{1,2},{2,1},{3,0},{4,7},{5,6},{6,5},{7,4},{8,11},{9,10},{10,... | collective-permute-start | bytes 393224 | tf_op jit(solution)/shard_map/ppermute | solution.py:457
  63.6 7.5 %collective-permute-start.7 = (f32[264,128]{1,0:T(8,128)}, f32[264,128]{1,0:T(8,128)}, u32[]{:S(2)}, u32[]{:S(2)}) collective-permute-start(f32[264,128]{1,0:T(8,128)} %get-tuple-element.35), channel_id=1, source_target_pairs={{0,1},{1,0},{2,3},{3,2},{4,5},{5,4},{6,7},{7,6},{8,9},{9,8},{10,11... | collective-permute-start | bytes 405512 | tf_op jit(solution)/shard_map/ppermute | solution.py:458
